TPU v7x, 128 devices: a whole 4x4x4 slice. The times are simulated.
128 devices in a mesh: intra: 8 (over y, z_hi), inter: 16 (over z_lo, x, core).
Axes of the slice: x: 4, y: 4, z: 4 (z_hi: 2, z_lo: 2; z = z_hi * 2 + z_lo), core: 2. Of those that a mesh axis runs over, the one named last changes fastest.
Arguments:
- activations: bfloat16 [65536, 8192], P(('intra', 'inter')), may hold values from -24 to 24
- key_grads: bfloat16 [65536, 1024], P(('intra', 'inter')), may hold values from -6 to 6
- key_weight: bfloat16 [8192, 1024], P('intra'), may hold values from -0.1875 to 0.1875
Outputs:
- input_grads: bfloat16 [65536, 8192], P(('intra', 'inter'))
- weight_grads: float32 [8192, 1024], P(('intra', 'inter'))
All inputs are finite; a program needn't handle non-finite values. Where the computation divides by a largest or mean magnitude, that divisor is 1e-20 or more.
Results may differ from a plain program's by a relative error of at most 0.013.
Values may be sent and summed in bfloat16 or wider, within the bound.
No kernel may reach another device: no remote copies, remote signals or barrier semaphores. Data moves between devices by JAX's collectives and lax.ppermute only.
A program may use at most 256 MiB of HBM per device.

v0:
```python
import jax
import jax.numpy as jnp
from jax import lax
from jax.sharding import PartitionSpec as P

EPS = 1e-06


def to_codes(values):
    maxima = jnp.max(jnp.abs(values), axis=-1) + EPS
    quantized = (values / maxima[..., None]).astype(jnp.bfloat16)
    return (quantized, maxima)


def from_codes(quantized, maxima, groups):
    row_count = quantized.shape[0] // groups
    scaled = quantized.reshape(groups, row_count, quantized.shape[1], 128).astype(
        jnp.float32
    ) * maxima.reshape(groups, row_count, maxima.shape[1], 1)
    return jnp.sum(scaled, axis=0)


def shards(activations, key_grads, key_weight):
    intra_count = lax.axis_size("intra")
    inter_count = lax.axis_size("inter")
    norm_factor = (activations.shape[0] * intra_count * inter_count) ** (-0.5)
    product = lax.dot_general(
        key_grads,
        lax.all_gather(key_weight, "intra", axis=0, tiled=True),
        (((1,), (1,)), ((), ())),
        preferred_element_type=jnp.float32,
    )
    input_grads = product.astype(jnp.bfloat16)
    partial_value = (
        lax.dot_general(
            activations, key_grads, (((0,), (0,)), ((), ())), preferred_element_type=jnp.float32
        )
        * norm_factor
    )
    quantized, maxima = to_codes(partial_value.reshape(partial_value.shape[0], -1, 128))
    node_total = from_codes(
        lax.all_to_all(quantized, "intra", split_axis=0, concat_axis=0, tiled=True),
        lax.all_to_all(
            maxima.astype(jnp.bfloat16), "intra", split_axis=0, concat_axis=0, tiled=True
        ).astype(maxima.dtype),
        intra_count,
    )
    second_codes, second_maxima = to_codes(node_total)
    owned = from_codes(
        lax.all_to_all(second_codes, "inter", split_axis=0, concat_axis=0, tiled=True),
        lax.all_to_all(
            second_maxima.astype(jnp.bfloat16), "inter", split_axis=0, concat_axis=0, tiled=True
        ).astype(second_maxima.dtype),
        inter_count,
    )
    weight_grads = owned.reshape(owned.shape[0], -1)
    return (input_grads, weight_grads)


def solution(mesh):
    in_specs = (P(("intra", "inter"), None), P(("intra", "inter"), None), P("intra", None))
    out_specs = (P(("intra", "inter"), None), P(("intra", "inter"), None))
    return jax.shard_map(shards, mesh=mesh, in_specs=in_specs, out_specs=out_specs, check_vma=False)
```

profile of v0, /device:TPU:1, one launch (start us, length us, event | category | flops | bytes accessed | tf_op | source)
XLA Modules:
  0.0 487.2 jit_solution(9699095303175030413)
XLA Ops:
  7.2 0.7 all-gather.2.cloned.1.call-update
  7.9 0.5 copy-done
  8.4 21.0 %abs_reduce_fusion = (f32[8192,8]{0,1:T(8,128)S(1)}, f32[8192,1024]{0,1:T(8,128)}) fusion(bf16[512,8192]{1,0:T(8,128)(2,1)} %param.3, bf16[512,1024]{1,0:T(8,128)(2,1)S(1)} %copy-done), kind=kOutput, calls=%fused_computation.2 | convolution fusion | flops 8615034880 | bytes 43253760 | tf_op jit(solution)/shard_map/dot_general | solution.py:35
  29.4 0.7 fusion.2
  30.0 8.4 %all-to-all-start.1 = ((bf16[8,1024,8]{1,2,0:T(8,128)(2,1)}), bf16[8,1024,8]{1,2,0:T(8,128)(2,1)S(1)}, u32[]{:S(2)}, u32[]{:S(2)}) async-start(bf16[8,1024,8]{1,2,0:T(8,128)(2,1)} %bitcast.2), calls=%async_computation.1 | async-start | bytes 262144 | tf_op jit(solution)/shard_map/all_to_all | solution.py:43
  38.4 2.7 copy.17
  41.1 33.6 %copy.18 = f32[8192,8,128]{2,1,0:T(8,128)} copy(f32[8192,8,128]{0,2,1:T(8,128)} %bitcast.21) | data formatting | bytes 67108864 | tf_op jit(solution)/shard_map/reshape | solution.py:40
  74.6 20.9 %divide_convert_fusion = bf16[8192,8,128]{2,1,0:T(8,128)(2,1)} fusion(f32[8192,8,128]{2,1,0:T(8,128)} %copy.18, f32[8192,8]{1,0:T(8,128)} %copy.17), kind=kLoop, calls=%fused_computation.1 | loop fusion | flops 16777216 | bytes 50593792 | tf_op jit(solution)/shard_map/convert_element_type | solution.py:11
  95.6 6.7 %all-to-all-start = ((bf16[8192,8,128]{2,1,0:T(8,128)(2,1)}), bf16[8192,8,128]{2,1,0:T(8,128)(2,1)}, u32[]{:S(2)}, u32[]{:S(2)}) async-start(bf16[8192,8,128]{2,1,0:T(8,128)(2,1)} %divide_convert_fusion), calls=%async_computation | async-start | bytes 33554432 | tf_op jit(solution)/shard_map/all_to_all | solution.py:42
  102.3 239.8 %all-to-all-done = bf16[8192,8,128]{2,1,0:T(8,128)(2,1)} async-done(((bf16[8192,8,128]{2,1,0:T(8,128)(2,1)}), bf16[8192,8,128]{2,1,0:T(8,128)(2,1)}, u32[]{:S(2)}, u32[]{:S(2)}) %all-to-all-start) | async-done | bytes 16777248 | tf_op jit(solution)/shard_map/all_to_all | solution.py:42
  342.1 40.6 %copy.20 = f32[8,1024,8,128]{1,0,3,2:T(8,128)} copy(bf16[8,1024,8,128]{3,2,1,0:T(8,128)(2,1)} %bitcast.4) | data formatting | bytes 50331648 | tf_op jit(solution)/shard_map/convert_element_type | solution.py:17
  382.8 16.8 %multiply_reduce_fusion = f32[1024,8,128]{0,2,1:T(8,128)S(1)} fusion(f32[8,1024,8,128]{1,0,3,2:T(8,128)} %copy.20, f32[8,1024,8]{1,0,2:T(8,128)S(1)} %copy.19), kind=kLoop, calls=%fused_computation | loop fusion | flops 15728640 | bytes 38010880 | tf_op jit(solution)/shard_map/reduce_sum | solution.py:20
  399.6 2.0 copy-done.1
  401.6 0.5 abs_reduce_fusion.1
  402.3 0.7 reshape.46
  403.0 5.7 %all-to-all-start.3 = ((bf16[16,2,256]{2,1,0:T(2,128)(2,1)}), bf16[16,2,256]{2,1,0:T(2,128)(2,1)S(1)}, u32[]{:S(2)}, u32[]{:S(2)}) async-start(bf16[16,2,256]{2,1,0:T(2,128)(2,1)} %reshape.46), calls=%async_computation.3 | async-start | bytes 32768 | tf_op jit(solution)/shard_map/all_to_all | solution.py:51
  408.6 2.8 divide_convert_fusion.1
  411.4 2.9 copy.21
  414.4 5.6 %all-to-all-start.2 = ((bf16[1024,8,128]{2,1,0:T(8,128)(2,1)}), bf16[1024,8,128]{2,1,0:T(8,128)(2,1)S(1)}, u32[]{:S(2)}, u32[]{:S(2)}) async-start(bf16[1024,8,128]{2,1,0:T(8,128)(2,1)} %copy.21), calls=%async_computation.2 | async-start | bytes 4194304 | tf_op jit(solution)/shard_map/all_to_all | solution.py:50
  420.1 0.9 copy.23
  421.1 26.7 %all-to-all-done.2 = bf16[1024,8,128]{2,1,0:T(8,128)(2,1)S(1)} async-done(((bf16[1024,8,128]{2,1,0:T(8,128)(2,1)}), bf16[1024,8,128]{2,1,0:T(8,128)(2,1)S(1)}, u32[]{:S(2)}, u32[]{:S(2)}) %all-to-all-start.2) | async-done | bytes 2097184 | tf_op jit(solution)/shard_map/all_to_all | solution.py:50
  447.7 2.2 fusion
  450.0 0.8 copy.27
  450.7 29.6 %convolution_convert_fusion = bf16[512,8192]{1,0:T(8,128)(2,1)} fusion(bf16[512,1024]{1,0:T(8,128)(2,1)S(1)} %copy-done, bf16[8192,1024]{1,0:T(8,128)(2,1)} %all-gather.2.cloned.1.call-done), kind=kOutput, calls=%fused_computation.4 | convolution fusion | flops 8594128896 | bytes 26214400 | tf_op jit(solution)/shard_map/dot_general | solution.py:27
  (11 shorter events, 0.4 us)
Async XLA Ops:
  7.2 1.2 copy-start
  7.2 443.5 %all-gather.2.cloned.1.call-start = ((), (), s32[]{:S(2)}) async-start(), calls=%async_computation.4 | async-start | bytes 18874368 | tf_op jit(solution)/shard_map/all_gather | solution.py:29
  30.0 65.5 %all-to-all-start.1 = ((bf16[8,1024,8]{1,2,0:T(8,128)(2,1)}), bf16[8,1024,8]{1,2,0:T(8,128)(2,1)S(1)}, u32[]{:S(2)}, u32[]{:S(2)}) async-start(bf16[8,1024,8]{1,2,0:T(8,128)(2,1)} %bitcast.2), calls=%async_computation.1 | async-start | bytes 262144 | tf_op jit(solution)/shard_map/all_to_all | solution.py:43
  95.6 246.5 %all-to-all-start = ((bf16[8192,8,128]{2,1,0:T(8,128)(2,1)}), bf16[8192,8,128]{2,1,0:T(8,128)(2,1)}, u32[]{:S(2)}, u32[]{:S(2)}) async-start(bf16[8192,8,128]{2,1,0:T(8,128)(2,1)} %divide_convert_fusion), calls=%async_computation | async-start | bytes 33554432 | tf_op jit(solution)/shard_map/all_to_all | solution.py:42
  399.6 2.0 copy-start.1
  403.0 11.5 %all-to-all-start.3 = ((bf16[16,2,256]{2,1,0:T(2,128)(2,1)}), bf16[16,2,256]{2,1,0:T(2,128)(2,1)S(1)}, u32[]{:S(2)}, u32[]{:S(2)}) async-start(bf16[16,2,256]{2,1,0:T(2,128)(2,1)} %reshape.46), calls=%async_computation.3 | async-start | bytes 32768 | tf_op jit(solution)/shard_map/all_to_all | solution.py:51
  414.4 33.3 %all-to-all-start.2 = ((bf16[1024,8,128]{2,1,0:T(8,128)(2,1)}), bf16[1024,8,128]{2,1,0:T(8,128)(2,1)S(1)}, u32[]{:S(2)}, u32[]{:S(2)}) async-start(bf16[1024,8,128]{2,1,0:T(8,128)(2,1)} %copy.21), calls=%async_computation.2 | async-start | bytes 4194304 | tf_op jit(solution)/shard_map/all_to_all | solution.py:50
Sparse Core Ops, SparseCore 0:
  10.4 370.0 all-gather.1
where the time goes:
time: 489 us; the launch traced here: 487 us
  waiting for transfers between devices  267 us (55%)
  local copies, waits for them, and re-layouts  84.9 us (17%)
  matrix products  50.6 us (10%)
  other arithmetic  44 us (9%)
  starting transfers between devices  26.4 us (5%)
  between operations  14.1 us (3%)
    all_to_all x1, waiting for transfers between devices, shards(): lax.all_to_all(quantized, 'intra', split_axis=0, concat_axis=0, tiled=True)  240 us
    convert_element_type x1, local copies, waits for them, and re-layouts, from_codes(): quantized.reshape(groups, row_count, quantized.shape[1], 128)  40.6 us
    reshape x1, local copies, waits for them, and re-layouts, shards(): partial_value.reshape(partial_value.shape[0], -1, 128)  33.6 us
    dot_general x1, matrix products, shards(): lax.dot_general(key_grads, lax.all_gather(key_weight, 'intra', axis=0, ti...  29.6 us
    all_to_all x1, waiting for transfers between devices, shards(): lax.all_to_all(second_codes, 'inter', split_axis=0, concat_axis=0, tiled=...  26.7 us
    convert_element_type x2, other arithmetic, to_codes(): quantized = (values / maxima[..., None]).astype(jnp.bfloat16)  23.7 us
    dot_general x1, matrix products, shards(): lax.dot_general(activations, key_grads, (((0,), (0,)), ((), ())), preferr...  21 us
    reduce_sum x2, other arithmetic, from_codes(): return jnp.sum(scaled, axis=0)  19.1 us
  transfers between devices with their start and end apart: 5, of which 3 were waited for; matrix products, arithmetic and copies ran while one was open for 30% of the time, Pallas kernels for 0%

commit v1 on v0

v1 whole, which is shorter than its diff:
```python
import functools

import jax
import jax.numpy as jnp
import numpy as np
from jax import lax
from jax.experimental import pallas as pl
from jax.experimental.pallas import tpu as pltpu
from jax.sharding import PartitionSpec as P

SIZES = (4, 2, 2, 4, 2)
AXES = ("intra", "inter")
S1 = 640
T1 = 336
BLK = 128

RS_A = ((("xA", "xB", "zD"), ("zD", "xA", "xB")), (("xB", "zD", "xA"), ("zD", "xA", "xB")))
RS_B = ((("zC", "yA"), ("yA", "zC")), (("yA", "zC"), ("zC", "yA")))
AG = ((("yA", "yB", "zC"), ("zC", "yA", "yB")), (("yB", "zC", "yA"), ("zC", "yA", "yB")))


def coords(device):
    return tuple(int(v) for v in np.unravel_index(device, SIZES))


def ident(at):
    return int(np.ravel_multi_index(at, SIZES))


def flip(at, dim):
    y, zh, zl, x, c = at
    return {
        "yA": (y ^ 1, zh, zl, x, c),
        "yB": (3 - y, zh, zl, x, c),
        "zC": (y, zh ^ 1, zl ^ 1, x, c),
        "zD": (y, zh, zl ^ 1, x, c),
        "xA": (y, zh, zl, x ^ 1, c),
        "xB": (y, zh, zl, 3 - x, c),
        "core": (y, zh, zl, x, 1 - c),
    }[dim]


def table():
    rows = []
    for device in range(128):
        at = coords(device)
        core = at[4]
        row = []
        for stream in range(2):
            dims = RS_A[core][stream] + RS_B[core][stream]
            for j in range(32):
                owner = at
                if (at[0] >> 1) != core:
                    owner = flip(owner, "yB")
                for k, dim in enumerate(dims):
                    if (j >> (4 - k)) & 1:
                        owner = flip(owner, dim)
                assert owner[0] >> 1 == core
                row.append(ident(owner) // 2 - 32 * core)
        for gatherer in (core, 1 - core):
            for stream in range(2):
                for j in range(8):
                    holder = at
                    for k, dim in enumerate(AG[gatherer][stream]):
                        if (j >> k) & 1:
                            holder = flip(holder, dim)
                    row.append(holder[0] * 2 + holder[1])
        rows.append(row)
    return np.array(rows, np.int32)


def move(value, dims_of_core):
    pairs = []
    for device in range(128):
        at = coords(device)
        pairs.append((device, ident(flip(at, dims_of_core[at[4]]))))
    return lax.ppermute(value, AXES, pairs)


def move_some(value, want_mine, dims):
    pairs = []
    for device in range(128):
        at = coords(device)
        if ((at[0] >> 1) == at[4]) == want_mine:
            to = at
            for dim in dims:
                to = flip(to, dim)
            pairs.append((device, ident(to)))
    return lax.ppermute(value, AXES, pairs)


def partial_body(low, high, norm, idx_ref, *refs):
    own = jnp.concatenate([ref[...] for ref in refs[0:4]], axis=1)
    got = jnp.concatenate([ref[...] for ref in refs[4:8]], axis=1)
    kt_own, kt_got, out_ref = refs[8:]
    total = jnp.dot(kt_own[low:high, :], own, preferred_element_type=jnp.float32)
    total += jnp.dot(kt_got[low:high, :], got, preferred_element_type=jnp.float32)
    total = (total * norm).astype(jnp.bfloat16)
    for k in range(4):
        out_ref[k] = total[:, k * BLK : (k + 1) * BLK]


def partial_blocks(idx, core, acts, acts_got, kt_own, kt_got, low, high, norm):
    tokens = acts.shape[0]
    count = idx.shape[0]
    where = jnp.concatenate([idx + 32 * core, idx])
    specs = [
        pl.BlockSpec((tokens, BLK), functools.partial(lambda k, i, w: (0, w[4 * i + k]), k))
        for k in range(4)
    ] + [
        pl.BlockSpec((tokens, BLK), functools.partial(lambda k, i, w: (0, w[count + 4 * i + k]), k))
        for k in range(4)
    ]
    specs += [pl.BlockSpec(kt_own.shape, lambda i, w: (0, 0))] * 2
    width = high - low
    return pl.pallas_call(
        functools.partial(partial_body, low, high, norm),
        grid_spec=pltpu.PrefetchScalarGridSpec(
            num_scalar_prefetch=1,
            grid=(count // 4,),
            in_specs=specs,
            out_specs=pl.BlockSpec((4, width, BLK), lambda i, w: (i, 0, 0)),
        ),
        out_shape=jax.ShapeDtypeStruct((count, width, BLK), jnp.bfloat16),
        compiler_params=pltpu.CompilerParams(vmem_limit_bytes=32 * 1024 * 1024),
        cost_estimate=pl.CostEstimate(
            flops=4 * tokens * width * count * BLK, bytes_accessed=count * BLK * (4 * tokens + 2 * width), transcendentals=0
        ),
    )(where, *([acts] * 4), *([acts_got] * 4), kt_own, kt_got)


def project_body(half, rest, sched_ref, kg_ref, *refs):
    pieces, out_ref, wbuf, sem_a, sem_b = refs[:8], refs[8], refs[9], refs[10], refs[11]
    step = pl.program_id(0)

    def piece(side, stream, j):
        source = pieces[side * 4 + stream * 2 + j // 4].at[j % 4]
        shard = sched_ref[16 + side * 16 + stream * 8 + j]
        rows = T1 if stream == 0 else rest
        first = shard * (2 * half) + sched_ref[48 + side] * half + (0 if stream == 0 else T1)
        sem = (sem_a if stream == 0 else sem_b).at[side * 8 + j]
        return pltpu.make_async_copy(source, wbuf.at[pl.ds(pl.multiple_of(first, 16), rows), :], sem)

    @pl.when(step == 0)
    def _():
        for side in range(2):
            for stream in (1, 0):
                for j in range(8):
                    piece(side, stream, j).start()

    for side in range(2):

        @pl.when(step == 8 * side)
        def _(side=side):
            for j in range(8):
                piece(side, 1, j).wait()

        for j in range(8):

            @pl.when(step == 8 * side + j)
            def _(side=side, j=j):
                piece(side, 0, j).wait()

    start = pl.multiple_of(sched_ref[step] * half, half)
    out_ref[...] = lax.dot_general(
        kg_ref[...], wbuf[pl.ds(start, half), :], (((1,), (1,)), ((), ())), preferred_element_type=jnp.float32
    ).astype(jnp.bfloat16)


def project(sched, key_grads, pieces, half):
    tokens, width = key_grads.shape
    rest = half - T1
    return pl.pallas_call(
        functools.partial(project_body, half, rest),
        grid_spec=pltpu.PrefetchScalarGridSpec(
            num_scalar_prefetch=1,
            grid=(16,),
            in_specs=[pl.BlockSpec((tokens, width), lambda i, s: (0, 0))] + [pl.BlockSpec(memory_space=pl.ANY)] * 8,
            out_specs=pl.BlockSpec((tokens, half), lambda i, s: (0, s[i])),
            scratch_shapes=[
                pltpu.VMEM((16 * half, width), jnp.bfloat16),
                pltpu.SemaphoreType.DMA((16,)),
                pltpu.SemaphoreType.DMA((16,)),
            ],
        ),
        out_shape=jax.ShapeDtypeStruct((tokens, 16 * half), jnp.bfloat16),
        compiler_params=pltpu.CompilerParams(vmem_limit_bytes=40 * 1024 * 1024),
        cost_estimate=pl.CostEstimate(
            flops=2 * tokens * width * 16 * half, bytes_accessed=2 * 16 * half * (width + tokens), transcendentals=0
        ),
    )(sched, key_grads, *pieces)


def add16(a, b):
    return (a.astype(jnp.float32) + b.astype(jnp.float32)).astype(jnp.bfloat16)


def shards(acts, key_grads, key_weight):
    tokens, model = acts.shape
    norm = float((tokens * 128) ** -0.5)
    device = lax.axis_index(AXES)
    core = device % 2
    y_hi = device // 64
    mine = core == y_hi
    row = lax.dynamic_index_in_dim(jnp.asarray(table()), device, 0, keepdims=False)

    to_other = lax.dynamic_slice_in_dim(acts, (1 - core) * (model // 2), model // 2, axis=1)
    acts_got = move(to_other, ("core", "core"))
    kt_own = key_grads.T
    kt_got = move(kt_own, ("core", "core"))

    half = key_weight.shape[0] // 2
    own_half = lax.dynamic_slice_in_dim(key_weight, core * half, half, axis=0)
    gathered = []
    for stream in range(2):
        have = (own_half[:T1] if stream == 0 else own_half[T1:])[None]
        for stage in range(2):
            got = move(have, (AG[0][stream][stage], AG[1][stream][stage]))
            have = jnp.concatenate([have, got], axis=0)
        got = move(have, (AG[0][stream][2], AG[1][stream][2]))
        gathered += [have, got]
    swapped = [move(g, ("core", "core")) for g in gathered]

    lows = (0, S1, key_grads.shape[1])
    part = functools.partial(partial_blocks, core=core, acts=acts, acts_got=acts_got, kt_own=kt_own, kt_got=kt_got, norm=norm)
    sends, keeps = [], []
    for stream in range(2):
        idx = row[32 * stream : 32 * stream + 32]
        sends.append(part(idx[16:], low=lows[stream], high=lows[stream + 1]))
    for stream in range(2):
        idx = row[32 * stream : 32 * stream + 32]
        keeps.append(part(idx[:16], low=lows[stream], high=lows[stream + 1]))
    finals = []
    for stream in range(2):
        dims = [RS_A[k][stream] + RS_B[k][stream] for k in range(2)]
        send, keep = sends[stream], keeps[stream]
        for stage in range(5):
            got = move(send, (dims[0][stage], dims[1][stage]))
            n = keep.shape[0] // 2
            if stage < 4:
                send, keep = add16(keep[n:], got[n:]), add16(keep[:n], got[:n])
            else:
                finals.append(keep[0].astype(jnp.float32) + got[0].astype(jnp.float32))

    total = jnp.concatenate(finals, axis=0).T
    rows = total.shape[0] // 2
    for_me = lax.dynamic_slice_in_dim(total, core * rows, rows, axis=0)
    for_other = lax.dynamic_slice_in_dim(total, (1 - core) * rows, rows, axis=0)
    for_me16, for_other16 = for_me.astype(jnp.bfloat16), for_other.astype(jnp.bfloat16)
    local = move_some(for_other, True, ("core",))
    same = move_some(for_me16, False, ("yB",))
    cross = move_some(for_other16, False, ("yB", "core"))
    weight_grads = jnp.where(mine, for_me, 0.0) + local + same.astype(jnp.float32) + cross.astype(jnp.float32)

    own, other = row[64:80], row[80:96]
    cores = jnp.stack([core, 1 - core]).astype(jnp.int32)
    order = jnp.concatenate([own[:8] * 2 + core, other[:8] * 2 + 1 - core])
    sched = jnp.concatenate([order, own, other, cores]).astype(jnp.int32)
    input_grads = project(sched, key_grads, gathered + swapped, half)
    return input_grads, weight_grads


def solution(mesh):
    spec = P(AXES, None)
    return jax.shard_map(
        shards, mesh=mesh, in_specs=(spec, spec, P("intra", None)), out_specs=(spec, spec), check_vma=False
    )
```

time: 489 us -> 191 us (0.39)
  waiting for transfers between devices: 267 us -> 31.1 us
  local copies, waits for them, and re-layouts: 84.9 us -> 16.5 us
  starting transfers between devices: 26.4 us -> 83.4 us
  matrix products: 50.6 us -> 0 us
  Pallas kernels: 0 us -> 41.9 us
  other arithmetic: 44 us -> 16.3 us
  between operations: 14.1 us -> 0.97 us
    all_to_all x4 -> x0, waiting for transfers between devices: 267 us -> none  [the longest x1 240 us: shards(): lax.all_to_all(quantized, 'intra', split_axis=0, concat_axis=0, tiled=True)]
    ppermute x0 -> x25, starting transfers between devices: none -> 83.4 us  [the longest x22 70.7 us: move(): return lax.ppermute(value, AXES, pairs)]
    dot_general x2 -> x0, matrix products: 50.6 us -> none  [the longest x1 29.6 us: shards(): lax.dot_general(key_grads, lax.all_gather(key_weight, 'intra', axis=0, ti...]
    convert_element_type x6 -> x0, local copies, waits for them, and re-layouts: 44.7 us -> none  [the longest x1 40.6 us: from_codes(): quantized.reshape(groups, row_count, quantized.shape[1], 128)]
    pallas_call x0 -> x5, Pallas kernels: none -> 41.9 us  [the longest x4 25 us: partial_blocks(): pl.pallas_call(functools.partial(partial_body, low, high, norm), grid_spe...]
    reshape x1 -> x0, local copies, waits for them, and re-layouts: 33.6 us -> none  [shards(): partial_value.reshape(partial_value.shape[0], -1, 128)]
    ppermute x0 -> x25, waiting for transfers between devices: none -> 31.1 us  [the longest x22 31 us: move(): return lax.ppermute(value, AXES, pairs)]
    all_to_all x4 -> x0, starting transfers between devices: 26.4 us -> none  [the longest x1 8.37 us: shards(): lax.all_to_all(maxima.astype(jnp.bfloat16), 'intra', split_axis=0, concat...]
  transfers between devices with their start and end apart: 5 -> 25, of which waited for: 3 -> 8; matrix products, arithmetic and copies ran while one was open for 30% -> 10% of each run, Pallas kernels for 0% -> 22%
where the time goes in v1:
time: 191 us; the launch traced here: 190 us
  starting transfers between devices  83.4 us (44%)
  Pallas kernels  41.9 us (22%)
  waiting for transfers between devices  31.1 us (16%)
  local copies, waits for them, and re-layouts  16.5 us (9%)
  other arithmetic  16.3 us (9%)
    ppermute x22, starting transfers between devices, move(): return lax.ppermute(value, AXES, pairs)  70.7 us
    ppermute x22, waiting for transfers between devices, move(): return lax.ppermute(value, AXES, pairs)  31 us
    pallas_call x4, Pallas kernels, partial_blocks(): pl.pallas_call(functools.partial(partial_body, low, high, norm), grid_spe...  25 us
    pallas_call x1, Pallas kernels, project(): pl.pallas_call(functools.partial(project_body, half, rest), grid_spec=plt...  16.9 us
    ppermute x3, starting transfers between devices, move_some(): return lax.ppermute(value, AXES, pairs)  12.6 us
    unnamed x18, local copies, waits for them, and re-layouts  9.86 us
    convert_element_type x8, other arithmetic, add16(): return (a.astype(jnp.float32) + b.astype(jnp.float32)).astype(jnp.bfloat16)  7.1 us
    concatenate x4, other arithmetic, shards(): have = jnp.concatenate([have, got], axis=0)  6.3 us
  transfers between devices with their start and end apart: 25, of which 8 were waited for; matrix products, arithmetic and copies ran while one was open for 10% of the time, Pallas kernels for 22%

profile of v1, /device:TPU:1, one launch (start us, length us, event | category | flops | bytes accessed | tf_op | source)
XLA Modules:
  0.0 190.1 jit_solution(4293615902476568899)
XLA Ops:
  0.7 4.8 %constant_dynamic-slice_fusion = bf16[512,4096]{1,0:T(8,128)(2,1)} fusion(bf16[512,8192]{1,0:T(8,128)(2,1)} %refs_3_.7, s32[]{:T(128)S(6)} %select_n.43), kind=kLoop, calls=%fused_computation.35 | loop fusion | bytes 8388612 | tf_op jit(solution)/shard_map/dynamic_slice | solution.py:207
  9.5 2.8 %collective-permute-start = (bf16[1,336,1024]{2,1,0:T(8,128)(2,1)}, bf16[1,336,1024]{2,1,0:T(8,128)(2,1)}, u32[]{:S(2)}, u32[]{:S(2)}) collective-permute-start(bf16[1,336,1024]{2,1,0:T(8,128)(2,1)} %dynamic-slice_bitcast_fusion), channel_id=1, source_target_pairs={{0,32},{1,97},{2,34},{3,99},{4,36},{5,101},{6,38},{7,103},{8,40},{... | collective-permute-start | bytes 2064392 | tf_op jit(solution)/shard_map/ppermute | solution.py:77
  13.2 7.7 %collective-permute-done = bf16[1,336,1024]{2,1,0:T(8,128)(2,1)} collective-permute-done((bf16[1,336,1024]{2,1,0:T(8,128)(2,1)}, bf16[1,336,1024]{2,1,0:T(8,128)(2,1)}, u32[]{:S(2)}, u32[]{:S(2)}) %collective-permute-start) | collective-permute-done | bytes 688160 | tf_op jit(solution)/shard_map/ppermute | solution.py:77
  20.9 2.5 %pad_maximum_fusion.2 = bf16[2,336,1024]{2,1,0:T(8,128)(2,1)} fusion(bf16[1,336,1024]{2,1,0:T(8,128)(2,1)} %collective-permute-done, bf16[1,336,1024]{2,1,0:T(8,128)(2,1)} %dynamic-slice_bitcast_fusion), kind=kLoop, calls=%fused_computation.6 | loop fusion | flops 688128 | bytes 2752512 | tf_op jit(solution)/shard_map/concatenate | solution.py:219
  23.4 3.8 %collective-permute-start.1 = (bf16[2,336,1024]{2,1,0:T(8,128)(2,1)}, bf16[2,336,1024]{2,1,0:T(8,128)(2,1)}, u32[]{:S(2)}, u32[]{:S(2)}) collective-permute-start(bf16[2,336,1024]{2,1,0:T(8,128)(2,1)} %pad_maximum_fusion.2), channel_id=1, source_target_pairs={{0,96},{1,25},{2,98},{3,27},{4,100},{5,29},{6,102},{7,31},{8,104},... | collective-permute-start | bytes 4128776 | tf_op jit(solution)/shard_map/ppermute | solution.py:77
  27.2 3.4 %copy-done.2 = bf16[512,8192]{1,0:T(8,128)(2,1)S(1)} copy-done((bf16[512,8192]{1,0:T(8,128)(2,1)S(1)}, bf16[512,8192]{1,0:T(8,128)(2,1)}, u32[]{:S(2)}) %copy-start.2) | copy-done | bytes 8388632
  30.6 7.3 %shard_map.61 = bf16[16,640,128]{2,1,0:T(8,128)(2,1)} custom-call(s32[32]{0:T(128)S(1)} %pad_add_fusion.1.idx_ref, bf16[512,8192]{1,0:T(8,128)(2,1)S(1)} %copy-done.2, bf16[512,8192]{1,0:T(8,128)(2,1)S(1)} %copy-done.2, bf16[512,8192]{1,0:T(8,128)(2,1)S(1)} %copy-done.2, bf16[512,8192]{1,0:T(8,128)(2,1)S(1)} %copy-done.2, ...), custom_call_target="tpu_custom_call" | custom-call | flops 2684354560 | bytes 6815744 | tf_op jit(solution)/shard_map/pallas_call | solution.py:116
  40.4 2.9 %collective-permute-done.1 = bf16[2,336,1024]{2,1,0:T(8,128)(2,1)} collective-permute-done((bf16[2,336,1024]{2,1,0:T(8,128)(2,1)}, bf16[2,336,1024]{2,1,0:T(8,128)(2,1)}, u32[]{:S(2)}, u32[]{:S(2)}) %collective-permute-start.1) | collective-permute-done | bytes 1376288 | tf_op jit(solution)/shard_map/ppermute | solution.py:77
  43.2 3.6 %pad_maximum_fusion.refs_0_ = bf16[4,336,1024]{2,1,0:T(8,128)(2,1)} fusion(bf16[2,336,1024]{2,1,0:T(8,128)(2,1)} %collective-permute-done.1, bf16[1,336,1024]{2,1,0:T(8,128)(2,1)} %collective-permute-done, bf16[1,336,1024]{2,1,0:T(8,128)(2,1)} %dynamic-slice_bitcast_fusion), kind=kLoop, calls=%fused_computation | loop fusion | flops 2752512 | bytes 5505024 | tf_op jit(solution)/shard_map/concatenate | solution.py:219
  47.2 3.4 %copy-done.3 = bf16[512,8192]{1,0:T(8,128)(2,1)S(1)} copy-done((bf16[512,8192]{1,0:T(8,128)(2,1)S(1)}, bf16[512,8192]{1,0:T(8,128)(2,1)}, u32[]{:S(2)}) %copy-start.3) | copy-done | bytes 8388632
  50.6 5.6 %shard_map.63 = bf16[16,384,128]{2,1,0:T(8,128)(2,1)S(1)} custom-call(s32[32]{0:T(128)S(1)} %pad_add_fusion.3.idx_ref, bf16[512,8192]{1,0:T(8,128)(2,1)S(1)} %copy-done.3, bf16[512,8192]{1,0:T(8,128)(2,1)S(1)} %copy-done.3, bf16[512,8192]{1,0:T(8,128)(2,1)S(1)} %copy-done.3, bf16[512,8192]{1,0:T(8,128)(2,1)S(1)} %copy-done.3, ...), custom_call_target="tpu_custom_call" | custom-call | flops 1610612736 | bytes 5767168 | tf_op jit(solution)/shard_map/pallas_call | solution.py:116
  56.3 2.8 %collective-permute-start.3 = (bf16[1,176,1024]{2,1,0:T(8,128)(2,1)S(1)}, bf16[1,176,1024]{2,1,0:T(8,128)(2,1)S(1)}, u32[]{:S(2)}, u32[]{:S(2)}) collective-permute-start(bf16[1,176,1024]{2,1,0:T(8,128)(2,1)S(1)} %dynamic-slice_bitcast_fusion.1), channel_id=1, source_target_pairs={{0,24},{1,25},{2,26},{3,27},{4,28},{5,29},{6,30},{7,31},{8,16},{9,... | collective-permute-start | bytes 1081352 | tf_op jit(solution)/shard_map/ppermute | solution.py:77
  59.2 9.1 %collective-permute-done.3 = bf16[1,176,1024]{2,1,0:T(8,128)(2,1)S(1)} collective-permute-done((bf16[1,176,1024]{2,1,0:T(8,128)(2,1)S(1)}, bf16[1,176,1024]{2,1,0:T(8,128)(2,1)S(1)}, u32[]{:S(2)}, u32[]{:S(2)}) %collective-permute-start.3) | collective-permute-done | bytes 360480 | tf_op jit(solution)/shard_map/ppermute | solution.py:77
  69.8 6.5 %shard_map.60 = bf16[16,640,128]{2,1,0:T(8,128)(2,1)S(1)} custom-call(s32[32]{0:T(128)S(1)} %get-tuple-element.30.idx_ref, bf16[512,8192]{1,0:T(8,128)(2,1)S(1)} %copy-done.3, bf16[512,8192]{1,0:T(8,128)(2,1)S(1)} %copy-done.3, bf16[512,8192]{1,0:T(8,128)(2,1)S(1)} %copy-done.3, bf16[512,8192]{1,0:T(8,128)(2,1)S(1)} %copy-done.3, ...), custom_call_target="tpu_custom_call" | custom-call | flops 2684354560 | bytes 6815744 | tf_op jit(solution)/shard_map/pallas_call | solution.py:116
  79.6 5.6 %shard_map.62 = bf16[16,384,128]{2,1,0:T(8,128)(2,1)S(1)} custom-call(s32[32]{0:T(128)S(1)} %get-tuple-element.31.idx_ref, bf16[512,8192]{1,0:T(8,128)(2,1)S(1)} %copy-done.3, bf16[512,8192]{1,0:T(8,128)(2,1)S(1)} %copy-done.3, bf16[512,8192]{1,0:T(8,128)(2,1)S(1)} %copy-done.3, bf16[512,8192]{1,0:T(8,128)(2,1)S(1)} %copy-done.3, ...), custom_call_target="tpu_custom_call" | custom-call | flops 1610612736 | bytes 5767168 | tf_op jit(solution)/shard_map/pallas_call | solution.py:116
  85.3 2.8 %collective-permute-done.17 = bf16[16,384,128]{2,1,0:T(8,128)(2,1)S(1)} collective-permute-done((bf16[16,384,128]{2,1,0:T(8,128)(2,1)S(1)}, bf16[16,384,128]{2,1,0:T(8,128)(2,1)S(1)}, u32[]{:S(2)}, u32[]{:S(2)}) %collective-permute-start.17) | collective-permute-done | bytes 1572896 | tf_op jit(solution)/shard_map/ppermute | solution.py:77
  92.1 19.6 %collective-permute-start.6 = (bf16[4,336,1024]{2,1,0:T(8,128)(2,1)}, bf16[4,336,1024]{2,1,0:T(8,128)(2,1)}, u32[]{:S(2)}, u32[]{:S(2)}) collective-permute-start(bf16[4,336,1024]{2,1,0:T(8,128)(2,1)} %pad_maximum_fusion.refs_0_), channel_id=1, source_target_pairs={{0,1},{1,0},{2,3},{3,2},{4,5},{5,4},{6,7},{7,6},{8,9},{9,8},{10,11... | collective-permute-start | bytes 8257544 | tf_op jit(solution)/shard_map/ppermute | solution.py:77
  114.2 15.1 %collective-permute-start.8 = (bf16[4,176,1024]{2,1,0:T(8,128)(2,1)S(1)}, bf16[4,176,1024]{2,1,0:T(8,128)(2,1)}, u32[]{:S(2)}, u32[]{:S(2)}) collective-permute-start(bf16[4,176,1024]{2,1,0:T(8,128)(2,1)S(1)} %pad_maximum_fusion.1.refs_2_), channel_id=1, source_target_pairs={{0,1},{1,0},{2,3},{3,2},{4,5},{5,4},{6,7},{7,6},{8,9},{9,8},{10,11... | collective-permute-start | bytes 4325384 | tf_op jit(solution)/shard_map/ppermute | solution.py:77
  129.3 5.8 %collective-permute-start.9 = (bf16[4,176,1024]{2,1,0:T(8,128)(2,1)S(1)}, bf16[4,176,1024]{2,1,0:T(8,128)(2,1)}, u32[]{:S(2)}, u32[]{:S(2)}) collective-permute-start(bf16[4,176,1024]{2,1,0:T(8,128)(2,1)S(1)} %collective-permute-done.5.refs_3_), channel_id=1, source_target_pairs={{0,1},{1,0},{2,3},{3,2},{4,5},{5,4},{6,7},{7,6},{8,9},{9,8},{10,11... | collective-permute-start | bytes 4325384 | tf_op jit(solution)/shard_map/ppermute | solution.py:77
  135.8 3.0 %collective-permute-start.20 = (bf16[2,384,128]{2,1,0:T(8,128)(2,1)S(1)}, bf16[2,384,128]{2,1,0:T(8,128)(2,1)S(1)}, u32[]{:S(2)}, u32[]{:S(2)}) collective-permute-start(bf16[2,384,128]{2,1,0:T(8,128)(2,1)S(1)} %get-tuple-element.17), channel_id=1, source_target_pairs={{0,32},{1,25},{2,34},{3,27},{4,36},{5,29},{6,38},{7,31},{8,40},{9,... | collective-permute-start | bytes 589832 | tf_op jit(solution)/shard_map/ppermute | solution.py:77
  145.3 3.8 %collective-permute-done.15 = bf16[2,640,128]{2,1,0:T(8,128)(2,1)S(1)} collective-permute-done((bf16[2,640,128]{2,1,0:T(8,128)(2,1)}, bf16[2,640,128]{2,1,0:T(8,128)(2,1)S(1)}, u32[]{:S(2)}, u32[]{:S(2)}) %collective-permute-start.15) | collective-permute-done | bytes 327712 | tf_op jit(solution)/shard_map/ppermute | solution.py:77
  152.6 2.7 %collective-permute-start.16 = (bf16[1,640,128]{2,1,0:T(8,128)(2,1)S(1)}, bf16[1,640,128]{2,1,0:T(8,128)(2,1)S(1)}, u32[]{:S(2)}, u32[]{:S(2)}) collective-permute-start(bf16[1,640,128]{2,1,0:T(8,128)(2,1)S(1)} %add_convert_fusion.12), channel_id=1, source_target_pairs={{0,32},{1,25},{2,34},{3,27},{4,36},{5,29},{6,38},{7,31},{8,40},{9,... | collective-permute-start | bytes 491528 | tf_op jit(solution)/shard_map/ppermute | solution.py:77
  160.7 9.9 %collective-permute-start.24 = (bf16[64,1024]{0,1:T(8,128)(2,1)S(1)}, bf16[64,1024]{0,1:T(8,128)(2,1)S(1)}, u32[]{:S(2)}, u32[]{:S(2)}) collective-permute-start(bf16[64,1024]{0,1:T(8,128)(2,1)S(1)} %get-tuple-element.4), channel_id=1, source_target_pairs={{1,96},{3,98},{5,100},{7,102},{9,104},{11,106},{13,108},{15,110},{... | collective-permute-start | bytes 393224 | tf_op jit(solution)/shard_map/ppermute | solution.py:89
  172.1 16.9 %shard_map.59 = bf16[512,8192]{1,0:T(8,128)(2,1)} custom-call(s32[50]{0:T(128)S(1)} %concatenate.32.sched_ref, bf16[512,1024]{1,0:T(8,128)(2,1)S(1)} %copy-done.4, bf16[4,336,1024]{2,1,0:T(8,128)(2,1)} %pad_maximum_fusion.refs_0_, bf16[4,336,1024]{2,1,0:T(8,128)(2,1)} %collective-permute-done.2.refs_1_, bf16[4,176,1024]{2,1,0:T(8,128)(2,1)S(1)} %pad_maximum_fusion.1.refs_2_, ...), custom_call_target="tpu_custom_call" | custom-call | flops 8589934592 | bytes 25165824 | tf_op jit(solution)/shard_map/pallas_call | solution.py:173
  (77 shorter events, 38.0 us)
Async XLA Ops:
  5.5 21.7 %collective-permute-start.10 = (bf16[512,4096]{1,0:T(8,128)(2,1)}, bf16[512,4096]{1,0:T(8,128)(2,1)}, u32[]{:S(2)}, u32[]{:S(2)}) collective-permute-start(bf16[512,4096]{1,0:T(8,128)(2,1)} %constant_dynamic-slice_fusion), channel_id=1, source_target_pairs={{0,1},{1,0},{2,3},{3,2},{4,5},{5,4},{6,7},{7,6},{8,9},{9,8},{10,11... | collective-permute-start | bytes 12582920 | tf_op jit(solution)/shard_map/ppermute | solution.py:77
  8.4 18.8 %collective-permute-start.11 = (bf16[1024,512]{1,0:T(8,128)(2,1)S(1)}, bf16[1024,512]{1,0:T(8,128)(2,1)}, u32[]{:S(2)}, u32[]{:S(2)}) collective-permute-start(bf16[1024,512]{1,0:T(8,128)(2,1)S(1)} %bitcast.46), channel_id=1, source_target_pairs={{0,1},{1,0},{2,3},{3,2},{4,5},{5,4},{6,7},{7,6},{8,9},{9,8},{10,11... | collective-permute-start | bytes 3145736 | tf_op jit(solution)/shard_map/ppermute | solution.py:77
  9.5 11.5 %collective-permute-start = (bf16[1,336,1024]{2,1,0:T(8,128)(2,1)}, bf16[1,336,1024]{2,1,0:T(8,128)(2,1)}, u32[]{:S(2)}, u32[]{:S(2)}) collective-permute-start(bf16[1,336,1024]{2,1,0:T(8,128)(2,1)} %dynamic-slice_bitcast_fusion), channel_id=1, source_target_pairs={{0,32},{1,97},{2,34},{3,99},{4,36},{5,101},{6,38},{7,103},{8,40},{... | collective-permute-start | bytes 2064392 | tf_op jit(solution)/shard_map/ppermute | solution.py:77
  23.4 19.8 %collective-permute-start.1 = (bf16[2,336,1024]{2,1,0:T(8,128)(2,1)}, bf16[2,336,1024]{2,1,0:T(8,128)(2,1)}, u32[]{:S(2)}, u32[]{:S(2)}) collective-permute-start(bf16[2,336,1024]{2,1,0:T(8,128)(2,1)} %pad_maximum_fusion.2), channel_id=1, source_target_pairs={{0,96},{1,25},{2,98},{3,27},{4,100},{5,29},{6,102},{7,31},{8,104},... | collective-permute-start | bytes 4128776 | tf_op jit(solution)/shard_map/ppermute | solution.py:77
  37.9 38.4 %collective-permute-start.12 = (bf16[16,640,128]{2,1,0:T(8,128)(2,1)}, bf16[16,640,128]{2,1,0:T(8,128)(2,1)}, u32[]{:S(2)}, u32[]{:S(2)}) collective-permute-start(bf16[16,640,128]{2,1,0:T(8,128)(2,1)} %shard_map.61), channel_id=1, source_target_pairs={{0,2},{1,7},{2,0},{3,5},{4,6},{5,3},{6,4},{7,1},{8,10},{9,15},{10,... | collective-permute-start | bytes 7864328 | tf_op jit(solution)/shard_map/ppermute | solution.py:77
  46.8 65.0 %collective-permute-start.2 = (bf16[4,336,1024]{2,1,0:T(8,128)(2,1)}, bf16[4,336,1024]{2,1,0:T(8,128)(2,1)}, u32[]{:S(2)}, u32[]{:S(2)}) collective-permute-start(bf16[4,336,1024]{2,1,0:T(8,128)(2,1)} %pad_maximum_fusion.refs_0_), channel_id=1, source_target_pairs={{0,24},{1,33},{2,26},{3,35},{4,28},{5,37},{6,30},{7,39},{8,16},{9,... | collective-permute-start | bytes 8257544 | tf_op jit(solution)/shard_map/ppermute | solution.py:77
  56.2 31.8 %collective-permute-start.17 = (bf16[16,384,128]{2,1,0:T(8,128)(2,1)S(1)}, bf16[16,384,128]{2,1,0:T(8,128)(2,1)S(1)}, u32[]{:S(2)}, u32[]{:S(2)}) collective-permute-start(bf16[16,384,128]{2,1,0:T(8,128)(2,1)S(1)} %shard_map.63), channel_id=1, source_target_pairs={{0,8},{1,9},{2,10},{3,11},{4,12},{5,13},{6,14},{7,15},{8,0},{9,1},... | collective-permute-start | bytes 4718600 | tf_op jit(solution)/shard_map/ppermute | solution.py:77
  56.3 11.9 %collective-permute-start.3 = (bf16[1,176,1024]{2,1,0:T(8,128)(2,1)S(1)}, bf16[1,176,1024]{2,1,0:T(8,128)(2,1)S(1)}, u32[]{:S(2)}, u32[]{:S(2)}) collective-permute-start(bf16[1,176,1024]{2,1,0:T(8,128)(2,1)S(1)} %dynamic-slice_bitcast_fusion.1), channel_id=1, source_target_pairs={{0,24},{1,25},{2,26},{3,27},{4,28},{5,29},{6,30},{7,31},{8,16},{9,... | collective-permute-start | bytes 1081352 | tf_op jit(solution)/shard_map/ppermute | solution.py:77
  68.3 21.4 %collective-permute-start.4 = (bf16[2,176,1024]{2,1,0:T(8,128)(2,1)S(1)}, bf16[2,176,1024]{2,1,0:T(8,128)(2,1)S(1)}, u32[]{:S(2)}, u32[]{:S(2)}) collective-permute-start(bf16[2,176,1024]{2,1,0:T(8,128)(2,1)S(1)} %pad_maximum_fusion.3), channel_id=1, source_target_pairs={{0,32},{1,33},{2,34},{3,35},{4,36},{5,37},{6,38},{7,39},{8,40},{9,... | collective-permute-start | bytes 2162696 | tf_op jit(solution)/shard_map/ppermute | solution.py:77
  78.7 33.0 %collective-permute-start.13 = (bf16[8,640,128]{2,1,0:T(8,128)(2,1)S(1)}, bf16[8,640,128]{2,1,0:T(8,128)(2,1)S(1)}, u32[]{:S(2)}, u32[]{:S(2)}) collective-permute-start(bf16[8,640,128]{2,1,0:T(8,128)(2,1)S(1)} %get-tuple-element.7), channel_id=1, source_target_pairs={{0,6},{1,9},{2,4},{3,11},{4,2},{5,13},{6,0},{7,15},{8,14},{9,1},{1... | collective-permute-start | bytes 3932168 | tf_op jit(solution)/shard_map/ppermute | solution.py:77
  88.5 25.3 %collective-permute-start.18 = (bf16[8,384,128]{2,1,0:T(8,128)(2,1)S(1)}, bf16[8,384,128]{2,1,0:T(8,128)(2,1)S(1)}, u32[]{:S(2)}, u32[]{:S(2)}) collective-permute-start(bf16[8,384,128]{2,1,0:T(8,128)(2,1)S(1)} %get-tuple-element.9), channel_id=1, source_target_pairs={{0,2},{1,3},{2,0},{3,1},{4,6},{5,7},{6,4},{7,5},{8,10},{9,11},{10,... | collective-permute-start | bytes 2359304 | tf_op jit(solution)/shard_map/ppermute | solution.py:77
  89.9 24.3 %collective-permute-start.5 = (bf16[4,176,1024]{2,1,0:T(8,128)(2,1)S(1)}, bf16[4,176,1024]{2,1,0:T(8,128)(2,1)S(1)}, u32[]{:S(2)}, u32[]{:S(2)}) collective-permute-start(bf16[4,176,1024]{2,1,0:T(8,128)(2,1)S(1)} %pad_maximum_fusion.1.refs_2_), channel_id=1, source_target_pairs={{0,96},{1,97},{2,98},{3,99},{4,100},{5,101},{6,102},{7,103},{8,104... | collective-permute-start | bytes 4325384 | tf_op jit(solution)/shard_map/ppermute | solution.py:77
  92.1 79.9 %collective-permute-start.6 = (bf16[4,336,1024]{2,1,0:T(8,128)(2,1)}, bf16[4,336,1024]{2,1,0:T(8,128)(2,1)}, u32[]{:S(2)}, u32[]{:S(2)}) collective-permute-start(bf16[4,336,1024]{2,1,0:T(8,128)(2,1)} %pad_maximum_fusion.refs_0_), channel_id=1, source_target_pairs={{0,1},{1,0},{2,3},{3,2},{4,5},{5,4},{6,7},{7,6},{8,9},{9,8},{10,11... | collective-permute-start | bytes 8257544 | tf_op jit(solution)/shard_map/ppermute | solution.py:77
  111.7 60.3 %collective-permute-start.7 = (bf16[4,336,1024]{2,1,0:T(8,128)(2,1)}, bf16[4,336,1024]{2,1,0:T(8,128)(2,1)}, u32[]{:S(2)}, u32[]{:S(2)}) collective-permute-start(bf16[4,336,1024]{2,1,0:T(8,128)(2,1)} %collective-permute-done.2.refs_1_), channel_id=1, source_target_pairs={{0,1},{1,0},{2,3},{3,2},{4,5},{5,4},{6,7},{7,6},{8,9},{9,8},{10,11... | collective-permute-start | bytes 8257544 | tf_op jit(solution)/shard_map/ppermute | solution.py:77
  112.1 23.7 %collective-permute-start.14 = (bf16[4,640,128]{2,1,0:T(8,128)(2,1)S(1)}, bf16[4,640,128]{2,1,0:T(8,128)(2,1)S(1)}, u32[]{:S(2)}, u32[]{:S(2)}) collective-permute-start(bf16[4,640,128]{2,1,0:T(8,128)(2,1)S(1)} %get-tuple-element.11), channel_id=1, source_target_pairs={{0,8},{1,3},{2,10},{3,1},{4,12},{5,7},{6,14},{7,5},{8,0},{9,11},{1... | collective-permute-start | bytes 1966088 | tf_op jit(solution)/shard_map/ppermute | solution.py:77
  113.9 15.4 %collective-permute-start.19 = (bf16[4,384,128]{2,1,0:T(8,128)(2,1)S(1)}, bf16[4,384,128]{2,1,0:T(8,128)(2,1)S(1)}, u32[]{:S(2)}, u32[]{:S(2)}) collective-permute-start(bf16[4,384,128]{2,1,0:T(8,128)(2,1)S(1)} %get-tuple-element.13), channel_id=1, source_target_pairs={{0,6},{1,7},{2,4},{3,5},{4,2},{5,3},{6,0},{7,1},{8,14},{9,15},{10,... | collective-permute-start | bytes 1179656 | tf_op jit(solution)/shard_map/ppermute | solution.py:77
  114.2 46.4 %collective-permute-start.8 = (bf16[4,176,1024]{2,1,0:T(8,128)(2,1)S(1)}, bf16[4,176,1024]{2,1,0:T(8,128)(2,1)}, u32[]{:S(2)}, u32[]{:S(2)}) collective-permute-start(bf16[4,176,1024]{2,1,0:T(8,128)(2,1)S(1)} %pad_maximum_fusion.1.refs_2_), channel_id=1, source_target_pairs={{0,1},{1,0},{2,3},{3,2},{4,5},{5,4},{6,7},{7,6},{8,9},{9,8},{10,11... | collective-permute-start | bytes 4325384 | tf_op jit(solution)/shard_map/ppermute | solution.py:77
  129.3 41.2 %collective-permute-start.9 = (bf16[4,176,1024]{2,1,0:T(8,128)(2,1)S(1)}, bf16[4,176,1024]{2,1,0:T(8,128)(2,1)}, u32[]{:S(2)}, u32[]{:S(2)}) collective-permute-start(bf16[4,176,1024]{2,1,0:T(8,128)(2,1)S(1)} %collective-permute-done.5.refs_3_), channel_id=1, source_target_pairs={{0,1},{1,0},{2,3},{3,2},{4,5},{5,4},{6,7},{7,6},{8,9},{9,8},{10,11... | collective-permute-start | bytes 4325384 | tf_op jit(solution)/shard_map/ppermute | solution.py:77
  135.8 6.0 %collective-permute-start.20 = (bf16[2,384,128]{2,1,0:T(8,128)(2,1)S(1)}, bf16[2,384,128]{2,1,0:T(8,128)(2,1)S(1)}, u32[]{:S(2)}, u32[]{:S(2)}) collective-permute-start(bf16[2,384,128]{2,1,0:T(8,128)(2,1)S(1)} %get-tuple-element.17), channel_id=1, source_target_pairs={{0,32},{1,25},{2,34},{3,27},{4,36},{5,29},{6,38},{7,31},{8,40},{9,... | collective-permute-start | bytes 589832 | tf_op jit(solution)/shard_map/ppermute | solution.py:77
  142.5 6.6 %collective-permute-start.15 = (bf16[2,640,128]{2,1,0:T(8,128)(2,1)}, bf16[2,640,128]{2,1,0:T(8,128)(2,1)S(1)}, u32[]{:S(2)}, u32[]{:S(2)}) collective-permute-start(bf16[2,640,128]{2,1,0:T(8,128)(2,1)} %get-tuple-element.15), channel_id=1, source_target_pairs={{0,24},{1,33},{2,26},{3,35},{4,28},{5,37},{6,30},{7,39},{8,16},{9,... | collective-permute-start | bytes 983048 | tf_op jit(solution)/shard_map/ppermute | solution.py:77
  152.6 5.4 %collective-permute-start.16 = (bf16[1,640,128]{2,1,0:T(8,128)(2,1)S(1)}, bf16[1,640,128]{2,1,0:T(8,128)(2,1)S(1)}, u32[]{:S(2)}, u32[]{:S(2)}) collective-permute-start(bf16[1,640,128]{2,1,0:T(8,128)(2,1)S(1)} %add_convert_fusion.12), channel_id=1, source_target_pairs={{0,32},{1,25},{2,34},{3,27},{4,36},{5,29},{6,38},{7,31},{8,40},{9,... | collective-permute-start | bytes 491528 | tf_op jit(solution)/shard_map/ppermute | solution.py:77
  159.2 29.8 %collective-permute-start.22 = (f32[64,1024]{0,1:T(8,128)S(1)}, f32[64,1024]{0,1:T(8,128)S(1)}, u32[]{:S(2)}, u32[]{:S(2)}) collective-permute-start(f32[64,1024]{0,1:T(8,128)S(1)} %get-tuple-element.5), channel_id=1, source_target_pairs={{0,1},{2,3},{4,5},{6,7},{8,9},{10,11},{12,13},{14,15},{16,17},{18,... | collective-permute-start | bytes 786440 | tf_op jit(solution)/shard_map/ppermute | solution.py:89
  160.7 28.3 %collective-permute-start.24 = (bf16[64,1024]{0,1:T(8,128)(2,1)S(1)}, bf16[64,1024]{0,1:T(8,128)(2,1)S(1)}, u32[]{:S(2)}, u32[]{:S(2)}) collective-permute-start(bf16[64,1024]{0,1:T(8,128)(2,1)S(1)} %get-tuple-element.4), channel_id=1, source_target_pairs={{1,96},{3,98},{5,100},{7,102},{9,104},{11,106},{13,108},{15,110},{... | collective-permute-start | bytes 393224 | tf_op jit(solution)/shard_map/ppermute | solution.py:89
  170.5 18.4 %collective-permute-start.23 = (bf16[64,1024]{0,1:T(8,128)(2,1)S(1)}, bf16[64,1024]{0,1:T(8,128)(2,1)S(1)}, u32[]{:S(2)}, u32[]{:S(2)}) collective-permute-start(bf16[64,1024]{0,1:T(8,128)(2,1)S(1)} %convert_bitcast_fusion), channel_id=1, source_target_pairs={{1,97},{3,99},{5,101},{7,103},{9,105},{11,107},{13,109},{15,111},{... | collective-permute-start | bytes 393224 | tf_op jit(solution)/shard_map/ppermute | solution.py:89
  (9 other events, 94.0 us)

commit v2 on v1

v2 whole, which is shorter than its diff:
```python
import functools

import jax
import jax.numpy as jnp
import numpy as np
from jax import lax
from jax.experimental import pallas as pl
from jax.experimental.pallas import tpu as pltpu
from jax.sharding import PartitionSpec as P

SIZES = (4, 2, 2, 4, 2)
AXES = ("intra", "inter")
S1 = 640
T1 = 336
BLK = 128

RS_A = ((("xA", "xB", "zD"), ("zD", "xA", "xB")), (("xB", "zD", "xA"), ("zD", "xA", "xB")))
RS_B = ((("zC", "yA"), ("zC", "yA")), (("yA", "zC"), ("yA", "zC")))
AG = ((("yA", "yB", "zC"), ("zC", "yA", "yB")), (("yB", "zC", "yA"), ("zC", "yA", "yB")))


def coords(device):
    return tuple(int(v) for v in np.unravel_index(device, SIZES))


def ident(at):
    return int(np.ravel_multi_index(at, SIZES))


def flip(at, dim):
    y, zh, zl, x, c = at
    return {
        "yA": (y ^ 1, zh, zl, x, c),
        "yB": (3 - y, zh, zl, x, c),
        "zC": (y, zh ^ 1, zl ^ 1, x, c),
        "zD": (y, zh, zl ^ 1, x, c),
        "xA": (y, zh, zl, x ^ 1, c),
        "xB": (y, zh, zl, 3 - x, c),
        "core": (y, zh, zl, x, 1 - c),
    }[dim]


def blocks_of(device, stream):
    at = coords(device)
    core = at[4]
    base = at if (at[0] >> 1) == core else flip(at, "yB")
    out = []
    for j in range(32):
        owner = base
        for k, dim in enumerate(RS_A[core][stream] + RS_B[core][stream]):
            if (j >> (4 - k)) & 1:
                owner = flip(owner, dim)
        out.append(ident(owner) // 2)
    return out


def shards_of(device, stream):
    at = coords(device)
    out = []
    for j in range(8):
        holder = at
        for k, dim in enumerate(AG[at[4]][stream]):
            if (j >> k) & 1:
                holder = flip(holder, dim)
        out.append(holder[0] * 2 + holder[1])
    return out


def table():
    rows = []
    for device in range(128):
        other = device ^ 1
        first, second = blocks_of(device, 0), blocks_of(device, 1)
        row = blocks_of(other, 0) + first + second
        for base in (16, 0):
            groups = []
            for g in range(4):
                at = [first.index(v) for v in second[base + 4 * g : base + 4 * g + 4]]
                assert at[0] % 4 == 0 and at == list(range(at[0], at[0] + 4))
                groups.append(at[0] // 4)
            early = [max(g - 4, 0) for g in groups]
            late = [min(g, 3) for g in groups]
            row += [int(g >= 4) for g in groups]
            for g in range(1, 4):
                early[g] = early[g] if groups[g] >= 4 else early[g - 1]
                late[g] = late[g] if groups[g] < 4 else late[g - 1]
            row += early + late
        for gatherer in (device, other):
            core = gatherer % 2
            both = [shards_of(gatherer, stream) for stream in range(2)]
            row += [v * 2 + core for v in both[0]] + both[0] + both[1] + [core]
        rows.append(row)
    return np.array(rows, np.int32)


def move(value, dims_of_core):
    pairs = []
    for device in range(128):
        at = coords(device)
        pairs.append((device, ident(flip(at, dims_of_core[at[4]]))))
    return lax.ppermute(value, AXES, pairs)


def move_some(value, want_mine, dims):
    pairs = []
    for device in range(128):
        at = coords(device)
        if ((at[0] >> 1) == at[4]) == want_mine:
            to = at
            for dim in dims:
                to = flip(to, dim)
            pairs.append((device, ident(to)))
    return lax.ppermute(value, AXES, pairs)


VMEM = 56 * 1024 * 1024


def gather_body(idx_ref, *refs):
    for k in range(4):
        refs[4][0, :, k * BLK : (k + 1) * BLK] = refs[k][...]


def gather_blocks(idx, acts):
    tokens = acts.shape[0]
    groups = idx.shape[0] // 4
    specs = [pl.BlockSpec((tokens, BLK), functools.partial(lambda k, i, w: (0, w[4 * i + k]), k)) for k in range(4)]
    return pl.pallas_call(
        gather_body,
        grid_spec=pltpu.PrefetchScalarGridSpec(
            num_scalar_prefetch=1,
            grid=(groups,),
            in_specs=specs,
            out_specs=pl.BlockSpec((1, tokens, 4 * BLK), lambda i, w: (i, 0, 0)),
        ),
        out_shape=jax.ShapeDtypeStruct((groups, tokens, 4 * BLK), acts.dtype),
        compiler_params=pltpu.CompilerParams(vmem_limit_bytes=VMEM),
        cost_estimate=pl.CostEstimate(flops=0, bytes_accessed=1024, transcendentals=0),
    )(idx, *([acts] * 4))


def partial_body(low, high, norm, n_got, where_ref, *refs):
    own = jnp.concatenate([ref[...] for ref in refs[0:4]], axis=1)
    gots = refs[4 : 4 + n_got]
    kt_own, kt_got = refs[4 + n_got : 6 + n_got]
    out_ref = refs[-1]
    got = gots[0][0]
    if n_got == 2:
        step = pl.program_id(0)
        got = jnp.where(where_ref[4 * pl.num_programs(0) + step] == 1, got, gots[1][0])
    total = jnp.dot(kt_own[low:high, :], own, preferred_element_type=jnp.float32)
    total += jnp.dot(kt_got[low:high, :], got, preferred_element_type=jnp.float32)
    total = (total * norm).astype(jnp.bfloat16)
    for k in range(4):
        out_ref[k] = total[:, k * BLK : (k + 1) * BLK]


def partial_blocks(where, acts, gots, kt_own, kt_got, low, high, norm, after=()):
    tokens = acts.shape[0]
    groups = 4
    specs = [pl.BlockSpec((tokens, BLK), functools.partial(lambda k, i, w: (0, w[4 * i + k]), k)) for k in range(4)]
    if len(gots) == 1:
        specs += [pl.BlockSpec((1, tokens, 4 * BLK), lambda i, w: (i, 0, 0))]
    else:
        specs += [
            pl.BlockSpec((1, tokens, 4 * BLK), functools.partial(lambda k, i, w: (w[(5 + k) * groups + i], 0, 0), k))
            for k in range(2)
        ]
    specs += [pl.BlockSpec(kt_own.shape, lambda i, w: (0, 0))] * 2
    specs += [pl.BlockSpec(memory_space=pl.ANY)] * len(after)
    width = high - low
    return pl.pallas_call(
        functools.partial(partial_body, low, high, norm, len(gots)),
        grid_spec=pltpu.PrefetchScalarGridSpec(
            num_scalar_prefetch=1,
            grid=(groups,),
            in_specs=specs,
            out_specs=pl.BlockSpec((4, width, BLK), lambda i, w: (i, 0, 0)),
        ),
        out_shape=jax.ShapeDtypeStruct((4 * groups, width, BLK), jnp.bfloat16),
        compiler_params=pltpu.CompilerParams(vmem_limit_bytes=VMEM),
        cost_estimate=pl.CostEstimate(flops=0, bytes_accessed=1024, transcendentals=0),
    )(where, *([acts] * 4), *gots, kt_own, kt_got, *after)


def project_body(half, rest, n_last, sched_ref, kg_ref, *refs):
    pieces = refs[:4]
    out_ref, wbuf, sem_a, sem_b = refs[4 + n_last :]
    step = pl.program_id(0)

    def piece(stream, j):
        source = pieces[stream * 2 + j // 4].at[j % 4]
        rows = T1 if stream == 0 else rest
        first = sched_ref[8 + stream * 8 + j] * half + (0 if stream == 0 else T1)
        sem = (sem_a if stream == 0 else sem_b).at[j]
        return pltpu.make_async_copy(source, wbuf.at[pl.ds(pl.multiple_of(first, 16), rows), :], sem)

    @pl.when(step == 0)
    def _():
        for stream in (1, 0):
            for j in range(8):
                piece(stream, j).start()
        for j in range(8):
            piece(1, j).wait()

    for j in range(8):

        @pl.when(step == j)
        def _(j=j):
            piece(0, j).wait()

    start = pl.multiple_of(sched_ref[8 + step] * half, half)
    out_ref[...] = lax.dot_general(
        kg_ref[...], wbuf[pl.ds(start, half), :], (((1,), (1,)), ((), ())), preferred_element_type=jnp.float32
    ).astype(jnp.bfloat16)


def project(sched, key_grads, pieces, half, last=None):
    tokens, width = key_grads.shape
    rest = half - T1
    lasts = [] if last is None else [last]
    return pl.pallas_call(
        functools.partial(project_body, half, rest, len(lasts)),
        grid_spec=pltpu.PrefetchScalarGridSpec(
            num_scalar_prefetch=1,
            grid=(8,),
            in_specs=[pl.BlockSpec((tokens, width), lambda i, s: (0, 0))]
            + [pl.BlockSpec(memory_space=pl.ANY)] * (4 + len(lasts)),
            out_specs=pl.BlockSpec((tokens, half), lambda i, s: (0, s[i])),
            scratch_shapes=[
                pltpu.VMEM((8 * half, width), jnp.bfloat16),
                pltpu.SemaphoreType.DMA((8,)),
                pltpu.SemaphoreType.DMA((8,)),
            ],
        ),
        out_shape=jax.ShapeDtypeStruct((tokens, 16 * half), jnp.bfloat16),
        input_output_aliases={6: 0} if lasts else {},
        compiler_params=pltpu.CompilerParams(vmem_limit_bytes=VMEM),
        cost_estimate=pl.CostEstimate(flops=0, bytes_accessed=1024, transcendentals=0),
    )(sched, key_grads, *pieces, *lasts)


def add16(a, b):
    return (a.astype(jnp.float32) + b.astype(jnp.float32)).astype(jnp.bfloat16)


def shards(acts, key_grads, key_weight):
    tokens, model = acts.shape
    norm = float((tokens * 128) ** -0.5)
    device = lax.axis_index(AXES)
    core = device % 2
    y_hi = device // 64
    mine = core == y_hi
    row = lax.dynamic_index_in_dim(jnp.asarray(table()), device, 0, keepdims=False)

    half = key_weight.shape[0] // 2
    own_half = lax.dynamic_slice_in_dim(key_weight, core * half, half, axis=0)
    kt_own = key_grads.T
    kt_got = move(kt_own, ("core", "core"))
    early_sent, late_sent = gather_blocks(row[16:32], acts), gather_blocks(row[:16], acts)
    early, late = move(early_sent, ("core", "core")), move(late_sent, ("core", "core"))
    width = key_grads.shape[1]
    part = functools.partial(partial_blocks, acts=acts, kt_own=kt_own, kt_got=kt_got, norm=norm)
    first, second = row[32:64], row[64:96]
    part_second = part(jnp.concatenate([second[16:], row[96:108]]), gots=[early, late], low=S1, high=width)
    have = [own_half[None, :T1], own_half[None, T1:]]
    stages = []
    for stage in range(2):
        got = [move(have[k], (AG[0][k][stage], AG[1][k][stage])) for k in range(2)]
        if stage == 0:
            *got, late_sent = lax.optimization_barrier((*got, late_sent))
        else:
            *got, part_second = lax.optimization_barrier((*got, part_second))
        have = [jnp.concatenate([have[k], got[k]], axis=0) for k in range(2)]
        have = list(lax.optimization_barrier(tuple(have)))
        stages.append(have)
    got = [move(have[k], (AG[0][k][2], AG[1][k][2])) for k in range(2)]
    gathered = [have[0], got[0], have[1], got[1]]
    swapped = [move(g, ("core", "core")) for g in gathered]

    sends = [
        part(first[16:], gots=[early], low=0, high=S1, after=stages[0]),
        part_second,
    ]
    keeps = [
        part(first[:16], gots=[late], low=0, high=S1, after=stages[1]),
        part(jnp.concatenate([second[:16], row[108:120]]), gots=[early, late], low=S1, high=width),
    ]
    proj = project(row[120:145], key_grads, gathered, half)
    input_grads = project(row[145:170], key_grads, swapped, half, proj)
    before = [[], gathered, [proj], [input_grads], []]
    finals = []
    for stream in range(2):
        dims = [RS_A[k][stream] + RS_B[k][stream] for k in range(2)]
        send, keep = sends[stream], keeps[stream]
        for stage in range(5):
            got = move(send, (dims[0][stage], dims[1][stage]))
            if before[stage]:
                got, keep, *_ = lax.optimization_barrier((got, keep, *before[stage]))
            n = keep.shape[0] // 2
            if stage < 4:
                send, keep = add16(keep[n:], got[n:]), add16(keep[:n], got[:n])
            else:
                finals.append(keep[0].astype(jnp.float32) + got[0].astype(jnp.float32))

    total = jnp.concatenate(finals, axis=0).T
    rows = total.shape[0] // 2
    for_me = lax.dynamic_slice_in_dim(total, core * rows, rows, axis=0)
    for_other = lax.dynamic_slice_in_dim(total, (1 - core) * rows, rows, axis=0)
    for_me16, for_other16 = for_me.astype(jnp.bfloat16), for_other.astype(jnp.bfloat16)
    local = move_some(for_other, True, ("core",))
    same = move_some(for_me16, False, ("yB",))
    cross = move_some(for_other16, False, ("yB", "core"))
    weight_grads = jnp.where(mine, for_me, 0.0) + local + same.astype(jnp.float32) + cross.astype(jnp.float32)

    return input_grads, weight_grads


def solution(mesh):
    spec = P(AXES, None)
    return jax.shard_map(
        shards, mesh=mesh, in_specs=(spec, spec, P("intra", None)), out_specs=(spec, spec), check_vma=False
    )
```

time: 191 us -> 193 us (1.010)
  starting transfers between devices: 83.4 us -> 50.1 us
  Pallas kernels: 41.9 us -> 61.5 us
  waiting for transfers between devices: 31.1 us -> 47.2 us
  local copies, waits for them, and re-layouts: 16.5 us -> 9.54 us
  other arithmetic: 16.3 us -> 22.4 us
    ppermute x22 -> x23, starting transfers between devices: 70.7 us -> 37.8 us  [move(): return lax.ppermute(value, AXES, pairs)]
    pallas_call x5 -> x8, Pallas kernels: 41.9 us -> 61.5 us  [the longest x4 29.9 us: partial_blocks(): pl.pallas_call(functools.partial(partial_body, low, high, norm, len(gots)...]
    ppermute x22 -> x23, waiting for transfers between devices: 31 us -> 41.3 us  [move(): return lax.ppermute(value, AXES, pairs)]
    ppermute x3, waiting for transfers between devices: 0.01 us -> 5.87 us  [move_some(): return lax.ppermute(value, AXES, pairs)]
    dynamic_slice x2 -> x0, local copies, waits for them, and re-layouts: 5.54 us -> none  [the longest x1 4.85 us: shards(): lax.dynamic_slice_in_dim(acts, (1 - core) * (model // 2), model // 2, axi...]
    unnamed x18 -> x38, local copies, waits for them, and re-layouts: 9.86 us -> 5.65 us
    slice x1 -> x3, local copies, waits for them, and re-layouts: 0.07 us -> 3.82 us  [the longest x1 1.56 us: shards(): first[:16]]
    concatenate x7 -> x6, other arithmetic: 6.52 us -> 9.32 us  [the longest x4 8.11 us: shards(): have = [jnp.concatenate([have[k], got[k]], axis=0) for k in range(2)]]
  transfers between devices with their start and end apart: 25 -> 26, of which waited for: 8 -> 8; matrix products, arithmetic and copies ran while one was open for 10% -> 13% of each run, Pallas kernels for 22% -> 32%
where the time goes in v2:
time: 193 us; the launch traced here: 192 us
  Pallas kernels  61.5 us (32%)
  starting transfers between devices  50.1 us (26%)
  waiting for transfers between devices  47.2 us (24%)
  other arithmetic  22.4 us (12%)
  local copies, waits for them, and re-layouts  9.54 us (5%)
    ppermute x23, waiting for transfers between devices, move(): return lax.ppermute(value, AXES, pairs)  41.3 us
    ppermute x23, starting transfers between devices, move(): return lax.ppermute(value, AXES, pairs)  37.8 us
    pallas_call x4, Pallas kernels, partial_blocks(): pl.pallas_call(functools.partial(partial_body, low, high, norm, len(gots)...  29.9 us
    pallas_call x2, Pallas kernels, project(): pl.pallas_call(functools.partial(project_body, half, rest, len(lasts)), g...  22.2 us
    ppermute x3, starting transfers between devices, move_some(): return lax.ppermute(value, AXES, pairs)  12.2 us
    convert_element_type x8, other arithmetic, add16(): return (a.astype(jnp.float32) + b.astype(jnp.float32)).astype(jnp.bfloat16)  9.67 us
    pallas_call x2, Pallas kernels, gather_blocks(): pl.pallas_call(gather_body, grid_spec=pltpu.PrefetchScalarGridSpec(num_sc...  9.33 us
    concatenate x4, other arithmetic, shards(): have = [jnp.concatenate([have[k], got[k]], axis=0) for k in range(2)]  8.11 us
  transfers between devices with their start and end apart: 26, of which 8 were waited for; matrix products, arithmetic and copies ran while one was open for 13% of the time, Pallas kernels for 32%

profile of v2, /device:TPU:1, one launch (start us, length us, event | category | flops | bytes accessed | tf_op | source)
XLA Modules:
  0.0 191.8 jit_solution(1151126616880402469)
XLA Ops:
  2.3 3.6 %collective-permute-start = (bf16[1,336,1024]{2,1,0:T(8,128)(2,1)S(1)}, bf16[1,336,1024]{2,1,0:T(8,128)(2,1)S(1)}, u32[]{:S(2)}, u32[]{:S(2)}) collective-permute-start(bf16[1,336,1024]{2,1,0:T(8,128)(2,1)S(1)} %dynamic-slice_bitcast_fusion), channel_id=1, source_target_pairs={{0,32},{1,97},{2,34},{3,99},{4,36},{5,101},{6,38},{7,103},{8,40},{... | collective-permute-start | bytes 2064392 | tf_op jit(solution)/shard_map/ppermute | solution.py:101
  7.5 4.6 %shard_map.60 = bf16[4,512,512]{2,1,0:T(8,128)(2,1)} custom-call(s32[16]{0:T(128)} %get-tuple-element.63.idx_ref, bf16[512,8192]{1,0:T(8,128)(2,1)} %refs_3_.11, bf16[512,8192]{1,0:T(8,128)(2,1)} %refs_3_.11, bf16[512,8192]{1,0:T(8,128)(2,1)} %refs_3_.11, bf16[512,8192]{1,0:T(8,128)(2,1)} %refs_3_.11), custom_call_target="tpu_custom_call" | custom-call | bytes 1024 | tf_op jit(solution)/shard_map/pallas_call | solution.py:128
  12.2 4.7 %shard_map.59 = bf16[4,512,512]{2,1,0:T(8,128)(2,1)} custom-call(s32[16]{0:T(128)} %get-tuple-element.65.idx_ref, bf16[512,8192]{1,0:T(8,128)(2,1)} %refs_3_.11, bf16[512,8192]{1,0:T(8,128)(2,1)} %refs_3_.11, bf16[512,8192]{1,0:T(8,128)(2,1)} %refs_3_.11, bf16[512,8192]{1,0:T(8,128)(2,1)} %refs_3_.11), custom_call_target="tpu_custom_call" | custom-call | bytes 1024 | tf_op jit(solution)/shard_map/pallas_call | solution.py:128
  17.4 3.8 %collective-permute-start.1 = (bf16[1,176,1024]{2,1,0:T(8,128)(2,1)S(1)}, bf16[1,176,1024]{2,1,0:T(8,128)(2,1)S(1)}, u32[]{:S(2)}, u32[]{:S(2)}) collective-permute-start(bf16[1,176,1024]{2,1,0:T(8,128)(2,1)S(1)} %dynamic-slice_bitcast_fusion.1), channel_id=1, source_target_pairs={{0,24},{1,25},{2,26},{3,27},{4,28},{5,29},{6,30},{7,31},{8,16},{9,... | collective-permute-start | bytes 1081352 | tf_op jit(solution)/shard_map/ppermute | solution.py:101
  21.2 8.8 %collective-permute-done.1 = bf16[1,176,1024]{2,1,0:T(8,128)(2,1)S(1)} collective-permute-done((bf16[1,176,1024]{2,1,0:T(8,128)(2,1)S(1)}, bf16[1,176,1024]{2,1,0:T(8,128)(2,1)S(1)}, u32[]{:S(2)}, u32[]{:S(2)}) %collective-permute-start.1) | collective-permute-done | bytes 360480 | tf_op jit(solution)/shard_map/ppermute | solution.py:101
  33.3 2.5 %collective-permute-start.2 = (bf16[2,336,1024]{2,1,0:T(8,128)(2,1)S(1)}, bf16[2,336,1024]{2,1,0:T(8,128)(2,1)}, u32[]{:S(2)}, u32[]{:S(2)}) collective-permute-start(bf16[2,336,1024]{2,1,0:T(8,128)(2,1)S(1)} %pad_maximum_fusion.2.refs_7_), channel_id=1, source_target_pairs={{0,96},{1,25},{2,98},{3,27},{4,100},{5,29},{6,102},{7,31},{8,104},... | collective-permute-start | bytes 4128776 | tf_op jit(solution)/shard_map/ppermute | solution.py:101
  36.6 2.6 %collective-permute-done.6.refs_7_.refs_6_ = bf16[1024,512]{1,0:T(8,128)(2,1)S(1)} collective-permute-done((bf16[1024,512]{1,0:T(8,128)(2,1)S(1)}, bf16[1024,512]{1,0:T(8,128)(2,1)S(1)}, u32[]{:S(2)}, u32[]{:S(2)}) %collective-permute-start.6) | collective-permute-done | bytes 1048608 | tf_op jit(solution)/shard_map/ppermute | solution.py:101
  40.1 7.8 %shard_map.65 = bf16[16,640,128]{2,1,0:T(8,128)(2,1)} custom-call(s32[16]{0:T(128)} %get-tuple-element.62.where_ref, bf16[512,8192]{1,0:T(8,128)(2,1)} %refs_3_.11, bf16[512,8192]{1,0:T(8,128)(2,1)} %refs_3_.11, bf16[512,8192]{1,0:T(8,128)(2,1)} %refs_3_.11, bf16[512,8192]{1,0:T(8,128)(2,1)} %refs_3_.11, ...), custom_call_target="tpu_custom_call" | custom-call | bytes 1024 | tf_op jit(solution)/shard_map/pallas_call | solution.py:172
  51.9 7.1 %shard_map.61 = bf16[16,384,128]{2,1,0:T(8,128)(2,1)} custom-call(s32[28]{0:T(128)} %pad_add_fusion.where_ref, bf16[512,8192]{1,0:T(8,128)(2,1)} %refs_3_.11, bf16[512,8192]{1,0:T(8,128)(2,1)} %refs_3_.11, bf16[512,8192]{1,0:T(8,128)(2,1)} %refs_3_.11, bf16[512,8192]{1,0:T(8,128)(2,1)} %refs_3_.11, bf16[4,512,512]{2,1,0:T(8,128)(2,1)} %collective-permute-done.4.refs_4_, ...), custom_call_target="tpu_custom_call" | custom-call | bytes 1024 | tf_op jit(solution)/shard_map/pallas_call | solution.py:172
  61.5 3.2 %pad_maximum_fusion.refs_0_.refs_7_ = bf16[4,336,1024]{2,1,0:T(8,128)(2,1)} fusion(bf16[2,336,1024]{2,1,0:T(8,128)(2,1)} %collective-permute-done.2, bf16[2,336,1024]{2,1,0:T(8,128)(2,1)S(1)} %copy-done.5), kind=kLoop, calls=%fused_computation | loop fusion | flops 1376256 | bytes 5505024 | tf_op jit(solution)/shard_map/concatenate | solution.py:274
  66.7 7.9 %shard_map.64 = bf16[16,640,128]{2,1,0:T(8,128)(2,1)} custom-call(s32[16]{0:T(128)} %get-tuple-element.60.where_ref, bf16[512,8192]{1,0:T(8,128)(2,1)} %refs_3_.11, bf16[512,8192]{1,0:T(8,128)(2,1)} %refs_3_.11, bf16[512,8192]{1,0:T(8,128)(2,1)} %refs_3_.11, bf16[512,8192]{1,0:T(8,128)(2,1)} %refs_3_.11, ...), custom_call_target="tpu_custom_call" | custom-call | bytes 1024 | tf_op jit(solution)/shard_map/pallas_call | solution.py:172
  74.6 7.1 %shard_map.66 = bf16[16,384,128]{2,1,0:T(8,128)(2,1)} custom-call(s32[28]{0:T(128)} %pad_add_fusion.1.where_ref, bf16[512,8192]{1,0:T(8,128)(2,1)} %refs_3_.11, bf16[512,8192]{1,0:T(8,128)(2,1)} %refs_3_.11, bf16[512,8192]{1,0:T(8,128)(2,1)} %refs_3_.11, bf16[512,8192]{1,0:T(8,128)(2,1)} %refs_3_.11, bf16[4,512,512]{2,1,0:T(8,128)(2,1)} %collective-permute-done.4.refs_4_, ...), custom_call_target="tpu_custom_call" | custom-call | bytes 1024 | tf_op jit(solution)/shard_map/pallas_call | solution.py:172
  85.8 13.7 %collective-permute-done.18 = bf16[16,384,128]{2,1,0:T(8,128)(2,1)} collective-permute-done((bf16[16,384,128]{2,1,0:T(8,128)(2,1)S(1)}, bf16[16,384,128]{2,1,0:T(8,128)(2,1)}, u32[]{:S(2)}, u32[]{:S(2)}) %collective-permute-start.18) | collective-permute-done | bytes 1572896 | tf_op jit(solution)/shard_map/ppermute | solution.py:101
  101.3 4.6 %collective-permute-start.7 = (bf16[4,336,1024]{2,1,0:T(8,128)(2,1)}, bf16[4,336,1024]{2,1,0:T(8,128)(2,1)}, u32[]{:S(2)}, u32[]{:S(2)}) collective-permute-start(bf16[4,336,1024]{2,1,0:T(8,128)(2,1)} %pad_maximum_fusion.refs_0_.refs_7_), channel_id=1, source_target_pairs={{0,1},{1,0},{2,3},{3,2},{4,5},{5,4},{6,7},{7,6},{8,9},{9,8},{10,11... | collective-permute-start | bytes 8257544 | tf_op jit(solution)/shard_map/ppermute | solution.py:101
  106.0 10.3 %collective-permute-done.19 = bf16[8,384,128]{2,1,0:T(8,128)(2,1)S(1)} collective-permute-done((bf16[8,384,128]{2,1,0:T(8,128)(2,1)S(1)}, bf16[8,384,128]{2,1,0:T(8,128)(2,1)S(1)}, u32[]{:S(2)}, u32[]{:S(2)}) %collective-permute-start.19) | collective-permute-done | bytes 786464 | tf_op jit(solution)/shard_map/ppermute | solution.py:101
  117.2 5.0 %collective-permute-start.10 = (bf16[4,176,1024]{2,1,0:T(8,128)(2,1)}, bf16[4,176,1024]{2,1,0:T(8,128)(2,1)}, u32[]{:S(2)}, u32[]{:S(2)}) collective-permute-start(bf16[4,176,1024]{2,1,0:T(8,128)(2,1)} %pad_maximum_fusion.1.refs_2_.refs_8_), channel_id=1, source_target_pairs={{0,1},{1,0},{2,3},{3,2},{4,5},{5,4},{6,7},{7,6},{8,9},{9,8},{10,11... | collective-permute-start | bytes 4325384 | tf_op jit(solution)/shard_map/ppermute | solution.py:101
  127.3 11.1 %shard_map.62.refs_4_ = bf16[512,8192]{1,0:T(8,128)(2,1)} custom-call(s32[25]{0:T(128)} %get-tuple-element.68.sched_ref, bf16[512,1024]{1,0:T(8,128)(2,1)} %kg_ref.3, bf16[4,336,1024]{2,1,0:T(8,128)(2,1)} %pad_maximum_fusion.refs_0_.refs_7_, bf16[4,336,1024]{2,1,0:T(8,128)(2,1)} %copy-done.10, bf16[4,176,1024]{2,1,0:T(8,128)(2,1)} %pad_maximum_fusion.1.refs_2_.refs_8_, ...), custom_call_target="tpu_custom_call" | custom-call | bytes 1024 | tf_op jit(solution)/shard_map/pallas_call | solution.py:222
  140.5 6.4 %collective-permute-start.16 = (bf16[2,640,128]{2,1,0:T(8,128)(2,1)}, bf16[2,640,128]{2,1,0:T(8,128)(2,1)S(1)}, u32[]{:S(2)}, u32[]{:S(2)}) collective-permute-start(bf16[2,640,128]{2,1,0:T(8,128)(2,1)} %get-tuple-element.57), channel_id=1, source_target_pairs={{0,24},{1,33},{2,26},{3,35},{4,28},{5,37},{6,30},{7,39},{8,16},{9,... | collective-permute-start | bytes 983048 | tf_op jit(solution)/shard_map/ppermute | solution.py:101
  147.2 11.2 %shard_map.63 = bf16[512,8192]{1,0:T(8,128)(2,1)} custom-call(s32[25]{0:T(128)} %get-tuple-element.69.sched_ref, bf16[512,1024]{1,0:T(8,128)(2,1)} %kg_ref.3, bf16[4,336,1024]{2,1,0:T(8,128)(2,1)} %collective-permute-done.7.refs_0_, bf16[4,336,1024]{2,1,0:T(8,128)(2,1)} %collective-permute-done.9.refs_1_, ...), custom_call_target="tpu_custom_call", output_to_operand_aliasing={{}: (6, {})} | custom-call | bytes 1024 | tf_op jit(solution)/shard_map/pallas_call | solution.py:222
  159.3 5.4 %collective-permute-start.22 = (bf16[1,384,128]{2,1,0:T(8,128)(2,1)S(1)}, bf16[1,384,128]{2,1,0:T(8,128)(2,1)S(1)}, u32[]{:S(2)}, u32[]{:S(2)}) collective-permute-start(bf16[1,384,128]{2,1,0:T(8,128)(2,1)S(1)} %add_convert_fusion.14), channel_id=1, source_target_pairs={{0,32},{1,25},{2,34},{3,27},{4,36},{5,29},{6,38},{7,31},{8,40},{9,... | collective-permute-start | bytes 294920 | tf_op jit(solution)/shard_map/ppermute | solution.py:101
  167.7 2.6 %collective-permute-done.17 = bf16[1,640,128]{2,1,0:T(8,128)(2,1)S(1)} collective-permute-done((bf16[1,640,128]{2,1,0:T(8,128)(2,1)S(1)}, bf16[1,640,128]{2,1,0:T(8,128)(2,1)S(1)}, u32[]{:S(2)}, u32[]{:S(2)}) %collective-permute-start.17) | collective-permute-done | bytes 163872 | tf_op jit(solution)/shard_map/ppermute | solution.py:101
  172.7 7.9 %collective-permute-start.24 = (bf16[64,1024]{0,1:T(8,128)(2,1)}, bf16[64,1024]{0,1:T(8,128)(2,1)}, u32[]{:S(2)}, u32[]{:S(2)}) collective-permute-start(bf16[64,1024]{0,1:T(8,128)(2,1)} %convert_bitcast_fusion), channel_id=1, source_target_pairs={{1,97},{3,99},{5,101},{7,103},{9,105},{11,107},{13,109},{15,111},{... | collective-permute-start | bytes 393224 | tf_op jit(solution)/shard_map/ppermute | solution.py:113
  180.5 3.1 %collective-permute-start.25 = (bf16[64,1024]{0,1:T(8,128)(2,1)S(1)}, bf16[64,1024]{0,1:T(8,128)(2,1)}, u32[]{:S(2)}, u32[]{:S(2)}) collective-permute-start(bf16[64,1024]{0,1:T(8,128)(2,1)S(1)} %get-tuple-element.46), channel_id=1, source_target_pairs={{1,96},{3,98},{5,100},{7,102},{9,104},{11,106},{13,108},{15,110},{... | collective-permute-start | bytes 393224 | tf_op jit(solution)/shard_map/ppermute | solution.py:113
  183.7 5.9 %collective-permute-done.25 = bf16[64,1024]{0,1:T(8,128)(2,1)} collective-permute-done((bf16[64,1024]{0,1:T(8,128)(2,1)S(1)}, bf16[64,1024]{0,1:T(8,128)(2,1)}, u32[]{:S(2)}, u32[]{:S(2)}) %collective-permute-start.25) | collective-permute-done | bytes 131104 | tf_op jit(solution)/shard_map/ppermute | solution.py:113
  (98 shorter events, 40.1 us)
Async XLA Ops:
  2.3 27.7 %collective-permute-start = (bf16[1,336,1024]{2,1,0:T(8,128)(2,1)S(1)}, bf16[1,336,1024]{2,1,0:T(8,128)(2,1)S(1)}, u32[]{:S(2)}, u32[]{:S(2)}) collective-permute-start(bf16[1,336,1024]{2,1,0:T(8,128)(2,1)S(1)} %dynamic-slice_bitcast_fusion), channel_id=1, source_target_pairs={{0,32},{1,97},{2,34},{3,99},{4,36},{5,101},{6,38},{7,103},{8,40},{... | collective-permute-start | bytes 2064392 | tf_op jit(solution)/shard_map/ppermute | solution.py:101
  12.1 27.0 %collective-permute-start.4 = (bf16[4,512,512]{2,1,0:T(8,128)(2,1)}, bf16[4,512,512]{2,1,0:T(8,128)(2,1)}, u32[]{:S(2)}, u32[]{:S(2)}) collective-permute-start(bf16[4,512,512]{2,1,0:T(8,128)(2,1)} %shard_map.60), channel_id=1, source_target_pairs={{0,1},{1,0},{2,3},{3,2},{4,5},{5,4},{6,7},{7,6},{8,9},{9,8},{10,11... | collective-permute-start | bytes 6291464 | tf_op jit(solution)/shard_map/ppermute | solution.py:101
  16.8 35.1 %collective-permute-start.5 = (bf16[4,512,512]{2,1,0:T(8,128)(2,1)}, bf16[4,512,512]{2,1,0:T(8,128)(2,1)}, u32[]{:S(2)}, u32[]{:S(2)}) collective-permute-start(bf16[4,512,512]{2,1,0:T(8,128)(2,1)} %shard_map.59), channel_id=1, source_target_pairs={{0,1},{1,0},{2,3},{3,2},{4,5},{5,4},{6,7},{7,6},{8,9},{9,8},{10,11... | collective-permute-start | bytes 6291464 | tf_op jit(solution)/shard_map/ppermute | solution.py:101
  17.4 12.6 %collective-permute-start.1 = (bf16[1,176,1024]{2,1,0:T(8,128)(2,1)S(1)}, bf16[1,176,1024]{2,1,0:T(8,128)(2,1)S(1)}, u32[]{:S(2)}, u32[]{:S(2)}) collective-permute-start(bf16[1,176,1024]{2,1,0:T(8,128)(2,1)S(1)} %dynamic-slice_bitcast_fusion.1), channel_id=1, source_target_pairs={{0,24},{1,25},{2,26},{3,27},{4,28},{5,29},{6,30},{7,31},{8,16},{9,... | collective-permute-start | bytes 1081352 | tf_op jit(solution)/shard_map/ppermute | solution.py:101
  33.3 25.8 %collective-permute-start.2 = (bf16[2,336,1024]{2,1,0:T(8,128)(2,1)S(1)}, bf16[2,336,1024]{2,1,0:T(8,128)(2,1)}, u32[]{:S(2)}, u32[]{:S(2)}) collective-permute-start(bf16[2,336,1024]{2,1,0:T(8,128)(2,1)S(1)} %pad_maximum_fusion.2.refs_7_), channel_id=1, source_target_pairs={{0,96},{1,25},{2,98},{3,27},{4,100},{5,29},{6,102},{7,31},{8,104},... | collective-permute-start | bytes 4128776 | tf_op jit(solution)/shard_map/ppermute | solution.py:101
  36.5 22.6 %collective-permute-start.3 = (bf16[2,176,1024]{2,1,0:T(8,128)(2,1)}, bf16[2,176,1024]{2,1,0:T(8,128)(2,1)}, u32[]{:S(2)}, u32[]{:S(2)}) collective-permute-start(bf16[2,176,1024]{2,1,0:T(8,128)(2,1)} %pad_maximum_fusion.3.refs_8_), channel_id=1, source_target_pairs={{0,32},{1,33},{2,34},{3,35},{4,36},{5,37},{6,38},{7,39},{8,40},{9,... | collective-permute-start | bytes 2162696 | tf_op jit(solution)/shard_map/ppermute | solution.py:101
  47.9 33.8 %collective-permute-start.13 = (bf16[16,640,128]{2,1,0:T(8,128)(2,1)}, bf16[16,640,128]{2,1,0:T(8,128)(2,1)}, u32[]{:S(2)}, u32[]{:S(2)}) collective-permute-start(bf16[16,640,128]{2,1,0:T(8,128)(2,1)} %shard_map.65), channel_id=1, source_target_pairs={{0,2},{1,7},{2,0},{3,5},{4,6},{5,3},{6,4},{7,1},{8,10},{9,15},{10,... | collective-permute-start | bytes 7864328 | tf_op jit(solution)/shard_map/ppermute | solution.py:101
  64.7 41.2 %collective-permute-start.8 = (bf16[4,336,1024]{2,1,0:T(8,128)(2,1)}, bf16[4,336,1024]{2,1,0:T(8,128)(2,1)S(1)}, u32[]{:S(2)}, u32[]{:S(2)}) collective-permute-start(bf16[4,336,1024]{2,1,0:T(8,128)(2,1)} %pad_maximum_fusion.refs_0_.refs_7_), channel_id=1, source_target_pairs={{0,24},{1,33},{2,26},{3,35},{4,28},{5,37},{6,30},{7,39},{8,16},{9,... | collective-permute-start | bytes 8257544 | tf_op jit(solution)/shard_map/ppermute | solution.py:101
  64.7 34.7 %collective-permute-start.18 = (bf16[16,384,128]{2,1,0:T(8,128)(2,1)S(1)}, bf16[16,384,128]{2,1,0:T(8,128)(2,1)}, u32[]{:S(2)}, u32[]{:S(2)}) collective-permute-start(bf16[16,384,128]{2,1,0:T(8,128)(2,1)S(1)} %copy-done.12), channel_id=1, source_target_pairs={{0,8},{1,9},{2,10},{3,11},{4,12},{5,13},{6,14},{7,15},{8,0},{9,1},... | collective-permute-start | bytes 4718600 | tf_op jit(solution)/shard_map/ppermute | solution.py:101
  65.3 40.7 %collective-permute-start.11 = (bf16[4,176,1024]{2,1,0:T(8,128)(2,1)}, bf16[4,176,1024]{2,1,0:T(8,128)(2,1)}, u32[]{:S(2)}, u32[]{:S(2)}) collective-permute-start(bf16[4,176,1024]{2,1,0:T(8,128)(2,1)} %pad_maximum_fusion.1.refs_2_.refs_8_), channel_id=1, source_target_pairs={{0,96},{1,97},{2,98},{3,99},{4,100},{5,101},{6,102},{7,103},{8,104... | collective-permute-start | bytes 4325384 | tf_op jit(solution)/shard_map/ppermute | solution.py:101
  84.2 38.0 %collective-permute-start.14 = (bf16[8,640,128]{2,1,0:T(8,128)(2,1)S(1)}, bf16[8,640,128]{2,1,0:T(8,128)(2,1)S(1)}, u32[]{:S(2)}, u32[]{:S(2)}) collective-permute-start(bf16[8,640,128]{2,1,0:T(8,128)(2,1)S(1)} %get-tuple-element.49), channel_id=1, source_target_pairs={{0,6},{1,9},{2,4},{3,11},{4,2},{5,13},{6,0},{7,15},{8,14},{9,1},{1... | collective-permute-start | bytes 3932168 | tf_op jit(solution)/shard_map/ppermute | solution.py:101
  101.2 15.1 %collective-permute-start.19 = (bf16[8,384,128]{2,1,0:T(8,128)(2,1)S(1)}, bf16[8,384,128]{2,1,0:T(8,128)(2,1)S(1)}, u32[]{:S(2)}, u32[]{:S(2)}) collective-permute-start(bf16[8,384,128]{2,1,0:T(8,128)(2,1)S(1)} %get-tuple-element.51), channel_id=1, source_target_pairs={{0,2},{1,3},{2,0},{3,1},{4,6},{5,7},{6,4},{7,5},{8,10},{9,11},{10,... | collective-permute-start | bytes 2359304 | tf_op jit(solution)/shard_map/ppermute | solution.py:101
  101.3 45.8 %collective-permute-start.7 = (bf16[4,336,1024]{2,1,0:T(8,128)(2,1)}, bf16[4,336,1024]{2,1,0:T(8,128)(2,1)}, u32[]{:S(2)}, u32[]{:S(2)}) collective-permute-start(bf16[4,336,1024]{2,1,0:T(8,128)(2,1)} %pad_maximum_fusion.refs_0_.refs_7_), channel_id=1, source_target_pairs={{0,1},{1,0},{2,3},{3,2},{4,5},{5,4},{6,7},{7,6},{8,9},{9,8},{10,11... | collective-permute-start | bytes 8257544 | tf_op jit(solution)/shard_map/ppermute | solution.py:101
  105.9 41.3 %collective-permute-start.9 = (bf16[4,336,1024]{2,1,0:T(8,128)(2,1)S(1)}, bf16[4,336,1024]{2,1,0:T(8,128)(2,1)}, u32[]{:S(2)}, u32[]{:S(2)}) collective-permute-start(bf16[4,336,1024]{2,1,0:T(8,128)(2,1)S(1)} %collective-permute-done.8.refs_1_), channel_id=1, source_target_pairs={{0,1},{1,0},{2,3},{3,2},{4,5},{5,4},{6,7},{7,6},{8,9},{9,8},{10,11... | collective-permute-start | bytes 8257544 | tf_op jit(solution)/shard_map/ppermute | solution.py:101
  117.2 7.8 %collective-permute-start.20 = (bf16[4,384,128]{2,1,0:T(8,128)(2,1)S(1)}, bf16[4,384,128]{2,1,0:T(8,128)(2,1)S(1)}, u32[]{:S(2)}, u32[]{:S(2)}) collective-permute-start(bf16[4,384,128]{2,1,0:T(8,128)(2,1)S(1)} %get-tuple-element.55), channel_id=1, source_target_pairs={{0,6},{1,7},{2,4},{3,5},{4,2},{5,3},{6,0},{7,1},{8,14},{9,15},{10,... | collective-permute-start | bytes 1179656 | tf_op jit(solution)/shard_map/ppermute | solution.py:101
  117.2 29.8 %collective-permute-start.10 = (bf16[4,176,1024]{2,1,0:T(8,128)(2,1)}, bf16[4,176,1024]{2,1,0:T(8,128)(2,1)}, u32[]{:S(2)}, u32[]{:S(2)}) collective-permute-start(bf16[4,176,1024]{2,1,0:T(8,128)(2,1)} %pad_maximum_fusion.1.refs_2_.refs_8_), channel_id=1, source_target_pairs={{0,1},{1,0},{2,3},{3,2},{4,5},{5,4},{6,7},{7,6},{8,9},{9,8},{10,11... | collective-permute-start | bytes 4325384 | tf_op jit(solution)/shard_map/ppermute | solution.py:101
  122.2 24.9 %collective-permute-start.12 = (bf16[4,176,1024]{2,1,0:T(8,128)(2,1)}, bf16[4,176,1024]{2,1,0:T(8,128)(2,1)}, u32[]{:S(2)}, u32[]{:S(2)}) collective-permute-start(bf16[4,176,1024]{2,1,0:T(8,128)(2,1)} %collective-permute-done.11.refs_3_), channel_id=1, source_target_pairs={{0,1},{1,0},{2,3},{3,2},{4,5},{5,4},{6,7},{7,6},{8,9},{9,8},{10,11... | collective-permute-start | bytes 4325384 | tf_op jit(solution)/shard_map/ppermute | solution.py:101
  125.9 12.5 %collective-permute-start.15 = (bf16[4,640,128]{2,1,0:T(8,128)(2,1)}, bf16[4,640,128]{2,1,0:T(8,128)(2,1)}, u32[]{:S(2)}, u32[]{:S(2)}) collective-permute-start(bf16[4,640,128]{2,1,0:T(8,128)(2,1)} %get-tuple-element.53), channel_id=1, source_target_pairs={{0,8},{1,3},{2,10},{3,1},{4,12},{5,7},{6,14},{7,5},{8,0},{9,11},{1... | collective-permute-start | bytes 1966088 | tf_op jit(solution)/shard_map/ppermute | solution.py:101
  140.5 17.8 %collective-permute-start.16 = (bf16[2,640,128]{2,1,0:T(8,128)(2,1)}, bf16[2,640,128]{2,1,0:T(8,128)(2,1)S(1)}, u32[]{:S(2)}, u32[]{:S(2)}) collective-permute-start(bf16[2,640,128]{2,1,0:T(8,128)(2,1)} %get-tuple-element.57), channel_id=1, source_target_pairs={{0,24},{1,33},{2,26},{3,35},{4,28},{5,37},{6,30},{7,39},{8,16},{9,... | collective-permute-start | bytes 983048 | tf_op jit(solution)/shard_map/ppermute | solution.py:101
  147.0 11.4 %collective-permute-start.21 = (bf16[2,384,128]{2,1,0:T(8,128)(2,1)S(1)}, bf16[2,384,128]{2,1,0:T(8,128)(2,1)}, u32[]{:S(2)}, u32[]{:S(2)}) collective-permute-start(bf16[2,384,128]{2,1,0:T(8,128)(2,1)S(1)} %get-tuple-element.59), channel_id=1, source_target_pairs={{0,24},{1,33},{2,26},{3,35},{4,28},{5,37},{6,30},{7,39},{8,16},{9,... | collective-permute-start | bytes 589832 | tf_op jit(solution)/shard_map/ppermute | solution.py:101
  159.3 7.4 %collective-permute-start.22 = (bf16[1,384,128]{2,1,0:T(8,128)(2,1)S(1)}, bf16[1,384,128]{2,1,0:T(8,128)(2,1)S(1)}, u32[]{:S(2)}, u32[]{:S(2)}) collective-permute-start(bf16[1,384,128]{2,1,0:T(8,128)(2,1)S(1)} %add_convert_fusion.14), channel_id=1, source_target_pairs={{0,32},{1,25},{2,34},{3,27},{4,36},{5,29},{6,38},{7,31},{8,40},{9,... | collective-permute-start | bytes 294920 | tf_op jit(solution)/shard_map/ppermute | solution.py:101
  170.5 19.0 %collective-permute-start.23 = (f32[64,1024]{0,1:T(8,128)S(1)}, f32[64,1024]{0,1:T(8,128)}, u32[]{:S(2)}, u32[]{:S(2)}) collective-permute-start(f32[64,1024]{0,1:T(8,128)S(1)} %get-tuple-element.47), channel_id=1, source_target_pairs={{0,1},{2,3},{4,5},{6,7},{8,9},{10,11},{12,13},{14,15},{16,17},{18,... | collective-permute-start | bytes 786440 | tf_op jit(solution)/shard_map/ppermute | solution.py:113
  172.7 11.0 %collective-permute-start.24 = (bf16[64,1024]{0,1:T(8,128)(2,1)}, bf16[64,1024]{0,1:T(8,128)(2,1)}, u32[]{:S(2)}, u32[]{:S(2)}) collective-permute-start(bf16[64,1024]{0,1:T(8,128)(2,1)} %convert_bitcast_fusion), channel_id=1, source_target_pairs={{1,97},{3,99},{5,101},{7,103},{9,105},{11,107},{13,109},{15,111},{... | collective-permute-start | bytes 393224 | tf_op jit(solution)/shard_map/ppermute | solution.py:113
  180.5 9.0 %collective-permute-start.25 = (bf16[64,1024]{0,1:T(8,128)(2,1)S(1)}, bf16[64,1024]{0,1:T(8,128)(2,1)}, u32[]{:S(2)}, u32[]{:S(2)}) collective-permute-start(bf16[64,1024]{0,1:T(8,128)(2,1)S(1)} %get-tuple-element.46), channel_id=1, source_target_pairs={{1,96},{3,98},{5,100},{7,102},{9,104},{11,106},{13,108},{15,110},{... | collective-permute-start | bytes 393224 | tf_op jit(solution)/shard_map/ppermute | solution.py:113
  (20 other events, 145.0 us)

commit v3 on v0

v3 whole, which is shorter than its diff:
```python
import functools

import jax
import jax.numpy as jnp
import numpy as np
from jax import lax
from jax.experimental import pallas as pl
from jax.experimental.pallas import tpu as pltpu
from jax.sharding import PartitionSpec as P

SIZES = (4, 2, 2, 4, 2)
AXES = ("intra", "inter")
S1 = 688
T1 = 336
BLK = 128

RS_A = ((("xA", "xB", "zD"), ("zD", "xA", "xB")), (("xB", "zD", "xA"), ("zD", "xA", "xB")))
RS_B = ((("zC", "yA"), ("zC", "yA")), (("zC", "yA"), ("zC", "yA")))
PROJECT = ((0, 1), (1, 1))
AG = ((("yA", "yB", "zC"), ("zC", "yA", "yB")), (("yB", "zC", "yA"), ("zC", "yA", "yB")))


def coords(device):
    return tuple(int(v) for v in np.unravel_index(device, SIZES))


def ident(at):
    return int(np.ravel_multi_index(at, SIZES))


def flip(at, dim):
    y, zh, zl, x, c = at
    return {
        "yA": (y ^ 1, zh, zl, x, c),
        "yB": (3 - y, zh, zl, x, c),
        "zC": (y, zh ^ 1, zl ^ 1, x, c),
        "zD": (y, zh, zl ^ 1, x, c),
        "xA": (y, zh, zl, x ^ 1, c),
        "xB": (y, zh, zl, 3 - x, c),
        "core": (y, zh, zl, x, 1 - c),
    }[dim]


def blocks_of(device, stream):
    at = coords(device)
    core = at[4]
    base = at if (at[0] >> 1) == core else flip(at, "yB")
    out = []
    for j in range(32):
        owner = base
        for k, dim in enumerate(RS_A[core][stream] + RS_B[core][stream]):
            if (j >> (4 - k)) & 1:
                owner = flip(owner, dim)
        out.append(ident(owner) // 2)
    return out


def shards_of(device, stream):
    at = coords(device)
    out = []
    for j in range(8):
        holder = at
        for k, dim in enumerate(AG[at[4]][stream]):
            if (j >> k) & 1:
                holder = flip(holder, dim)
        out.append(holder[0] * 2 + holder[1])
    return out


def table():
    rows = []
    for device in range(128):
        other = device ^ 1
        row = []
        for stream in range(2):
            order = blocks_of(device, stream)
            row += [order.index(block + 32 * (device % 2)) for block in range(32)]
        for gatherer in (device, other):
            core = gatherer % 2
            both = [shards_of(gatherer, stream) for stream in range(2)]
            row += [v * 2 + core for v in both[0]] + [both[1].index(v) for v in both[0]]
        rows.append(row)
    return np.array(rows, np.int32)


def move(value, dims_of_core):
    pairs = []
    for device in range(128):
        at = coords(device)
        pairs.append((device, ident(flip(at, dims_of_core[at[4]]))))
    return lax.ppermute(value, AXES, pairs)


def deliver(value, dims, k):
    pairs = []
    for device in range(128):
        at = coords(device)
        y_hi = at[0] >> 1
        to = at if y_hi == at[4] else flip(at, "yB")
        for dim in dims:
            to = flip(to, dim)
        pairs.append((device, ident((*to[:4], y_hi ^ k))))
    return lax.ppermute(value, AXES, pairs)


VMEM = 56 * 1024 * 1024


def front_body(core_ref, acts, weight, own_a, own_b, act_a, act_b, wbuf, abuf, sems):
    half = weight.shape[0] // 2
    part = act_a.shape[1]
    core = core_ref[0]
    rows = pl.multiple_of(core * half, half)
    columns = pl.multiple_of((1 - core) * 2 * part, part)
    loads = [pltpu.make_async_copy(weight.at[pl.ds(rows, half)], wbuf, sems.at[0])] + [
        pltpu.make_async_copy(acts.at[:, pl.ds(columns + k * part, part)], abuf.at[k], sems.at[1 + k]) for k in range(2)
    ]
    stores = [
        pltpu.make_async_copy(wbuf.at[pl.ds(0, T1)], own_a.at[0], sems.at[3]),
        pltpu.make_async_copy(wbuf.at[pl.ds(T1, half - T1)], own_b.at[0], sems.at[4]),
        pltpu.make_async_copy(abuf.at[0], act_a, sems.at[5]),
        pltpu.make_async_copy(abuf.at[1], act_b, sems.at[6]),
    ]
    for load in loads:
        load.start()
    loads[0].wait()
    stores[0].start()
    stores[1].start()
    for k in range(2):
        loads[1 + k].wait()
        stores[2 + k].start()
    for store in stores:
        store.wait()


def front(core, acts, weight):
    tokens, model = acts.shape
    rows, width = weight.shape
    half, part = rows // 2, model // 4
    shapes = [(1, T1, width), (1, half - T1, width), (tokens, part), (tokens, part)]
    return pl.pallas_call(
        front_body,
        in_specs=[pl.BlockSpec(memory_space=pltpu.SMEM)] + [pl.BlockSpec(memory_space=pl.ANY)] * 2,
        out_specs=[pl.BlockSpec(memory_space=pl.ANY)] * 4,
        scratch_shapes=[
            pltpu.VMEM((half, width), jnp.bfloat16),
            pltpu.VMEM((2, tokens, part), jnp.bfloat16),
            pltpu.SemaphoreType.DMA((7,)),
        ],
        out_shape=[jax.ShapeDtypeStruct(shape, jnp.bfloat16) for shape in shapes],
        compiler_params=pltpu.CompilerParams(vmem_limit_bytes=VMEM),
        cost_estimate=pl.CostEstimate(flops=0, bytes_accessed=1024, transcendentals=0),
    )(core, acts, weight)


CHUNK = 4 * BLK
TILE = 256


def partial_body(norm, n_chunks, where_ref, acts, got_a, got_b, kt_own, kt_got, *refs):
    outs, rhs, kt, outbuf, sem_in, sem_kt, sem_out = refs[:4], *refs[4:]
    tokens = acts.shape[0]
    n_blocks = 4 * n_chunks
    base = where_ref[2 * n_blocks] * (n_chunks * CHUNK)
    lows = (0, S1, kt.shape[0])

    def own_copy(g):
        start = pl.multiple_of(base + g * CHUNK, CHUNK)
        return pltpu.make_async_copy(acts.at[:, pl.ds(start, CHUNK)], rhs.at[g, pl.ds(0, tokens), :], sem_in.at[2 * g])

    def got_copy(g):
        source = got_a if g < n_chunks // 2 else got_b
        start = (g % (n_chunks // 2)) * CHUNK
        return pltpu.make_async_copy(
            source.at[:, pl.ds(start, CHUNK)], rhs.at[g, pl.ds(tokens, tokens), :], sem_in.at[2 * g + 1]
        )

    def kt_copy(which):
        return pltpu.make_async_copy((kt_own, kt_got)[which], kt.at[:, pl.ds(which * tokens, tokens)], sem_kt.at[which])

    def out_copy(block, stream, target):
        source = outbuf.at[block, pl.ds(lows[stream], lows[stream + 1] - lows[stream]), :]
        return pltpu.make_async_copy(source, target, sem_out.at[2 * block + stream])

    def load(g):
        own_copy(g).start()
        got_copy(g).start()

    kt_copy(0).start()
    kt_copy(1).start()
    for g in range(3):
        load(g)
    kt_copy(0).wait()
    kt_copy(1).wait()
    for g in range(n_chunks):
        own_copy(g).wait()
        got_copy(g).wait()
        if g + 3 < n_chunks:
            load(g + 3)
        for row in range(0, kt.shape[0], TILE):
            total = jnp.dot(kt[row : row + TILE, :], rhs[g], preferred_element_type=jnp.float32)
            total = (total * norm).astype(jnp.bfloat16)
            for k in range(4):
                outbuf[4 * g + k, row : row + TILE, :] = total[:, k * BLK : (k + 1) * BLK]
        for k in range(4):
            block = 4 * g + k
            for stream in range(2):
                place = where_ref[stream * n_blocks + block]

                @pl.when(place >= n_blocks // 2)
                def _(block=block, stream=stream, place=place):
                    out_copy(block, stream, outs[2 * stream].at[place - n_blocks // 2]).start()

                @pl.when(place < n_blocks // 2)
                def _(block=block, stream=stream, place=place):
                    out_copy(block, stream, outs[2 * stream + 1].at[place]).start()

    for block in range(n_blocks):
        for stream in range(2):
            out_copy(block, stream, outs[2 * stream].at[0]).wait()


def partial_blocks(where, acts, got_a, got_b, kt_own, kt_got, norm, before=()):
    tokens, model = acts.shape
    width = kt_own.shape[0]
    n_chunks = model // 2 // CHUNK
    widths = (S1, S1, width - S1, width - S1)
    n_before = len(before)

    def body(where_ref, *refs):
        partial_body(norm, n_chunks, where_ref, *refs[:5], *refs[5 + n_before :])

    return pl.pallas_call(
        body,
        in_specs=[pl.BlockSpec(memory_space=pltpu.SMEM)] + [pl.BlockSpec(memory_space=pl.ANY)] * (5 + n_before),
        out_specs=[pl.BlockSpec(memory_space=pl.ANY)] * 4,
        scratch_shapes=[
            pltpu.VMEM((n_chunks, 2 * tokens, CHUNK), jnp.bfloat16),
            pltpu.VMEM((width, 2 * tokens), jnp.bfloat16),
            pltpu.VMEM((4 * n_chunks, width, BLK), jnp.bfloat16),
            pltpu.SemaphoreType.DMA((2 * n_chunks,)),
            pltpu.SemaphoreType.DMA((2,)),
            pltpu.SemaphoreType.DMA((8 * n_chunks,)),
        ],
        out_shape=[jax.ShapeDtypeStruct((2 * n_chunks, w, BLK), jnp.bfloat16) for w in widths],
        compiler_params=pltpu.CompilerParams(vmem_limit_bytes=VMEM),
        cost_estimate=pl.CostEstimate(flops=0, bytes_accessed=1024, transcendentals=0),
    )(where, acts, got_a, got_b, kt_own, kt_got, *before)


def project_body(half, rest, n_last, sched_ref, kg_ref, *refs):
    pieces = refs[:4]
    out, wbuf, outbuf, sem_a, sem_b, sem_out = refs[4 + n_last :]

    def first(j):
        return pltpu.make_async_copy(pieces[j // 4].at[j % 4], wbuf.at[j, pl.ds(0, T1), :], sem_a.at[j])

    def second(j, source):
        return pltpu.make_async_copy(source, wbuf.at[j, pl.ds(T1, rest), :], sem_b.at[j])

    def load(j):
        first(j).start()
        place = sched_ref[8 + j]
        for which in range(2):

            @pl.when(place // 4 == which)
            def _(which=which):
                second(j, pieces[2 + which].at[place % 4]).start()

    def out_copy(j):
        start = pl.multiple_of(sched_ref[j] * half, half)
        return pltpu.make_async_copy(outbuf.at[j], out.at[:, pl.ds(start, half)], sem_out.at[j])

    for j in range(2):
        load(j)
    for j in range(8):
        first(j).wait()
        second(j, pieces[2].at[0]).wait()
        if j + 2 < 8:
            load(j + 2)
        for row in range(0, half, TILE):
            outbuf[j, :, row : row + TILE] = lax.dot_general(
                kg_ref[...], wbuf[j, row : row + TILE, :], (((1,), (1,)), ((), ())), preferred_element_type=jnp.float32
            ).astype(jnp.bfloat16)
        out_copy(j).start()
    for j in range(8):
        out_copy(j).wait()


def project(sched, kg, pieces, half, last=None):
    tokens, width = kg.shape
    rest = half - T1
    lasts = [] if last is None else [last]
    return pl.pallas_call(
        functools.partial(project_body, half, rest, len(lasts)),
        in_specs=[pl.BlockSpec(memory_space=pltpu.SMEM), pl.BlockSpec(memory_space=pltpu.VMEM)]
        + [pl.BlockSpec(memory_space=pl.ANY)] * (4 + len(lasts)),
        out_specs=pl.BlockSpec(memory_space=pl.ANY),
        scratch_shapes=[
            pltpu.VMEM((8, half, width), jnp.bfloat16),
            pltpu.VMEM((8, tokens, half), jnp.bfloat16),
            pltpu.SemaphoreType.DMA((8,)),
            pltpu.SemaphoreType.DMA((8,)),
            pltpu.SemaphoreType.DMA((8,)),
        ],
        out_shape=jax.ShapeDtypeStruct((tokens, 16 * half), jnp.bfloat16),
        input_output_aliases={6: 0} if lasts else {},
        compiler_params=pltpu.CompilerParams(vmem_limit_bytes=VMEM),
        cost_estimate=pl.CostEstimate(flops=16 * tokens * width * half, bytes_accessed=30 * 1024 * 1024, transcendentals=0),
    )(sched, kg, *pieces, *lasts)


def join_body(n_in, *refs):
    ins, outs, bufs, sems = refs[:n_in], refs[n_in : n_in + n_in // 2], refs[n_in + n_in // 2 : -1], refs[-1]

    def load(k):
        count = ins[k].shape[0]
        return pltpu.make_async_copy(ins[k], bufs[k // 2].at[pl.ds((k % 2) * count, count)], sems.at[k])

    def store(k):
        return pltpu.make_async_copy(bufs[k], outs[k], sems.at[n_in + k])

    for k in range(n_in):
        load(k).start()
    for k in range(n_in // 2):
        load(2 * k).wait()
        load(2 * k + 1).wait()
        store(k).start()
    for k in range(n_in // 2):
        store(k).wait()


def join(pairs):
    ins = [v for pair in pairs for v in pair]
    shapes = [(2 * a.shape[0], *a.shape[1:]) for a, _ in pairs]
    return list(
        pl.pallas_call(
            functools.partial(join_body, len(ins)),
            in_specs=[pl.BlockSpec(memory_space=pl.ANY)] * len(ins),
            out_specs=[pl.BlockSpec(memory_space=pl.ANY)] * len(pairs),
            scratch_shapes=[pltpu.VMEM(shape, jnp.bfloat16) for shape in shapes]
            + [pltpu.SemaphoreType.DMA((len(ins) + len(pairs),))],
            out_shape=[jax.ShapeDtypeStruct(shape, jnp.bfloat16) for shape in shapes],
            compiler_params=pltpu.CompilerParams(vmem_limit_bytes=VMEM),
            cost_estimate=pl.CostEstimate(flops=0, bytes_accessed=1024, transcendentals=0),
        )(*ins)
    )


def split_body(y_hi_ref, *refs):
    ins, outs, whole = refs[:4], refs[4:12], refs[12]
    for j in range(4):
        low = 0
        for stream in range(2):
            keep, got = ins[2 * stream], ins[2 * stream + 1]
            width = keep.shape[1]
            whole[low : low + width, :] = keep[j].astype(jnp.float32) + got[j].astype(jnp.float32)
            low += width
        turned = whole[...].T.astype(jnp.bfloat16)
        half = turned.shape[0] // 2
        for k in range(2):
            outs[2 * j + k][...] = jnp.where(y_hi_ref[0] == k, turned[:half], turned[half:])


def split_blocks(y_hi, streams):
    ins = [v for pair in streams for v in pair]
    width = sum(keep.shape[1] for keep, _ in streams)
    return pl.pallas_call(
        split_body,
        in_specs=[pl.BlockSpec(memory_space=pltpu.SMEM)] + [pl.BlockSpec(memory_space=pltpu.VMEM)] * 4,
        out_specs=[pl.BlockSpec(memory_space=pltpu.VMEM)] * 8,
        scratch_shapes=[pltpu.VMEM((width, BLK), jnp.float32)],
        out_shape=[jax.ShapeDtypeStruct((BLK // 2, width), jnp.bfloat16)] * 8,
        compiler_params=pltpu.CompilerParams(vmem_limit_bytes=VMEM),
        cost_estimate=pl.CostEstimate(flops=0, bytes_accessed=1024, transcendentals=0),
    )(y_hi, *ins)


def after(values, *before):
    return lax.optimization_barrier((*values, *before))[: len(values)]


def add16(a, b):
    return (a.astype(jnp.float32) + b.astype(jnp.float32)).astype(jnp.bfloat16)


def shards(acts, key_grads, key_weight):
    tokens, model = acts.shape
    norm = float((tokens * 128) ** -0.5)
    device = lax.axis_index(AXES)
    core = device % 2
    y_hi = device // 64
    row = lax.dynamic_index_in_dim(jnp.asarray(table()), device, 0, keepdims=False)

    pair = ("core", "core")
    half = key_weight.shape[0] // 2
    width = key_grads.shape[1]
    kt_own = key_grads.T
    *have, act_a, act_b = front(core[None].astype(jnp.int32), acts, key_weight)
    kt_got, got_a, got_b = move(kt_own, pair), move(act_a, pair), move(act_b, pair)
    for stage in range(2):
        got = [move(have[k], (AG[0][k][stage], AG[1][k][stage])) for k in range(2)]
        if stage == 1:
            got = after(got, sends[0], keeps[0])
        have = join(list(zip(have, got)))
        if stage == 0:
            where = jnp.concatenate([row[:64], core[None].astype(jnp.int32)])
            parts = partial_blocks(where, acts, got_a, got_b, kt_own, kt_got, norm, have)
            sends, keeps = [parts[0], parts[2]], [parts[1], parts[3]]
    got = [move(have[k], (AG[0][k][2], AG[1][k][2])) for k in range(2)]
    gathered = [have[0], got[0], have[1], got[1]]
    swapped = [move(g, pair) for g in gathered]

    last, held = [], ()
    done = have[0]
    input_grads = None
    for stage in range(3):
        for stream in range(2):
            got = move(sends[stream], (RS_A[0][stream][stage], RS_A[1][stream][stage]))
            got, keep = after((got, keeps[stream]), done, *(held if stream == 1 else ()))
            if stage == 2:
                last.append((keep, got))
                continue
            n = keep.shape[0] // 2
            done = sends[stream] = add16(keep[n:], got[n:])
            keeps[stream] = add16(keep[:n], got[:n])
            if (stage, stream) == PROJECT[0]:
                (sched,) = after((row[64:80],), done)
                input_grads = project(sched, key_grads, gathered, half)
                held = (input_grads,)
            if (stage, stream) == PROJECT[1]:
                (sched,) = after((row[80:96],), done)
                input_grads = project(sched, key_grads, swapped, half, input_grads)
                held = (input_grads,)

    pieces = split_blocks(y_hi[None].astype(jnp.int32), last)
    weight_grads = 0.0
    for j in range(4):
        dims = [dim for bit, dim in zip((2, 1), RS_B[0][0]) if j & bit]
        for k in range(2):
            weight_grads = weight_grads + deliver(pieces[2 * j + k], dims, k).astype(jnp.float32)
    return input_grads, weight_grads


def solution(mesh):
    spec = P(AXES, None)
    return jax.shard_map(
        shards, mesh=mesh, in_specs=(spec, spec, P("intra", None)), out_specs=(spec, spec), check_vma=False
    )
```

time: 489 us -> 160 us (0.33)
  waiting for transfers between devices: 267 us -> 62 us
  local copies, waits for them, and re-layouts: 84.9 us -> 8.79 us
  matrix products: 50.6 us -> 0 us
  Pallas kernels: 0 us -> 47.6 us
  other arithmetic: 44 us -> 6.1 us
  between operations: 14.1 us -> 0.86 us
  starting transfers between devices: 26.4 us -> 33.9 us
    all_to_all x4 -> x0, waiting for transfers between devices: 267 us -> none  [the longest x1 240 us: shards(): lax.all_to_all(quantized, 'intra', split_axis=0, concat_axis=0, tiled=True)]
    ppermute x0 -> x27, waiting for transfers between devices: none -> 62 us  [the longest x19 53.6 us: move(): return lax.ppermute(value, AXES, pairs)]
    dot_general x2 -> x0, matrix products: 50.6 us -> none  [the longest x1 29.6 us: shards(): lax.dot_general(key_grads, lax.all_gather(key_weight, 'intra', axis=0, ti...]
    pallas_call x0 -> x7, Pallas kernels: none -> 47.6 us  [the longest x2 18.9 us: project(): pl.pallas_call(functools.partial(project_body, half, rest, len(lasts)), i...]
    convert_element_type x6 -> x0, local copies, waits for them, and re-layouts: 44.7 us -> none  [the longest x1 40.6 us: from_codes(): quantized.reshape(groups, row_count, quantized.shape[1], 128)]
    ppermute x0 -> x27, starting transfers between devices: none -> 33.9 us  [the longest x8 17.1 us: deliver(): return lax.ppermute(value, AXES, pairs)]
    reshape x1 -> x0, local copies, waits for them, and re-layouts: 33.6 us -> none  [shards(): partial_value.reshape(partial_value.shape[0], -1, 128)]
    all_to_all x4 -> x0, starting transfers between devices: 26.4 us -> none  [the longest x1 8.37 us: shards(): lax.all_to_all(maxima.astype(jnp.bfloat16), 'intra', split_axis=0, concat...]
  transfers between devices with their start and end apart: 5 -> 27, of which waited for: 3 -> 8; matrix products, arithmetic and copies ran while one was open for 30% -> 4% of each run, Pallas kernels for 0% -> 25%
where the time goes in v3:
time: 160 us; the launch traced here: 159 us
  waiting for transfers between devices  62 us (39%)
  Pallas kernels  47.6 us (30%)
  starting transfers between devices  33.9 us (21%)
  local copies, waits for them, and re-layouts  8.79 us (5%)
  other arithmetic  6.1 us (4%)
    ppermute x19, waiting for transfers between devices, move(): return lax.ppermute(value, AXES, pairs)  53.6 us
    pallas_call x2, Pallas kernels, project(): pl.pallas_call(functools.partial(project_body, half, rest, len(lasts)), i...  18.9 us
    ppermute x8, starting transfers between devices, deliver(): return lax.ppermute(value, AXES, pairs)  17.1 us
    ppermute x19, starting transfers between devices, move(): return lax.ppermute(value, AXES, pairs)  16.8 us
    pallas_call x1, Pallas kernels, partial_blocks(): pl.pallas_call(body, in_specs=[pl.BlockSpec(memory_space=pltpu.SMEM)] + [...  14.8 us
    ppermute x8, waiting for transfers between devices, deliver(): return lax.ppermute(value, AXES, pairs)  8.44 us
    unnamed x23, local copies, waits for them, and re-layouts  7.5 us
    pallas_call x2, Pallas kernels, join(): pl.pallas_call(functools.partial(join_body, len(ins)), in_specs=[pl.Block...  6.66 us
  transfers between devices with their start and end apart: 27, of which 8 were waited for; matrix products, arithmetic and copies ran while one was open for 4% of the time, Pallas kernels for 25%

profile of v3, /device:TPU:1, one launch (start us, length us, event | category | flops | bytes accessed | tf_op | source)
XLA Modules:
  0.0 159.3 jit_solution(3520537748416652544)
XLA Ops:
  0.7 4.5 %shard_map.59 = (bf16[1,336,1024]{2,1,0:T(8,128)(2,1)}, bf16[1,176,1024]{2,1,0:T(8,128)(2,1)}, bf16[512,2048]{1,0:T(8,128)(2,1)}, bf16[512,2048]{1,0:T(8,128)(2,1)}) custom-call(s32[1]{0:T(128)} %bitcast.2.core_ref, bf16[512,8192]{1,0:T(8,128)(2,1)} %refs_0_.1, bf16[1024,1024]{1,0:T(8,128)(2,1)} %weight.1), custom_call_target="tpu_custom_call" | custom-call | bytes 1024 | tf_op jit(solution)/shard_map/pallas_call | solution.py:141
  5.1 1.5 collective-permute-start
  6.7 2.8 %collective-permute-start.3 = (bf16[1,336,1024]{2,1,0:T(8,128)(2,1)}, bf16[1,336,1024]{2,1,0:T(8,128)(2,1)S(1)}, u32[]{:S(2)}, u32[]{:S(2)}) collective-permute-start(bf16[1,336,1024]{2,1,0:T(8,128)(2,1)} %get-tuple-element.40.refs_0_), channel_id=1, source_target_pairs={{0,32},{1,97},{2,34},{3,99},{4,36},{5,101},{6,38},{7,103},{8,40},{... | collective-permute-start | bytes 2064392 | tf_op jit(solution)/shard_map/ppermute | solution.py:91
  9.6 3.8 %collective-permute-start.4 = (bf16[1,176,1024]{2,1,0:T(8,128)(2,1)}, bf16[1,176,1024]{2,1,0:T(8,128)(2,1)S(1)}, u32[]{:S(2)}, u32[]{:S(2)}) collective-permute-start(bf16[1,176,1024]{2,1,0:T(8,128)(2,1)} %get-tuple-element.41.refs_2_), channel_id=1, source_target_pairs={{0,24},{1,25},{2,26},{3,27},{4,28},{5,29},{6,30},{7,31},{8,16},{9,... | collective-permute-start | bytes 1081352 | tf_op jit(solution)/shard_map/ppermute | solution.py:91
  14.0 7.7 %collective-permute-done.4.refs_3_ = bf16[1,176,1024]{2,1,0:T(8,128)(2,1)S(1)} collective-permute-done((bf16[1,176,1024]{2,1,0:T(8,128)(2,1)}, bf16[1,176,1024]{2,1,0:T(8,128)(2,1)S(1)}, u32[]{:S(2)}, u32[]{:S(2)}) %collective-permute-start.4) | collective-permute-done | bytes 360480 | tf_op jit(solution)/shard_map/ppermute | solution.py:91
  23.3 2.7 %shard_map.60 = (bf16[2,336,1024]{2,1,0:T(8,128)(2,1)}, bf16[2,176,1024]{2,1,0:T(8,128)(2,1)}) custom-call(bf16[1,336,1024]{2,1,0:T(8,128)(2,1)} %get-tuple-element.40.refs_0_, bf16[1,336,1024]{2,1,0:T(8,128)(2,1)} %copy-done.8, bf16[1,176,1024]{2,1,0:T(8,128)(2,1)} %get-tuple-element.41.refs_2_, bf16[1,176,1024]{2,1,0:T(8,128)(2,1)} %copy-done.9), custom_call_target="tpu_custom_call" | custom-call | bytes 1024 | tf_op jit(solution)/shard_map/pallas_call | solution.py:337
  26.0 3.0 %collective-permute-start.7 = (bf16[2,336,1024]{2,1,0:T(8,128)(2,1)}, bf16[2,336,1024]{2,1,0:T(8,128)(2,1)S(1)}, u32[]{:S(2)}, u32[]{:S(2)}) collective-permute-start(bf16[2,336,1024]{2,1,0:T(8,128)(2,1)} %get-tuple-element.42.refs_5_.refs_0_), channel_id=1, source_target_pairs={{0,96},{1,25},{2,98},{3,27},{4,100},{5,29},{6,102},{7,31},{8,104},... | collective-permute-start | bytes 4128776 | tf_op jit(solution)/shard_map/ppermute | solution.py:91
  31.9 14.8 %shard_map.61 = (bf16[16,688,128]{2,1,0:T(8,128)(2,1)}, bf16[16,688,128]{2,1,0:T(8,128)(2,1)}, bf16[16,336,128]{2,1,0:T(8,128)(2,1)}, bf16[16,336,128]{2,1,0:T(8,128)(2,1)}) custom-call(s32[65]{0:T(128)} %pad_add_fusion.where_ref, bf16[512,8192]{1,0:T(8,128)(2,1)} %refs_0_.1, bf16[512,2048]{1,0:T(8,128)(2,1)} %collective-permute-done.refs_1_, ...), custom_call_target="tpu_custom_call" | custom-call | bytes 1024 | tf_op jit(solution)/shard_map/pallas_call | solution.py:233
  46.7 2.6 %collective-permute-start.6 = (bf16[16,688,128]{2,1,0:T(8,128)(2,1)}, bf16[16,688,128]{2,1,0:T(8,128)(2,1)S(1)}, u32[]{:S(2)}, u32[]{:S(2)}) collective-permute-start(bf16[16,688,128]{2,1,0:T(8,128)(2,1)} %get-tuple-element.46), channel_id=1, source_target_pairs={{0,2},{1,7},{2,0},{3,5},{4,6},{5,3},{6,4},{7,1},{8,10},{9,15},{10,... | collective-permute-start | bytes 8454152 | tf_op jit(solution)/shard_map/ppermute | solution.py:91
  51.3 4.0 %shard_map.62 = (bf16[4,336,1024]{2,1,0:T(8,128)(2,1)}, bf16[4,176,1024]{2,1,0:T(8,128)(2,1)}) custom-call(bf16[2,336,1024]{2,1,0:T(8,128)(2,1)} %get-tuple-element.42.refs_5_.refs_0_, bf16[2,336,1024]{2,1,0:T(8,128)(2,1)} %copy-done.5, bf16[2,176,1024]{2,1,0:T(8,128)(2,1)} %get-tuple-element.43.refs_6_.refs_2_, bf16[2,176,1024]{2,1,0:T(8,128)(2,1)} %copy-done.7), custom_call_target="tpu_custom_call" | custom-call | bytes 1024 | tf_op jit(solution)/shard_map/pallas_call | solution.py:337
  56.4 24.8 %collective-permute-done.6 = bf16[16,688,128]{2,1,0:T(8,128)(2,1)S(1)} collective-permute-done((bf16[16,688,128]{2,1,0:T(8,128)(2,1)}, bf16[16,688,128]{2,1,0:T(8,128)(2,1)S(1)}, u32[]{:S(2)}, u32[]{:S(2)}) %collective-permute-start.6) | collective-permute-done | bytes 2818080 | tf_op jit(solution)/shard_map/ppermute | solution.py:91
  82.8 5.1 %collective-permute-done.11.refs_1_ = bf16[4,336,1024]{2,1,0:T(8,128)(2,1)} collective-permute-done((bf16[4,336,1024]{2,1,0:T(8,128)(2,1)}, bf16[4,336,1024]{2,1,0:T(8,128)(2,1)}, u32[]{:S(2)}, u32[]{:S(2)}) %collective-permute-start.11) | collective-permute-done | bytes 2752544 | tf_op jit(solution)/shard_map/ppermute | solution.py:91
  89.2 2.1 %collective-permute-done.12.refs_3_ = bf16[4,176,1024]{2,1,0:T(8,128)(2,1)} collective-permute-done((bf16[4,176,1024]{2,1,0:T(8,128)(2,1)}, bf16[4,176,1024]{2,1,0:T(8,128)(2,1)}, u32[]{:S(2)}, u32[]{:S(2)}) %collective-permute-start.12) | collective-permute-done | bytes 1441824 | tf_op jit(solution)/shard_map/ppermute | solution.py:91
  91.6 12.2 %collective-permute-done.10 = bf16[8,688,128]{2,1,0:T(8,128)(2,1)S(1)} collective-permute-done((bf16[8,688,128]{2,1,0:T(8,128)(2,1)S(1)}, bf16[8,688,128]{2,1,0:T(8,128)(2,1)S(1)}, u32[]{:S(2)}, u32[]{:S(2)}) %collective-permute-start.10) | collective-permute-done | bytes 1409056 | tf_op jit(solution)/shard_map/ppermute | solution.py:91
  103.9 1.5 add_convert_fusion.2
  106.8 9.4 %shard_map.63.refs_4_ = bf16[512,8192]{1,0:T(8,128)(2,1)} custom-call(s32[16]{0:T(128)} %get-tuple-element.57.sched_ref, bf16[512,1024]{1,0:T(8,128)(2,1)} %kg_ref.3, bf16[4,336,1024]{2,1,0:T(8,128)(2,1)} %get-tuple-element.50.refs_0_, bf16[4,336,1024]{2,1,0:T(8,128)(2,1)} %collective-permute-done.11.refs_1_, ...), custom_call_target="tpu_custom_call" | custom-call | flops 4294967296 | bytes 31457280 | tf_op jit(solution)/shard_map/pallas_call | solution.py:294
  116.3 2.0 %add_convert_fusion.6 = (bf16[4,336,128]{2,1,0:T(8,128)(2,1)}, bf16[4,336,128]{2,1,0:T(8,128)(2,1)S(1)}) fusion(bf16[8,336,128]{2,1,0:T(8,128)(2,1)} %collective-permute-done.9, bf16[8,336,128]{2,1,0:T(8,128)(2,1)S(1)} %get-tuple-element.59), kind=kLoop, calls=%fused_computation.6 | loop fusion | flops 1376256 | bytes 2064384 | tf_op jit(solution)/shard_map/convert_element_type | solution.py:384
  118.4 1.5 copy-done.3
  119.9 9.4 %shard_map.64 = bf16[512,8192]{1,0:T(8,128)(2,1)} custom-call(s32[16]{0:T(128)} %get-tuple-element.61.sched_ref, bf16[512,1024]{1,0:T(8,128)(2,1)} %kg_ref.3, bf16[4,336,1024]{2,1,0:T(8,128)(2,1)} %copy-done.3, bf16[4,336,1024]{2,1,0:T(8,128)(2,1)} %collective-permute-done.14.refs_1_, ...), custom_call_target="tpu_custom_call", output_to_operand_aliasing={{}: (6, {})} | custom-call | flops 4294967296 | bytes 31457280 | tf_op jit(solution)/shard_map/pallas_call | solution.py:294
  130.1 2.7 %shard_map.65 = (bf16[64,1024]{1,0:T(8,128)(2,1)}, bf16[64,1024]{1,0:T(8,128)(2,1)}, bf16[64,1024]{1,0:T(8,128)(2,1)}, bf16[64,1024]{1,0:T(8,128)(2,1)}, bf16[64...) custom-call(s32[1]{0:T(128)} %bitcast.5.y_hi_ref, ...), custom_call_target="tpu_custom_call" | custom-call | bytes 1024 | tf_op jit(solution)/shard_map/pallas_call | solution.py:368
  132.8 5.2 %collective-permute-start.19 = (bf16[64,1024]{1,0:T(8,128)(2,1)}, bf16[64,1024]{1,0:T(8,128)(2,1)S(1)}, u32[]{:S(2)}, u32[]{:S(2)}) collective-permute-start(bf16[64,1024]{1,0:T(8,128)(2,1)} %get-tuple-element.66), channel_id=1, source_target_pairs={{0,0},{1,96},{2,2},{3,98},{4,4},{5,100},{6,6},{7,102},{8,8},{9,104... | collective-permute-start | bytes 393224 | tf_op jit(solution)/shard_map/ppermute | solution.py:103
  139.5 5.9 %collective-permute-start.23 = (bf16[64,1024]{1,0:T(8,128)(2,1)}, bf16[64,1024]{1,0:T(8,128)(2,1)S(1)}, u32[]{:S(2)}, u32[]{:S(2)}) collective-permute-start(bf16[64,1024]{1,0:T(8,128)(2,1)} %get-tuple-element.70), channel_id=1, source_target_pairs={{0,24},{1,120},{2,26},{3,122},{4,28},{5,124},{6,30},{7,126},{8,16}... | collective-permute-start | bytes 393224 | tf_op jit(solution)/shard_map/ppermute | solution.py:103
  145.4 3.3 %collective-permute-start.25 = (bf16[64,1024]{1,0:T(8,128)(2,1)}, bf16[64,1024]{1,0:T(8,128)(2,1)S(1)}, u32[]{:S(2)}, u32[]{:S(2)}) collective-permute-start(bf16[64,1024]{1,0:T(8,128)(2,1)} %get-tuple-element.72), channel_id=1, source_target_pairs={{0,56},{1,88},{2,58},{3,90},{4,60},{5,92},{6,62},{7,94},{8,48},{9,... | collective-permute-start | bytes 393224 | tf_op jit(solution)/shard_map/ppermute | solution.py:103
  150.0 8.4 %collective-permute-done.24 = bf16[64,1024]{1,0:T(8,128)(2,1)S(1)} collective-permute-done((bf16[64,1024]{1,0:T(8,128)(2,1)}, bf16[64,1024]{1,0:T(8,128)(2,1)S(1)}, u32[]{:S(2)}, u32[]{:S(2)}) %collective-permute-start.24) | collective-permute-done | bytes 131104 | tf_op jit(solution)/shard_map/ppermute | solution.py:103
  (69 shorter events, 17.4 us)
Async XLA Ops:
  5.1 25.6 %collective-permute-start = (bf16[512,2048]{1,0:T(8,128)(2,1)}, bf16[512,2048]{1,0:T(8,128)(2,1)}, u32[]{:S(2)}, u32[]{:S(2)}) collective-permute-start(bf16[512,2048]{1,0:T(8,128)(2,1)} %get-tuple-element.38), channel_id=1, source_target_pairs={{0,1},{1,0},{2,3},{3,2},{4,5},{5,4},{6,7},{7,6},{8,9},{9,8},{10,11... | collective-permute-start | bytes 6291464 | tf_op jit(solution)/shard_map/ppermute | solution.py:91
  6.7 24.1 %collective-permute-start.1 = (bf16[512,2048]{1,0:T(8,128)(2,1)}, bf16[512,2048]{1,0:T(8,128)(2,1)}, u32[]{:S(2)}, u32[]{:S(2)}) collective-permute-start(bf16[512,2048]{1,0:T(8,128)(2,1)} %get-tuple-element.39), channel_id=1, source_target_pairs={{0,1},{1,0},{2,3},{3,2},{4,5},{5,4},{6,7},{7,6},{8,9},{9,8},{10,11... | collective-permute-start | bytes 6291464 | tf_op jit(solution)/shard_map/ppermute | solution.py:91
  6.7 14.9 %collective-permute-start.3 = (bf16[1,336,1024]{2,1,0:T(8,128)(2,1)}, bf16[1,336,1024]{2,1,0:T(8,128)(2,1)S(1)}, u32[]{:S(2)}, u32[]{:S(2)}) collective-permute-start(bf16[1,336,1024]{2,1,0:T(8,128)(2,1)} %get-tuple-element.40.refs_0_), channel_id=1, source_target_pairs={{0,32},{1,97},{2,34},{3,99},{4,36},{5,101},{6,38},{7,103},{8,40},{... | collective-permute-start | bytes 2064392 | tf_op jit(solution)/shard_map/ppermute | solution.py:91
  9.6 12.1 %collective-permute-start.4 = (bf16[1,176,1024]{2,1,0:T(8,128)(2,1)}, bf16[1,176,1024]{2,1,0:T(8,128)(2,1)S(1)}, u32[]{:S(2)}, u32[]{:S(2)}) collective-permute-start(bf16[1,176,1024]{2,1,0:T(8,128)(2,1)} %get-tuple-element.41.refs_2_), channel_id=1, source_target_pairs={{0,24},{1,25},{2,26},{3,27},{4,28},{5,29},{6,30},{7,31},{8,16},{9,... | collective-permute-start | bytes 1081352 | tf_op jit(solution)/shard_map/ppermute | solution.py:91
  13.9 16.9 %collective-permute-start.2 = (bf16[1024,512]{1,0:T(8,128)(2,1)S(1)}, bf16[1024,512]{1,0:T(8,128)(2,1)S(1)}, u32[]{:S(2)}, u32[]{:S(2)}) collective-permute-start(bf16[1024,512]{1,0:T(8,128)(2,1)S(1)} %bitcast.9), channel_id=1, source_target_pairs={{0,1},{1,0},{2,3},{3,2},{4,5},{5,4},{6,7},{7,6},{8,9},{9,8},{10,11... | collective-permute-start | bytes 3145736 | tf_op jit(solution)/shard_map/ppermute | solution.py:91
  26.0 23.3 %collective-permute-start.7 = (bf16[2,336,1024]{2,1,0:T(8,128)(2,1)}, bf16[2,336,1024]{2,1,0:T(8,128)(2,1)S(1)}, u32[]{:S(2)}, u32[]{:S(2)}) collective-permute-start(bf16[2,336,1024]{2,1,0:T(8,128)(2,1)} %get-tuple-element.42.refs_5_.refs_0_), channel_id=1, source_target_pairs={{0,96},{1,25},{2,98},{3,27},{4,100},{5,29},{6,102},{7,31},{8,104},... | collective-permute-start | bytes 4128776 | tf_op jit(solution)/shard_map/ppermute | solution.py:91
  29.7 19.5 %collective-permute-start.8 = (bf16[2,176,1024]{2,1,0:T(8,128)(2,1)}, bf16[2,176,1024]{2,1,0:T(8,128)(2,1)S(1)}, u32[]{:S(2)}, u32[]{:S(2)}) collective-permute-start(bf16[2,176,1024]{2,1,0:T(8,128)(2,1)} %get-tuple-element.43.refs_6_.refs_2_), channel_id=1, source_target_pairs={{0,32},{1,33},{2,34},{3,35},{4,36},{5,37},{6,38},{7,39},{8,40},{9,... | collective-permute-start | bytes 2162696 | tf_op jit(solution)/shard_map/ppermute | solution.py:91
  46.7 34.5 %collective-permute-start.6 = (bf16[16,688,128]{2,1,0:T(8,128)(2,1)}, bf16[16,688,128]{2,1,0:T(8,128)(2,1)S(1)}, u32[]{:S(2)}, u32[]{:S(2)}) collective-permute-start(bf16[16,688,128]{2,1,0:T(8,128)(2,1)} %get-tuple-element.46), channel_id=1, source_target_pairs={{0,2},{1,7},{2,0},{3,5},{4,6},{5,3},{6,4},{7,1},{8,10},{9,15},{10,... | collective-permute-start | bytes 8454152 | tf_op jit(solution)/shard_map/ppermute | solution.py:91
  55.3 32.6 %collective-permute-start.11 = (bf16[4,336,1024]{2,1,0:T(8,128)(2,1)}, bf16[4,336,1024]{2,1,0:T(8,128)(2,1)}, u32[]{:S(2)}, u32[]{:S(2)}) collective-permute-start(bf16[4,336,1024]{2,1,0:T(8,128)(2,1)} %get-tuple-element.50.refs_0_), channel_id=1, source_target_pairs={{0,24},{1,33},{2,26},{3,35},{4,28},{5,37},{6,30},{7,39},{8,16},{9,... | collective-permute-start | bytes 8257544 | tf_op jit(solution)/shard_map/ppermute | solution.py:91
  56.4 32.4 %collective-permute-start.5 = (bf16[16,336,128]{2,1,0:T(8,128)(2,1)}, bf16[16,336,128]{2,1,0:T(8,128)(2,1)S(1)}, u32[]{:S(2)}, u32[]{:S(2)}) collective-permute-start(bf16[16,336,128]{2,1,0:T(8,128)(2,1)} %get-tuple-element.44), channel_id=1, source_target_pairs={{0,8},{1,9},{2,10},{3,11},{4,12},{5,13},{6,14},{7,15},{8,0},{9,1},... | collective-permute-start | bytes 4128776 | tf_op jit(solution)/shard_map/ppermute | solution.py:91
  56.4 34.9 %collective-permute-start.12 = (bf16[4,176,1024]{2,1,0:T(8,128)(2,1)}, bf16[4,176,1024]{2,1,0:T(8,128)(2,1)}, u32[]{:S(2)}, u32[]{:S(2)}) collective-permute-start(bf16[4,176,1024]{2,1,0:T(8,128)(2,1)} %get-tuple-element.58.refs_2_), channel_id=1, source_target_pairs={{0,96},{1,97},{2,98},{3,99},{4,100},{5,101},{6,102},{7,103},{8,104... | collective-permute-start | bytes 4325384 | tf_op jit(solution)/shard_map/ppermute | solution.py:91
  81.9 21.9 %collective-permute-start.10 = (bf16[8,688,128]{2,1,0:T(8,128)(2,1)S(1)}, bf16[8,688,128]{2,1,0:T(8,128)(2,1)S(1)}, u32[]{:S(2)}, u32[]{:S(2)}) collective-permute-start(bf16[8,688,128]{2,1,0:T(8,128)(2,1)S(1)} %get-tuple-element.75), channel_id=1, source_target_pairs={{0,6},{1,9},{2,4},{3,11},{4,2},{5,13},{6,0},{7,15},{8,14},{9,1},{1... | collective-permute-start | bytes 4227080 | tf_op jit(solution)/shard_map/ppermute | solution.py:91
  82.0 36.3 %collective-permute-start.13 = (bf16[4,336,1024]{2,1,0:T(8,128)(2,1)}, bf16[4,336,1024]{2,1,0:T(8,128)(2,1)S(1)}, u32[]{:S(2)}, u32[]{:S(2)}) collective-permute-start(bf16[4,336,1024]{2,1,0:T(8,128)(2,1)} %get-tuple-element.50.refs_0_), channel_id=1, source_target_pairs={{0,1},{1,0},{2,3},{3,2},{4,5},{5,4},{6,7},{7,6},{8,9},{9,8},{10,11... | collective-permute-start | bytes 8257544 | tf_op jit(solution)/shard_map/ppermute | solution.py:91
  87.9 30.5 %collective-permute-start.14 = (bf16[4,336,1024]{2,1,0:T(8,128)(2,1)}, bf16[4,336,1024]{2,1,0:T(8,128)(2,1)}, u32[]{:S(2)}, u32[]{:S(2)}) collective-permute-start(bf16[4,336,1024]{2,1,0:T(8,128)(2,1)} %collective-permute-done.11.refs_1_), channel_id=1, source_target_pairs={{0,1},{1,0},{2,3},{3,2},{4,5},{5,4},{6,7},{7,6},{8,9},{9,8},{10,11... | collective-permute-start | bytes 8257544 | tf_op jit(solution)/shard_map/ppermute | solution.py:91
  89.1 17.1 %collective-permute-start.9 = (bf16[8,336,128]{2,1,0:T(8,128)(2,1)S(1)}, bf16[8,336,128]{2,1,0:T(8,128)(2,1)}, u32[]{:S(2)}, u32[]{:S(2)}) collective-permute-start(bf16[8,336,128]{2,1,0:T(8,128)(2,1)S(1)} %get-tuple-element.79), channel_id=1, source_target_pairs={{0,2},{1,3},{2,0},{3,1},{4,6},{5,7},{6,4},{7,5},{8,10},{9,11},{10,... | collective-permute-start | bytes 2064392 | tf_op jit(solution)/shard_map/ppermute | solution.py:91
  91.3 27.1 %collective-permute-start.15 = (bf16[4,176,1024]{2,1,0:T(8,128)(2,1)}, bf16[4,176,1024]{2,1,0:T(8,128)(2,1)}, u32[]{:S(2)}, u32[]{:S(2)}) collective-permute-start(bf16[4,176,1024]{2,1,0:T(8,128)(2,1)} %get-tuple-element.58.refs_2_), channel_id=1, source_target_pairs={{0,1},{1,0},{2,3},{3,2},{4,5},{5,4},{6,7},{7,6},{8,9},{9,8},{10,11... | collective-permute-start | bytes 4325384 | tf_op jit(solution)/shard_map/ppermute | solution.py:91
  103.9 14.5 %collective-permute-start.16 = (bf16[4,176,1024]{2,1,0:T(8,128)(2,1)}, bf16[4,176,1024]{2,1,0:T(8,128)(2,1)}, u32[]{:S(2)}, u32[]{:S(2)}) collective-permute-start(bf16[4,176,1024]{2,1,0:T(8,128)(2,1)} %collective-permute-done.12.refs_3_), channel_id=1, source_target_pairs={{0,1},{1,0},{2,3},{3,2},{4,5},{5,4},{6,7},{7,6},{8,9},{9,8},{10,11... | collective-permute-start | bytes 4325384 | tf_op jit(solution)/shard_map/ppermute | solution.py:91
  106.2 12.0 %collective-permute-start.17 = (bf16[4,688,128]{2,1,0:T(8,128)(2,1)}, bf16[4,688,128]{2,1,0:T(8,128)(2,1)}, u32[]{:S(2)}, u32[]{:S(2)}) collective-permute-start(bf16[4,688,128]{2,1,0:T(8,128)(2,1)} %get-tuple-element.77), channel_id=1, source_target_pairs={{0,8},{1,3},{2,10},{3,1},{4,12},{5,7},{6,14},{7,5},{8,0},{9,11},{1... | collective-permute-start | bytes 2113544 | tf_op jit(solution)/shard_map/ppermute | solution.py:91
  118.3 11.1 %collective-permute-start.18 = (bf16[4,336,128]{2,1,0:T(8,128)(2,1)S(1)}, bf16[4,336,128]{2,1,0:T(8,128)(2,1)S(1)}, u32[]{:S(2)}, u32[]{:S(2)}) collective-permute-start(bf16[4,336,128]{2,1,0:T(8,128)(2,1)S(1)} %get-tuple-element.81), channel_id=1, source_target_pairs={{0,6},{1,7},{2,4},{3,5},{4,2},{5,3},{6,0},{7,1},{8,14},{9,15},{10,... | collective-permute-start | bytes 1032200 | tf_op jit(solution)/shard_map/ppermute | solution.py:91
  132.8 12.6 %collective-permute-start.19 = (bf16[64,1024]{1,0:T(8,128)(2,1)}, bf16[64,1024]{1,0:T(8,128)(2,1)S(1)}, u32[]{:S(2)}, u32[]{:S(2)}) collective-permute-start(bf16[64,1024]{1,0:T(8,128)(2,1)} %get-tuple-element.66), channel_id=1, source_target_pairs={{0,0},{1,96},{2,2},{3,98},{4,4},{5,100},{6,6},{7,102},{8,8},{9,104... | collective-permute-start | bytes 393224 | tf_op jit(solution)/shard_map/ppermute | solution.py:103
  138.2 10.6 %collective-permute-start.21 = (bf16[64,1024]{1,0:T(8,128)(2,1)}, bf16[64,1024]{1,0:T(8,128)(2,1)S(1)}, u32[]{:S(2)}, u32[]{:S(2)}) collective-permute-start(bf16[64,1024]{1,0:T(8,128)(2,1)} %get-tuple-element.68), channel_id=1, source_target_pairs={{0,32},{1,64},{2,34},{3,66},{4,36},{5,68},{6,38},{7,70},{8,40},{9,... | collective-permute-start | bytes 393224 | tf_op jit(solution)/shard_map/ppermute | solution.py:103
  139.4 10.6 %collective-permute-start.22 = (bf16[64,1024]{1,0:T(8,128)(2,1)}, bf16[64,1024]{1,0:T(8,128)(2,1)S(1)}, u32[]{:S(2)}, u32[]{:S(2)}) collective-permute-start(bf16[64,1024]{1,0:T(8,128)(2,1)} %get-tuple-element.69), channel_id=1, source_target_pairs={{0,33},{1,65},{2,35},{3,67},{4,37},{5,69},{6,39},{7,71},{8,41},{9,... | collective-permute-start | bytes 393224 | tf_op jit(solution)/shard_map/ppermute | solution.py:103
  145.4 13.0 %collective-permute-start.24 = (bf16[64,1024]{1,0:T(8,128)(2,1)}, bf16[64,1024]{1,0:T(8,128)(2,1)S(1)}, u32[]{:S(2)}, u32[]{:S(2)}) collective-permute-start(bf16[64,1024]{1,0:T(8,128)(2,1)} %get-tuple-element.71), channel_id=1, source_target_pairs={{0,25},{1,121},{2,27},{3,123},{4,29},{5,125},{6,31},{7,127},{8,17}... | collective-permute-start | bytes 393224 | tf_op jit(solution)/shard_map/ppermute | solution.py:103
  145.4 13.0 %collective-permute-start.25 = (bf16[64,1024]{1,0:T(8,128)(2,1)}, bf16[64,1024]{1,0:T(8,128)(2,1)S(1)}, u32[]{:S(2)}, u32[]{:S(2)}) collective-permute-start(bf16[64,1024]{1,0:T(8,128)(2,1)} %get-tuple-element.72), channel_id=1, source_target_pairs={{0,56},{1,88},{2,58},{3,90},{4,60},{5,92},{6,62},{7,94},{8,48},{9,... | collective-permute-start | bytes 393224 | tf_op jit(solution)/shard_map/ppermute | solution.py:103
  (14 other events, 126.5 us)

commit v4 on v3

--- a/solution.py
+++ b/solution.py
@@ -91,15 +91,14 @@
     return lax.ppermute(value, AXES, pairs)
 
 
-def deliver(value, dims, k):
+def deliver(value, dims):
     pairs = []
     for device in range(128):
         at = coords(device)
-        y_hi = at[0] >> 1
-        to = at if y_hi == at[4] else flip(at, "yB")
+        to = at if (at[0] >> 1) == at[4] else flip(flip(at, "yB"), "core")
         for dim in dims:
             to = flip(to, dim)
-        pairs.append((device, ident((*to[:4], y_hi ^ k))))
+        pairs.append((device, ident(to)))
     return lax.ppermute(value, AXES, pairs)
 
 
@@ -347,8 +346,8 @@
     )
 
 
-def split_body(y_hi_ref, *refs):
-    ins, outs, whole = refs[:4], refs[4:12], refs[12]
+def split_body(*refs):
+    ins, outs, whole = refs[:4], refs[4:8], refs[8]
     for j in range(4):
         low = 0
         for stream in range(2):
@@ -356,24 +355,21 @@
             width = keep.shape[1]
             whole[low : low + width, :] = keep[j].astype(jnp.float32) + got[j].astype(jnp.float32)
             low += width
-        turned = whole[...].T.astype(jnp.bfloat16)
-        half = turned.shape[0] // 2
-        for k in range(2):
-            outs[2 * j + k][...] = jnp.where(y_hi_ref[0] == k, turned[:half], turned[half:])
-
-
-def split_blocks(y_hi, streams):
+        outs[j][...] = whole[...].T.astype(jnp.bfloat16)
+
+
+def split_blocks(streams):
     ins = [v for pair in streams for v in pair]
     width = sum(keep.shape[1] for keep, _ in streams)
     return pl.pallas_call(
         split_body,
-        in_specs=[pl.BlockSpec(memory_space=pltpu.SMEM)] + [pl.BlockSpec(memory_space=pltpu.VMEM)] * 4,
-        out_specs=[pl.BlockSpec(memory_space=pltpu.VMEM)] * 8,
+        in_specs=[pl.BlockSpec(memory_space=pltpu.VMEM)] * 4,
+        out_specs=[pl.BlockSpec(memory_space=pltpu.VMEM)] * 4,
         scratch_shapes=[pltpu.VMEM((width, BLK), jnp.float32)],
-        out_shape=[jax.ShapeDtypeStruct((BLK // 2, width), jnp.bfloat16)] * 8,
+        out_shape=[jax.ShapeDtypeStruct((BLK, width), jnp.bfloat16)] * 4,
         compiler_params=pltpu.CompilerParams(vmem_limit_bytes=VMEM),
         cost_estimate=pl.CostEstimate(flops=0, bytes_accessed=1024, transcendentals=0),
-    )(y_hi, *ins)
+    )(*ins)
 
 
 def after(values, *before):
@@ -389,7 +385,6 @@
     norm = float((tokens * 128) ** -0.5)
     device = lax.axis_index(AXES)
     core = device % 2
-    y_hi = device // 64
     row = lax.dynamic_index_in_dim(jnp.asarray(table()), device, 0, keepdims=False)
 
     pair = ("core", "core")
@@ -433,12 +428,14 @@
                 input_grads = project(sched, key_grads, swapped, half, input_grads)
                 held = (input_grads,)
 
-    pieces = split_blocks(y_hi[None].astype(jnp.int32), last)
-    weight_grads = 0.0
+    pieces = split_blocks(last)
+    total = 0.0
     for j in range(4):
         dims = [dim for bit, dim in zip((2, 1), RS_B[0][0]) if j & bit]
-        for k in range(2):
-            weight_grads = weight_grads + deliver(pieces[2 * j + k], dims, k).astype(jnp.float32)
+        total = total + deliver(pieces[j], dims).astype(jnp.float32)
+    rows = total.shape[0] // 2
+    for_other = lax.dynamic_slice_in_dim(total, (1 - core) * rows, rows, axis=0)
+    weight_grads = lax.dynamic_slice_in_dim(total, core * rows, rows, axis=0) + move(for_other, pair)
     return input_grads, weight_grads
 
 

time: 160 us -> 158 us (0.988)
  starting transfers between devices: 33.9 us -> 28.7 us
  waiting for transfers between devices: 62 us -> 65.3 us
  local copies, waits for them, and re-layouts: 8.79 us -> 10.4 us
    ppermute x8 -> x4, starting transfers between devices: 17.1 us -> 11.8 us  [deliver(): return lax.ppermute(value, AXES, pairs)]
    ppermute x8 -> x4, waiting for transfers between devices: 8.44 us -> 10.3 us  [deliver(): return lax.ppermute(value, AXES, pairs)]
    unnamed x23 -> x31, local copies, waits for them, and re-layouts: 7.5 us -> 9.04 us
    ppermute x19 -> x20, waiting for transfers between devices: 53.6 us -> 55 us  [move(): return lax.ppermute(value, AXES, pairs)]
    ppermute x19 -> x20, starting transfers between devices: 16.8 us -> 16.9 us  [move(): return lax.ppermute(value, AXES, pairs)]
  transfers between devices with their start and end apart: 27 -> 24, of which waited for: 8 -> 11; matrix products, arithmetic and copies ran while one was open for 4% -> 4% of each run, Pallas kernels for 25% -> 26%
where the time goes in v4:
time: 158 us
  waiting for transfers between devices  65.3 us (41%)
  Pallas kernels  47.5 us (30%)
  starting transfers between devices  28.7 us (18%)
  local copies, waits for them, and re-layouts  10.4 us (7%)
  other arithmetic  5.16 us (3%)
    ppermute x20, waiting for transfers between devices, move(): return lax.ppermute(value, AXES, pairs)  55 us
    pallas_call x2, Pallas kernels, project(): pl.pallas_call(functools.partial(project_body, half, rest, len(lasts)), i...  18.9 us
    ppermute x20, starting transfers between devices, move(): return lax.ppermute(value, AXES, pairs)  16.9 us
    pallas_call x1, Pallas kernels, partial_blocks(): pl.pallas_call(body, in_specs=[pl.BlockSpec(memory_space=pltpu.SMEM)] + [...  14.8 us
    ppermute x4, starting transfers between devices, deliver(): return lax.ppermute(value, AXES, pairs)  11.8 us
    ppermute x4, waiting for transfers between devices, deliver(): return lax.ppermute(value, AXES, pairs)  10.3 us
    unnamed x31, local copies, waits for them, and re-layouts  9.04 us
    pallas_call x2, Pallas kernels, join(): pl.pallas_call(functools.partial(join_body, len(ins)), in_specs=[pl.Block...  6.65 us
  transfers between devices with their start and end apart: 24, of which 11 were waited for; matrix products, arithmetic and copies ran while one was open for 4% of the time, Pallas kernels for 26%

profile of v4, /device:TPU:1, one launch (start us, length us, event | category | flops | bytes accessed | tf_op | source)
XLA Modules:
  0.0 157.9 jit_solution(7046121410081179791)
XLA Ops:
  0.7 4.5 %shard_map.59 = (bf16[1,336,1024]{2,1,0:T(8,128)(2,1)}, bf16[1,176,1024]{2,1,0:T(8,128)(2,1)}, bf16[512,2048]{1,0:T(8,128)(2,1)}, bf16[512,2048]{1,0:T(8,128)(2,1)}) custom-call(s32[1]{0:T(128)} %bitcast.2.core_ref, bf16[512,8192]{1,0:T(8,128)(2,1)} %refs_0_.1, bf16[1024,1024]{1,0:T(8,128)(2,1)} %weight.1), custom_call_target="tpu_custom_call" | custom-call | bytes 1024 | tf_op jit(solution)/shard_map/pallas_call | solution.py:140
  6.7 2.8 %collective-permute-start.3 = (bf16[1,336,1024]{2,1,0:T(8,128)(2,1)}, bf16[1,336,1024]{2,1,0:T(8,128)(2,1)S(1)}, u32[]{:S(2)}, u32[]{:S(2)}) collective-permute-start(bf16[1,336,1024]{2,1,0:T(8,128)(2,1)} %get-tuple-element.36.refs_0_), channel_id=1, source_target_pairs={{0,32},{1,97},{2,34},{3,99},{4,36},{5,101},{6,38},{7,103},{8,40},{... | collective-permute-start | bytes 2064392 | tf_op jit(solution)/shard_map/ppermute | solution.py:91
  9.6 3.8 %collective-permute-start.4 = (bf16[1,176,1024]{2,1,0:T(8,128)(2,1)}, bf16[1,176,1024]{2,1,0:T(8,128)(2,1)S(1)}, u32[]{:S(2)}, u32[]{:S(2)}) collective-permute-start(bf16[1,176,1024]{2,1,0:T(8,128)(2,1)} %get-tuple-element.37.refs_2_), channel_id=1, source_target_pairs={{0,24},{1,25},{2,26},{3,27},{4,28},{5,29},{6,30},{7,31},{8,16},{9,... | collective-permute-start | bytes 1081352 | tf_op jit(solution)/shard_map/ppermute | solution.py:91
  14.0 7.7 %collective-permute-done.4.refs_3_ = bf16[1,176,1024]{2,1,0:T(8,128)(2,1)S(1)} collective-permute-done((bf16[1,176,1024]{2,1,0:T(8,128)(2,1)}, bf16[1,176,1024]{2,1,0:T(8,128)(2,1)S(1)}, u32[]{:S(2)}, u32[]{:S(2)}) %collective-permute-start.4) | collective-permute-done | bytes 360480 | tf_op jit(solution)/shard_map/ppermute | solution.py:91
  23.3 2.7 %shard_map.60 = (bf16[2,336,1024]{2,1,0:T(8,128)(2,1)}, bf16[2,176,1024]{2,1,0:T(8,128)(2,1)}) custom-call(bf16[1,336,1024]{2,1,0:T(8,128)(2,1)} %get-tuple-element.36.refs_0_, bf16[1,336,1024]{2,1,0:T(8,128)(2,1)} %copy-done.10, bf16[1,176,1024]{2,1,0:T(8,128)(2,1)} %get-tuple-element.37.refs_2_, bf16[1,176,1024]{2,1,0:T(8,128)(2,1)} %copy-done.11), custom_call_target="tpu_custom_call" | custom-call | bytes 1024 | tf_op jit(solution)/shard_map/pallas_call | solution.py:336
  26.0 3.0 %collective-permute-start.7 = (bf16[2,336,1024]{2,1,0:T(8,128)(2,1)}, bf16[2,336,1024]{2,1,0:T(8,128)(2,1)S(1)}, u32[]{:S(2)}, u32[]{:S(2)}) collective-permute-start(bf16[2,336,1024]{2,1,0:T(8,128)(2,1)} %get-tuple-element.38.refs_5_.refs_0_), channel_id=1, source_target_pairs={{0,96},{1,25},{2,98},{3,27},{4,100},{5,29},{6,102},{7,31},{8,104},... | collective-permute-start | bytes 4128776 | tf_op jit(solution)/shard_map/ppermute | solution.py:91
  31.8 14.8 %shard_map.61 = (bf16[16,688,128]{2,1,0:T(8,128)(2,1)}, bf16[16,688,128]{2,1,0:T(8,128)(2,1)}, bf16[16,336,128]{2,1,0:T(8,128)(2,1)}, bf16[16,336,128]{2,1,0:T(8,128)(2,1)}) custom-call(s32[65]{0:T(128)} %pad_add_fusion.where_ref, bf16[512,8192]{1,0:T(8,128)(2,1)} %refs_0_.1, bf16[512,2048]{1,0:T(8,128)(2,1)} %collective-permute-done.refs_1_, ...), custom_call_target="tpu_custom_call" | custom-call | bytes 1024 | tf_op jit(solution)/shard_map/pallas_call | solution.py:232
  46.7 2.6 %collective-permute-start.6 = (bf16[16,688,128]{2,1,0:T(8,128)(2,1)}, bf16[16,688,128]{2,1,0:T(8,128)(2,1)S(1)}, u32[]{:S(2)}, u32[]{:S(2)}) collective-permute-start(bf16[16,688,128]{2,1,0:T(8,128)(2,1)} %get-tuple-element.42), channel_id=1, source_target_pairs={{0,2},{1,7},{2,0},{3,5},{4,6},{5,3},{6,4},{7,1},{8,10},{9,15},{10,... | collective-permute-start | bytes 8454152 | tf_op jit(solution)/shard_map/ppermute | solution.py:91
  51.2 4.0 %shard_map.62 = (bf16[4,336,1024]{2,1,0:T(8,128)(2,1)}, bf16[4,176,1024]{2,1,0:T(8,128)(2,1)}) custom-call(bf16[2,336,1024]{2,1,0:T(8,128)(2,1)} %get-tuple-element.38.refs_5_.refs_0_, bf16[2,336,1024]{2,1,0:T(8,128)(2,1)} %copy-done.7, bf16[2,176,1024]{2,1,0:T(8,128)(2,1)} %get-tuple-element.39.refs_6_.refs_2_, bf16[2,176,1024]{2,1,0:T(8,128)(2,1)} %copy-done.9), custom_call_target="tpu_custom_call" | custom-call | bytes 1024 | tf_op jit(solution)/shard_map/pallas_call | solution.py:336
  56.4 24.8 %collective-permute-done.6 = bf16[16,688,128]{2,1,0:T(8,128)(2,1)S(1)} collective-permute-done((bf16[16,688,128]{2,1,0:T(8,128)(2,1)}, bf16[16,688,128]{2,1,0:T(8,128)(2,1)S(1)}, u32[]{:S(2)}, u32[]{:S(2)}) %collective-permute-start.6) | collective-permute-done | bytes 2818080 | tf_op jit(solution)/shard_map/ppermute | solution.py:91
  82.8 5.0 %collective-permute-done.11.refs_1_ = bf16[4,336,1024]{2,1,0:T(8,128)(2,1)} collective-permute-done((bf16[4,336,1024]{2,1,0:T(8,128)(2,1)}, bf16[4,336,1024]{2,1,0:T(8,128)(2,1)}, u32[]{:S(2)}, u32[]{:S(2)}) %collective-permute-start.11) | collective-permute-done | bytes 2752544 | tf_op jit(solution)/shard_map/ppermute | solution.py:91
  89.2 2.1 %collective-permute-done.12.refs_3_ = bf16[4,176,1024]{2,1,0:T(8,128)(2,1)} collective-permute-done((bf16[4,176,1024]{2,1,0:T(8,128)(2,1)}, bf16[4,176,1024]{2,1,0:T(8,128)(2,1)}, u32[]{:S(2)}, u32[]{:S(2)}) %collective-permute-start.12) | collective-permute-done | bytes 1441824 | tf_op jit(solution)/shard_map/ppermute | solution.py:91
  91.6 12.1 %collective-permute-done.10 = bf16[8,688,128]{2,1,0:T(8,128)(2,1)S(1)} collective-permute-done((bf16[8,688,128]{2,1,0:T(8,128)(2,1)S(1)}, bf16[8,688,128]{2,1,0:T(8,128)(2,1)S(1)}, u32[]{:S(2)}, u32[]{:S(2)}) %collective-permute-start.10) | collective-permute-done | bytes 1409056 | tf_op jit(solution)/shard_map/ppermute | solution.py:91
  103.7 1.5 add_convert_fusion.2
  106.7 9.4 %shard_map.63.refs_4_ = bf16[512,8192]{1,0:T(8,128)(2,1)} custom-call(s32[16]{0:T(128)} %get-tuple-element.53.sched_ref, bf16[512,1024]{1,0:T(8,128)(2,1)} %kg_ref.3, bf16[4,336,1024]{2,1,0:T(8,128)(2,1)} %get-tuple-element.46.refs_0_, bf16[4,336,1024]{2,1,0:T(8,128)(2,1)} %collective-permute-done.11.refs_1_, ...), custom_call_target="tpu_custom_call" | custom-call | flops 4294967296 | bytes 31457280 | tf_op jit(solution)/shard_map/pallas_call | solution.py:293
  118.8 1.6 copy-done.4
  120.4 9.4 %shard_map.64 = bf16[512,8192]{1,0:T(8,128)(2,1)} custom-call(s32[16]{0:T(128)} %get-tuple-element.57.sched_ref, bf16[512,1024]{1,0:T(8,128)(2,1)} %kg_ref.3, bf16[4,336,1024]{2,1,0:T(8,128)(2,1)} %copy-done.3, bf16[4,336,1024]{2,1,0:T(8,128)(2,1)} %copy-done.4, ...), custom_call_target="tpu_custom_call", output_to_operand_aliasing={{}: (6, {})} | custom-call | flops 4294967296 | bytes 31457280 | tf_op jit(solution)/shard_map/pallas_call | solution.py:293
  130.6 2.6 %shard_map.65 = (bf16[128,1024]{1,0:T(8,128)(2,1)}, bf16[128,1024]{1,0:T(8,128)(2,1)}, bf16[128,1024]{1,0:T(8,128)(2,1)}, bf16[128,1024]{1,0:T(8,128)(2,1)}) custom-call(bf16[4,688,128]{2,1,0:T(8,128)(2,1)} %get-tuple-element.58.refs_0_, bf16[4,688,128]{2,1,0:T(8,128)(2,1)} %collective-permute-done.17.refs_1_, ...), custom_call_target="tpu_custom_call" | custom-call | bytes 1024 | tf_op jit(solution)/shard_map/pallas_call | solution.py:364
  133.2 5.6 %collective-permute-start.19 = (bf16[128,1024]{1,0:T(8,128)(2,1)}, bf16[128,1024]{1,0:T(8,128)(2,1)S(1)}, u32[]{:S(2)}, u32[]{:S(2)}) collective-permute-start(bf16[128,1024]{1,0:T(8,128)(2,1)} %get-tuple-element.62), channel_id=1, source_target_pairs={{0,0},{1,96},{2,2},{3,98},{4,4},{5,100},{6,6},{7,102},{8,8},{9,104... | collective-permute-start | bytes 786440 | tf_op jit(solution)/shard_map/ppermute | solution.py:102
  140.0 5.0 %collective-permute-start.21 = (bf16[128,1024]{1,0:T(8,128)(2,1)}, bf16[128,1024]{1,0:T(8,128)(2,1)S(1)}, u32[]{:S(2)}, u32[]{:S(2)}) collective-permute-start(bf16[128,1024]{1,0:T(8,128)(2,1)} %get-tuple-element.64), channel_id=1, source_target_pairs={{0,24},{1,120},{2,26},{3,122},{4,28},{5,124},{6,30},{7,126},{8,16}... | collective-permute-start | bytes 786440 | tf_op jit(solution)/shard_map/ppermute | solution.py:102
  145.0 3.6 %collective-permute-done.20 = bf16[128,1024]{1,0:T(8,128)(2,1)S(1)} collective-permute-done((bf16[128,1024]{1,0:T(8,128)(2,1)}, bf16[128,1024]{1,0:T(8,128)(2,1)S(1)}, u32[]{:S(2)}, u32[]{:S(2)}) %collective-permute-start.20) | collective-permute-done | bytes 262176 | tf_op jit(solution)/shard_map/ppermute | solution.py:102
  148.6 3.9 %collective-permute-done.21 = bf16[128,1024]{1,0:T(8,128)(2,1)S(1)} collective-permute-done((bf16[128,1024]{1,0:T(8,128)(2,1)}, bf16[128,1024]{1,0:T(8,128)(2,1)S(1)}, u32[]{:S(2)}, u32[]{:S(2)}) %collective-permute-start.21) | collective-permute-done | bytes 262176 | tf_op jit(solution)/shard_map/ppermute | solution.py:102
  152.5 2.8 %collective-permute-done.22 = bf16[128,1024]{1,0:T(8,128)(2,1)S(1)} collective-permute-done((bf16[128,1024]{1,0:T(8,128)(2,1)}, bf16[128,1024]{1,0:T(8,128)(2,1)S(1)}, u32[]{:S(2)}, u32[]{:S(2)}) %collective-permute-start.22) | collective-permute-done | bytes 262176 | tf_op jit(solution)/shard_map/ppermute | solution.py:102
  155.6 1.5 collective-permute-done.23
  (73 shorter events, 20.1 us)
Async XLA Ops:
  5.1 25.6 %collective-permute-start = (bf16[512,2048]{1,0:T(8,128)(2,1)}, bf16[512,2048]{1,0:T(8,128)(2,1)}, u32[]{:S(2)}, u32[]{:S(2)}) collective-permute-start(bf16[512,2048]{1,0:T(8,128)(2,1)} %get-tuple-element.34), channel_id=1, source_target_pairs={{0,1},{1,0},{2,3},{3,2},{4,5},{5,4},{6,7},{7,6},{8,9},{9,8},{10,11... | collective-permute-start | bytes 6291464 | tf_op jit(solution)/shard_map/ppermute | solution.py:91
  6.6 24.1 %collective-permute-start.1 = (bf16[512,2048]{1,0:T(8,128)(2,1)}, bf16[512,2048]{1,0:T(8,128)(2,1)}, u32[]{:S(2)}, u32[]{:S(2)}) collective-permute-start(bf16[512,2048]{1,0:T(8,128)(2,1)} %get-tuple-element.35), channel_id=1, source_target_pairs={{0,1},{1,0},{2,3},{3,2},{4,5},{5,4},{6,7},{7,6},{8,9},{9,8},{10,11... | collective-permute-start | bytes 6291464 | tf_op jit(solution)/shard_map/ppermute | solution.py:91
  6.7 14.9 %collective-permute-start.3 = (bf16[1,336,1024]{2,1,0:T(8,128)(2,1)}, bf16[1,336,1024]{2,1,0:T(8,128)(2,1)S(1)}, u32[]{:S(2)}, u32[]{:S(2)}) collective-permute-start(bf16[1,336,1024]{2,1,0:T(8,128)(2,1)} %get-tuple-element.36.refs_0_), channel_id=1, source_target_pairs={{0,32},{1,97},{2,34},{3,99},{4,36},{5,101},{6,38},{7,103},{8,40},{... | collective-permute-start | bytes 2064392 | tf_op jit(solution)/shard_map/ppermute | solution.py:91
  9.6 12.1 %collective-permute-start.4 = (bf16[1,176,1024]{2,1,0:T(8,128)(2,1)}, bf16[1,176,1024]{2,1,0:T(8,128)(2,1)S(1)}, u32[]{:S(2)}, u32[]{:S(2)}) collective-permute-start(bf16[1,176,1024]{2,1,0:T(8,128)(2,1)} %get-tuple-element.37.refs_2_), channel_id=1, source_target_pairs={{0,24},{1,25},{2,26},{3,27},{4,28},{5,29},{6,30},{7,31},{8,16},{9,... | collective-permute-start | bytes 1081352 | tf_op jit(solution)/shard_map/ppermute | solution.py:91
  13.9 16.9 %collective-permute-start.2 = (bf16[1024,512]{1,0:T(8,128)(2,1)S(1)}, bf16[1024,512]{1,0:T(8,128)(2,1)S(1)}, u32[]{:S(2)}, u32[]{:S(2)}) collective-permute-start(bf16[1024,512]{1,0:T(8,128)(2,1)S(1)} %bitcast.8), channel_id=1, source_target_pairs={{0,1},{1,0},{2,3},{3,2},{4,5},{5,4},{6,7},{7,6},{8,9},{9,8},{10,11... | collective-permute-start | bytes 3145736 | tf_op jit(solution)/shard_map/ppermute | solution.py:91
  26.0 23.2 %collective-permute-start.7 = (bf16[2,336,1024]{2,1,0:T(8,128)(2,1)}, bf16[2,336,1024]{2,1,0:T(8,128)(2,1)S(1)}, u32[]{:S(2)}, u32[]{:S(2)}) collective-permute-start(bf16[2,336,1024]{2,1,0:T(8,128)(2,1)} %get-tuple-element.38.refs_5_.refs_0_), channel_id=1, source_target_pairs={{0,96},{1,25},{2,98},{3,27},{4,100},{5,29},{6,102},{7,31},{8,104},... | collective-permute-start | bytes 4128776 | tf_op jit(solution)/shard_map/ppermute | solution.py:91
  29.7 19.5 %collective-permute-start.8 = (bf16[2,176,1024]{2,1,0:T(8,128)(2,1)}, bf16[2,176,1024]{2,1,0:T(8,128)(2,1)S(1)}, u32[]{:S(2)}, u32[]{:S(2)}) collective-permute-start(bf16[2,176,1024]{2,1,0:T(8,128)(2,1)} %get-tuple-element.39.refs_6_.refs_2_), channel_id=1, source_target_pairs={{0,32},{1,33},{2,34},{3,35},{4,36},{5,37},{6,38},{7,39},{8,40},{9,... | collective-permute-start | bytes 2162696 | tf_op jit(solution)/shard_map/ppermute | solution.py:91
  46.7 34.5 %collective-permute-start.6 = (bf16[16,688,128]{2,1,0:T(8,128)(2,1)}, bf16[16,688,128]{2,1,0:T(8,128)(2,1)S(1)}, u32[]{:S(2)}, u32[]{:S(2)}) collective-permute-start(bf16[16,688,128]{2,1,0:T(8,128)(2,1)} %get-tuple-element.42), channel_id=1, source_target_pairs={{0,2},{1,7},{2,0},{3,5},{4,6},{5,3},{6,4},{7,1},{8,10},{9,15},{10,... | collective-permute-start | bytes 8454152 | tf_op jit(solution)/shard_map/ppermute | solution.py:91
  55.2 32.6 %collective-permute-start.11 = (bf16[4,336,1024]{2,1,0:T(8,128)(2,1)}, bf16[4,336,1024]{2,1,0:T(8,128)(2,1)}, u32[]{:S(2)}, u32[]{:S(2)}) collective-permute-start(bf16[4,336,1024]{2,1,0:T(8,128)(2,1)} %get-tuple-element.46.refs_0_), channel_id=1, source_target_pairs={{0,24},{1,33},{2,26},{3,35},{4,28},{5,37},{6,30},{7,39},{8,16},{9,... | collective-permute-start | bytes 8257544 | tf_op jit(solution)/shard_map/ppermute | solution.py:91
  56.4 32.4 %collective-permute-start.5 = (bf16[16,336,128]{2,1,0:T(8,128)(2,1)}, bf16[16,336,128]{2,1,0:T(8,128)(2,1)S(1)}, u32[]{:S(2)}, u32[]{:S(2)}) collective-permute-start(bf16[16,336,128]{2,1,0:T(8,128)(2,1)} %get-tuple-element.40), channel_id=1, source_target_pairs={{0,8},{1,9},{2,10},{3,11},{4,12},{5,13},{6,14},{7,15},{8,0},{9,1},... | collective-permute-start | bytes 4128776 | tf_op jit(solution)/shard_map/ppermute | solution.py:91
  56.4 34.9 %collective-permute-start.12 = (bf16[4,176,1024]{2,1,0:T(8,128)(2,1)}, bf16[4,176,1024]{2,1,0:T(8,128)(2,1)}, u32[]{:S(2)}, u32[]{:S(2)}) collective-permute-start(bf16[4,176,1024]{2,1,0:T(8,128)(2,1)} %get-tuple-element.54.refs_2_), channel_id=1, source_target_pairs={{0,96},{1,97},{2,98},{3,99},{4,100},{5,101},{6,102},{7,103},{8,104... | collective-permute-start | bytes 4325384 | tf_op jit(solution)/shard_map/ppermute | solution.py:91
  81.9 21.8 %collective-permute-start.10 = (bf16[8,688,128]{2,1,0:T(8,128)(2,1)S(1)}, bf16[8,688,128]{2,1,0:T(8,128)(2,1)S(1)}, u32[]{:S(2)}, u32[]{:S(2)}) collective-permute-start(bf16[8,688,128]{2,1,0:T(8,128)(2,1)S(1)} %get-tuple-element.67), channel_id=1, source_target_pairs={{0,6},{1,9},{2,4},{3,11},{4,2},{5,13},{6,0},{7,15},{8,14},{9,1},{1... | collective-permute-start | bytes 4227080 | tf_op jit(solution)/shard_map/ppermute | solution.py:91
  82.0 35.3 %collective-permute-start.13 = (bf16[4,336,1024]{2,1,0:T(8,128)(2,1)}, bf16[4,336,1024]{2,1,0:T(8,128)(2,1)S(1)}, u32[]{:S(2)}, u32[]{:S(2)}) collective-permute-start(bf16[4,336,1024]{2,1,0:T(8,128)(2,1)} %get-tuple-element.46.refs_0_), channel_id=1, source_target_pairs={{0,1},{1,0},{2,3},{3,2},{4,5},{5,4},{6,7},{7,6},{8,9},{9,8},{10,11... | collective-permute-start | bytes 8257544 | tf_op jit(solution)/shard_map/ppermute | solution.py:91
  87.8 29.5 %collective-permute-start.14 = (bf16[4,336,1024]{2,1,0:T(8,128)(2,1)}, bf16[4,336,1024]{2,1,0:T(8,128)(2,1)S(1)}, u32[]{:S(2)}, u32[]{:S(2)}) collective-permute-start(bf16[4,336,1024]{2,1,0:T(8,128)(2,1)} %collective-permute-done.11.refs_1_), channel_id=1, source_target_pairs={{0,1},{1,0},{2,3},{3,2},{4,5},{5,4},{6,7},{7,6},{8,9},{9,8},{10,11... | collective-permute-start | bytes 8257544 | tf_op jit(solution)/shard_map/ppermute | solution.py:91
  89.1 17.0 %collective-permute-start.9 = (bf16[8,336,128]{2,1,0:T(8,128)(2,1)S(1)}, bf16[8,336,128]{2,1,0:T(8,128)(2,1)S(1)}, u32[]{:S(2)}, u32[]{:S(2)}) collective-permute-start(bf16[8,336,128]{2,1,0:T(8,128)(2,1)S(1)} %get-tuple-element.71), channel_id=1, source_target_pairs={{0,2},{1,3},{2,0},{3,1},{4,6},{5,7},{6,4},{7,5},{8,10},{9,11},{10,... | collective-permute-start | bytes 2064392 | tf_op jit(solution)/shard_map/ppermute | solution.py:91
  91.2 26.1 %collective-permute-start.15 = (bf16[4,176,1024]{2,1,0:T(8,128)(2,1)S(1)}, bf16[4,176,1024]{2,1,0:T(8,128)(2,1)}, u32[]{:S(2)}, u32[]{:S(2)}) collective-permute-start(bf16[4,176,1024]{2,1,0:T(8,128)(2,1)S(1)} %copy-done.5), channel_id=1, source_target_pairs={{0,1},{1,0},{2,3},{3,2},{4,5},{5,4},{6,7},{7,6},{8,9},{9,8},{10,11... | collective-permute-start | bytes 4325384 | tf_op jit(solution)/shard_map/ppermute | solution.py:91
  103.7 13.6 %collective-permute-start.16 = (bf16[4,176,1024]{2,1,0:T(8,128)(2,1)}, bf16[4,176,1024]{2,1,0:T(8,128)(2,1)}, u32[]{:S(2)}, u32[]{:S(2)}) collective-permute-start(bf16[4,176,1024]{2,1,0:T(8,128)(2,1)} %collective-permute-done.12.refs_3_), channel_id=1, source_target_pairs={{0,1},{1,0},{2,3},{3,2},{4,5},{5,4},{6,7},{7,6},{8,9},{9,8},{10,11... | collective-permute-start | bytes 4325384 | tf_op jit(solution)/shard_map/ppermute | solution.py:91
  106.1 11.1 %collective-permute-start.17 = (bf16[4,688,128]{2,1,0:T(8,128)(2,1)}, bf16[4,688,128]{2,1,0:T(8,128)(2,1)}, u32[]{:S(2)}, u32[]{:S(2)}) collective-permute-start(bf16[4,688,128]{2,1,0:T(8,128)(2,1)} %get-tuple-element.69), channel_id=1, source_target_pairs={{0,8},{1,3},{2,10},{3,1},{4,12},{5,7},{6,14},{7,5},{8,0},{9,11},{1... | collective-permute-start | bytes 2113544 | tf_op jit(solution)/shard_map/ppermute | solution.py:91
  117.2 12.7 %collective-permute-start.18 = (bf16[4,336,128]{2,1,0:T(8,128)(2,1)}, bf16[4,336,128]{2,1,0:T(8,128)(2,1)S(1)}, u32[]{:S(2)}, u32[]{:S(2)}) collective-permute-start(bf16[4,336,128]{2,1,0:T(8,128)(2,1)} %get-tuple-element.73), channel_id=1, source_target_pairs={{0,6},{1,7},{2,4},{3,5},{4,2},{5,3},{6,0},{7,1},{8,14},{9,15},{10,... | collective-permute-start | bytes 1032200 | tf_op jit(solution)/shard_map/ppermute | solution.py:91
  133.2 11.8 %collective-permute-start.19 = (bf16[128,1024]{1,0:T(8,128)(2,1)}, bf16[128,1024]{1,0:T(8,128)(2,1)S(1)}, u32[]{:S(2)}, u32[]{:S(2)}) collective-permute-start(bf16[128,1024]{1,0:T(8,128)(2,1)} %get-tuple-element.62), channel_id=1, source_target_pairs={{0,0},{1,96},{2,2},{3,98},{4,4},{5,100},{6,6},{7,102},{8,8},{9,104... | collective-permute-start | bytes 786440 | tf_op jit(solution)/shard_map/ppermute | solution.py:102
  138.8 9.8 %collective-permute-start.20 = (bf16[128,1024]{1,0:T(8,128)(2,1)}, bf16[128,1024]{1,0:T(8,128)(2,1)S(1)}, u32[]{:S(2)}, u32[]{:S(2)}) collective-permute-start(bf16[128,1024]{1,0:T(8,128)(2,1)} %get-tuple-element.63), channel_id=1, source_target_pairs={{0,32},{1,64},{2,34},{3,66},{4,36},{5,68},{6,38},{7,70},{8,40},{9,... | collective-permute-start | bytes 786440 | tf_op jit(solution)/shard_map/ppermute | solution.py:102
  140.0 12.5 %collective-permute-start.21 = (bf16[128,1024]{1,0:T(8,128)(2,1)}, bf16[128,1024]{1,0:T(8,128)(2,1)S(1)}, u32[]{:S(2)}, u32[]{:S(2)}) collective-permute-start(bf16[128,1024]{1,0:T(8,128)(2,1)} %get-tuple-element.64), channel_id=1, source_target_pairs={{0,24},{1,120},{2,26},{3,122},{4,28},{5,124},{6,30},{7,126},{8,16}... | collective-permute-start | bytes 786440 | tf_op jit(solution)/shard_map/ppermute | solution.py:102
  145.0 10.3 %collective-permute-start.22 = (bf16[128,1024]{1,0:T(8,128)(2,1)}, bf16[128,1024]{1,0:T(8,128)(2,1)S(1)}, u32[]{:S(2)}, u32[]{:S(2)}) collective-permute-start(bf16[128,1024]{1,0:T(8,128)(2,1)} %get-tuple-element.65), channel_id=1, source_target_pairs={{0,56},{1,88},{2,58},{3,90},{4,60},{5,92},{6,62},{7,94},{8,48},{9,... | collective-permute-start | bytes 786440 | tf_op jit(solution)/shard_map/ppermute | solution.py:102
  155.5 1.6 %collective-permute-start.23 = (f32[64,1024]{1,0:T(8,128)S(1)}, f32[64,1024]{1,0:T(8,128)S(1)}, u32[]{:S(2)}, u32[]{:S(2)}) collective-permute-start(f32[64,1024]{1,0:T(8,128)S(1)} %constant_dynamic-slice_fusion), channel_id=1, source_target_pairs={{0,1},{1,0},{2,3},{3,2},{4,5},{5,4},{6,7},{7,6},{8,9},{9,8},{10,11... | collective-permute-start | bytes 786440 | tf_op jit(solution)/shard_map/ppermute | solution.py:91
  (15 other events, 122.2 us)

commit v5 on v4

--- a/solution.py
+++ b/solution.py
@@ -16,6 +16,7 @@
 
 RS_A = ((("xA", "xB", "zD"), ("zD", "xA", "xB")), (("xB", "zD", "xA"), ("zD", "xA", "xB")))
 RS_B = ((("zC", "yA"), ("zC", "yA")), (("zC", "yA"), ("zC", "yA")))
+LATE = (0, 0)
 PROJECT = ((0, 1), (1, 1))
 AG = ((("yA", "yB", "zC"), ("zC", "yA", "yB")), (("yB", "zC", "yA"), ("zC", "yA", "yB")))
 
@@ -402,23 +403,25 @@
             where = jnp.concatenate([row[:64], core[None].astype(jnp.int32)])
             parts = partial_blocks(where, acts, got_a, got_b, kt_own, kt_got, norm, have)
             sends, keeps = [parts[0], parts[2]], [parts[1], parts[3]]
-    got = [move(have[k], (AG[0][k][2], AG[1][k][2])) for k in range(2)]
+    got_last = got = [move(have[k], (AG[0][k][2], AG[1][k][2])) for k in range(2)]
     gathered = [have[0], got[0], have[1], got[1]]
-    swapped = [move(g, pair) for g in gathered]
-
-    last, held = [], ()
+    swapped = [move(have[0], pair), None, move(have[1], pair), None]
+
+    last, held = [], (swapped[0],)
     done = have[0]
     input_grads = None
     for stage in range(3):
         for stream in range(2):
             got = move(sends[stream], (RS_A[0][stream][stage], RS_A[1][stream][stage]))
-            got, keep = after((got, keeps[stream]), done, *(held if stream == 1 else ()))
+            got, keep = after((got, keeps[stream]), done, *(held if (stage, stream) != (0, 0) else ()))
             if stage == 2:
                 last.append((keep, got))
                 continue
             n = keep.shape[0] // 2
             done = sends[stream] = add16(keep[n:], got[n:])
             keeps[stream] = add16(keep[:n], got[:n])
+            if (stage, stream) == LATE:
+                swapped[1], swapped[3] = (move(v, pair) for v in after(got_last, done))
             if (stage, stream) == PROJECT[0]:
                 (sched,) = after((row[64:80],), done)
                 input_grads = project(sched, key_grads, gathered, half)

time: 158 us -> 151 us (0.956)
  waiting for transfers between devices: 65.3 us -> 53.9 us
  other arithmetic: 5.16 us -> 9.65 us
  local copies, waits for them, and re-layouts: 10.4 us -> 8.51 us
  starting transfers between devices: 28.7 us -> 30.3 us
    ppermute x20, waiting for transfers between devices: 55 us -> 45.8 us  [move(): return lax.ppermute(value, AXES, pairs)]
    convert_element_type x4, other arithmetic: 3.67 us -> 8.18 us  [add16(): return (a.astype(jnp.float32) + b.astype(jnp.float32)).astype(jnp.bfloat16)]
    ppermute x20, starting transfers between devices: 16.9 us -> 20.7 us  [move(): return lax.ppermute(value, AXES, pairs)]
    ppermute x4, waiting for transfers between devices: 10.3 us -> 8.08 us  [deliver(): return lax.ppermute(value, AXES, pairs)]
    ppermute x4, starting transfers between devices: 11.8 us -> 9.61 us  [deliver(): return lax.ppermute(value, AXES, pairs)]
    unnamed x31 -> x27, local copies, waits for them, and re-layouts: 9.04 us -> 7.19 us
  transfers between devices with their start and end apart: 24 -> 24, of which waited for: 11 -> 8; matrix products, arithmetic and copies ran while one was open for 4% -> 7% of each run, Pallas kernels for 26% -> 27%
where the time goes in v5:
time: 151 us
  waiting for transfers between devices  53.9 us (36%)
  Pallas kernels  47.5 us (31%)
  starting transfers between devices  30.3 us (20%)
  other arithmetic  9.65 us (6%)
  local copies, waits for them, and re-layouts  8.51 us (6%)
    ppermute x20, waiting for transfers between devices, move(): return lax.ppermute(value, AXES, pairs)  45.8 us
    ppermute x20, starting transfers between devices, move(): return lax.ppermute(value, AXES, pairs)  20.7 us
    pallas_call x2, Pallas kernels, project(): pl.pallas_call(functools.partial(project_body, half, rest, len(lasts)), i...  18.9 us
    pallas_call x1, Pallas kernels, partial_blocks(): pl.pallas_call(body, in_specs=[pl.BlockSpec(memory_space=pltpu.SMEM)] + [...  14.8 us
    ppermute x4, starting transfers between devices, deliver(): return lax.ppermute(value, AXES, pairs)  9.61 us
    convert_element_type x4, other arithmetic, add16(): return (a.astype(jnp.float32) + b.astype(jnp.float32)).astype(jnp.bfloat16)  8.18 us
    ppermute x4, waiting for transfers between devices, deliver(): return lax.ppermute(value, AXES, pairs)  8.08 us
    unnamed x27, local copies, waits for them, and re-layouts  7.19 us
  transfers between devices with their start and end apart: 24, of which 8 were waited for; matrix products, arithmetic and copies ran while one was open for 7% of the time, Pallas kernels for 27%

profile of v5, /device:TPU:1, one launch (start us, length us, event | category | flops | bytes accessed | tf_op | source)
XLA Modules:
  0.0 150.8 jit_solution(3025620286153231491)
XLA Ops:
  0.7 4.5 %shard_map.59 = (bf16[1,336,1024]{2,1,0:T(8,128)(2,1)}, bf16[1,176,1024]{2,1,0:T(8,128)(2,1)}, bf16[512,2048]{1,0:T(8,128)(2,1)}, bf16[512,2048]{1,0:T(8,128)(2,1)}) custom-call(s32[1]{0:T(128)} %bitcast.2.core_ref, bf16[512,8192]{1,0:T(8,128)(2,1)} %refs_0_.1, bf16[1024,1024]{1,0:T(8,128)(2,1)} %weight.1), custom_call_target="tpu_custom_call" | custom-call | bytes 1024 | tf_op jit(solution)/shard_map/pallas_call | solution.py:141
  6.7 2.8 %collective-permute-start.3 = (bf16[1,336,1024]{2,1,0:T(8,128)(2,1)}, bf16[1,336,1024]{2,1,0:T(8,128)(2,1)}, u32[]{:S(2)}, u32[]{:S(2)}) collective-permute-start(bf16[1,336,1024]{2,1,0:T(8,128)(2,1)} %get-tuple-element.38.refs_0_), channel_id=1, source_target_pairs={{0,32},{1,97},{2,34},{3,99},{4,36},{5,101},{6,38},{7,103},{8,40},{... | collective-permute-start | bytes 2064392 | tf_op jit(solution)/shard_map/ppermute | solution.py:92
  9.5 3.8 %collective-permute-start.4 = (bf16[1,176,1024]{2,1,0:T(8,128)(2,1)}, bf16[1,176,1024]{2,1,0:T(8,128)(2,1)}, u32[]{:S(2)}, u32[]{:S(2)}) collective-permute-start(bf16[1,176,1024]{2,1,0:T(8,128)(2,1)} %get-tuple-element.39.refs_2_), channel_id=1, source_target_pairs={{0,24},{1,25},{2,26},{3,27},{4,28},{5,29},{6,30},{7,31},{8,16},{9,... | collective-permute-start | bytes 1081352 | tf_op jit(solution)/shard_map/ppermute | solution.py:92
  14.0 7.8 %collective-permute-done.4.refs_3_ = bf16[1,176,1024]{2,1,0:T(8,128)(2,1)} collective-permute-done((bf16[1,176,1024]{2,1,0:T(8,128)(2,1)}, bf16[1,176,1024]{2,1,0:T(8,128)(2,1)}, u32[]{:S(2)}, u32[]{:S(2)}) %collective-permute-start.4) | collective-permute-done | bytes 360480 | tf_op jit(solution)/shard_map/ppermute | solution.py:92
  21.7 2.7 %shard_map.60 = (bf16[2,336,1024]{2,1,0:T(8,128)(2,1)}, bf16[2,176,1024]{2,1,0:T(8,128)(2,1)}) custom-call(bf16[1,336,1024]{2,1,0:T(8,128)(2,1)} %get-tuple-element.38.refs_0_, bf16[1,336,1024]{2,1,0:T(8,128)(2,1)} %collective-permute-done.3.refs_1_, bf16[1,176,1024]{2,1,0:T(8,128)(2,1)} %get-tuple-element.39.refs_2_, ...), custom_call_target="tpu_custom_call" | custom-call | bytes 1024 | tf_op jit(solution)/shard_map/pallas_call | solution.py:337
  24.4 3.0 %collective-permute-start.7 = (bf16[2,336,1024]{2,1,0:T(8,128)(2,1)}, bf16[2,336,1024]{2,1,0:T(8,128)(2,1)S(1)}, u32[]{:S(2)}, u32[]{:S(2)}) collective-permute-start(bf16[2,336,1024]{2,1,0:T(8,128)(2,1)} %get-tuple-element.40.refs_5_.refs_0_), channel_id=1, source_target_pairs={{0,96},{1,25},{2,98},{3,27},{4,100},{5,29},{6,102},{7,31},{8,104},... | collective-permute-start | bytes 4128776 | tf_op jit(solution)/shard_map/ppermute | solution.py:92
  30.1 14.8 %shard_map.61 = (bf16[16,688,128]{2,1,0:T(8,128)(2,1)}, bf16[16,688,128]{2,1,0:T(8,128)(2,1)}, bf16[16,336,128]{2,1,0:T(8,128)(2,1)}, bf16[16,336,128]{2,1,0:T(8,128)(2,1)}) custom-call(s32[65]{0:T(128)} %pad_add_fusion.where_ref, bf16[512,8192]{1,0:T(8,128)(2,1)} %refs_0_.1, bf16[512,2048]{1,0:T(8,128)(2,1)} %collective-permute-done.refs_1_, ...), custom_call_target="tpu_custom_call" | custom-call | bytes 1024 | tf_op jit(solution)/shard_map/pallas_call | solution.py:233
  45.0 2.6 %collective-permute-start.6 = (bf16[16,688,128]{2,1,0:T(8,128)(2,1)}, bf16[16,688,128]{2,1,0:T(8,128)(2,1)S(1)}, u32[]{:S(2)}, u32[]{:S(2)}) collective-permute-start(bf16[16,688,128]{2,1,0:T(8,128)(2,1)} %get-tuple-element.44), channel_id=1, source_target_pairs={{0,2},{1,7},{2,0},{3,5},{4,6},{5,3},{6,4},{7,1},{8,10},{9,15},{10,... | collective-permute-start | bytes 8454152 | tf_op jit(solution)/shard_map/ppermute | solution.py:92
  48.9 4.1 %shard_map.62 = (bf16[4,336,1024]{2,1,0:T(8,128)(2,1)}, bf16[4,176,1024]{2,1,0:T(8,128)(2,1)}) custom-call(bf16[2,336,1024]{2,1,0:T(8,128)(2,1)} %get-tuple-element.40.refs_5_.refs_0_, bf16[2,336,1024]{2,1,0:T(8,128)(2,1)} %copy-done.8, bf16[2,176,1024]{2,1,0:T(8,128)(2,1)} %get-tuple-element.41.refs_6_.refs_2_, bf16[2,176,1024]{2,1,0:T(8,128)(2,1)} %copy-done.10), custom_call_target="tpu_custom_call" | custom-call | bytes 1024 | tf_op jit(solution)/shard_map/pallas_call | solution.py:337
  55.7 23.8 %collective-permute-done.6 = bf16[16,688,128]{2,1,0:T(8,128)(2,1)S(1)} collective-permute-done((bf16[16,688,128]{2,1,0:T(8,128)(2,1)}, bf16[16,688,128]{2,1,0:T(8,128)(2,1)S(1)}, u32[]{:S(2)}, u32[]{:S(2)}) %collective-permute-start.6) | collective-permute-done | bytes 2818080 | tf_op jit(solution)/shard_map/ppermute | solution.py:92
  79.5 1.8 %add_convert_fusion = (bf16[8,688,128]{2,1,0:T(8,128)(2,1)S(1)}, bf16[8,688,128]{2,1,0:T(8,128)(2,1)}) fusion(bf16[16,688,128]{2,1,0:T(8,128)(2,1)S(1)} %collective-permute-done.6, bf16[16,688,128]{2,1,0:T(8,128)(2,1)S(1)} %copy-done.2), kind=kLoop, calls=%fused_computation | loop fusion | flops 5636096 | bytes 8454144 | tf_op jit(solution)/shard_map/convert_element_type | solution.py:381
  81.3 7.6 %collective-permute-done.13.refs_3_ = bf16[4,176,1024]{2,1,0:T(8,128)(2,1)} collective-permute-done((bf16[4,176,1024]{2,1,0:T(8,128)(2,1)}, bf16[4,176,1024]{2,1,0:T(8,128)(2,1)}, u32[]{:S(2)}, u32[]{:S(2)}) %collective-permute-start.13) | collective-permute-done | bytes 1441824 | tf_op jit(solution)/shard_map/ppermute | solution.py:92
  92.5 9.4 %shard_map.63.refs_4_ = bf16[512,8192]{1,0:T(8,128)(2,1)} custom-call(s32[16]{0:T(128)} %get-tuple-element.53.sched_ref, bf16[512,1024]{1,0:T(8,128)(2,1)} %kg_ref.3, bf16[4,336,1024]{2,1,0:T(8,128)(2,1)} %get-tuple-element.48.refs_0_, bf16[4,336,1024]{2,1,0:T(8,128)(2,1)} %collective-permute-done.12.refs_1_, ...), custom_call_target="tpu_custom_call" | custom-call | flops 4294967296 | bytes 31457280 | tf_op jit(solution)/shard_map/pallas_call | solution.py:294
  102.0 5.5 %collective-permute-done.11 = bf16[8,688,128]{2,1,0:T(8,128)(2,1)} collective-permute-done((bf16[8,688,128]{2,1,0:T(8,128)(2,1)}, bf16[8,688,128]{2,1,0:T(8,128)(2,1)}, u32[]{:S(2)}, u32[]{:S(2)}) %collective-permute-start.11) | collective-permute-done | bytes 1409056 | tf_op jit(solution)/shard_map/ppermute | solution.py:92
  107.4 2.8 %add_convert_fusion.2 = (bf16[4,688,128]{2,1,0:T(8,128)(2,1)}, bf16[4,688,128]{2,1,0:T(8,128)(2,1)}) fusion(bf16[8,688,128]{2,1,0:T(8,128)(2,1)} %collective-permute-done.11, bf16[8,688,128]{2,1,0:T(8,128)(2,1)S(1)} %get-tuple-element.55), kind=kLoop, calls=%fused_computation.2 | loop fusion | flops 2818048 | bytes 4227072 | tf_op jit(solution)/shard_map/convert_element_type | solution.py:381
  110.5 2.0 %add_convert_fusion.6 = (bf16[4,336,128]{2,1,0:T(8,128)(2,1)}, bf16[4,336,128]{2,1,0:T(8,128)(2,1)S(1)}) fusion(bf16[8,336,128]{2,1,0:T(8,128)(2,1)} %collective-permute-done.10, bf16[8,336,128]{2,1,0:T(8,128)(2,1)S(1)} %get-tuple-element.57), kind=kLoop, calls=%fused_computation.6 | loop fusion | flops 1376256 | bytes 2064384 | tf_op jit(solution)/shard_map/convert_element_type | solution.py:381
  115.2 1.5 %copy-done.4 = bf16[4,336,1024]{2,1,0:T(8,128)(2,1)} copy-done((bf16[4,336,1024]{2,1,0:T(8,128)(2,1)}, bf16[4,336,1024]{2,1,0:T(8,128)(2,1)S(1)}, u32[]{:S(2)}) %copy-start.4) | copy-done | bytes 2752536
  116.7 9.4 %shard_map.64 = bf16[512,8192]{1,0:T(8,128)(2,1)} custom-call(s32[16]{0:T(128)} %get-tuple-element.59.sched_ref, bf16[512,1024]{1,0:T(8,128)(2,1)} %kg_ref.3, bf16[4,336,1024]{2,1,0:T(8,128)(2,1)} %copy-done.3, bf16[4,336,1024]{2,1,0:T(8,128)(2,1)} %copy-done.4, bf16[4,176,1024]{2,1,0:T(8,128)(2,1)} %copy-done.5, ...), custom_call_target="tpu_custom_call", output_to_operand_aliasing={{}: (6, {})} | custom-call | flops 4294967296 | bytes 31457280 | tf_op jit(solution)/shard_map/pallas_call | solution.py:294
  127.2 2.6 %shard_map.65 = (bf16[128,1024]{1,0:T(8,128)(2,1)}, bf16[128,1024]{1,0:T(8,128)(2,1)}, bf16[128,1024]{1,0:T(8,128)(2,1)}, bf16[128,1024]{1,0:T(8,128)(2,1)}) custom-call(bf16[4,688,128]{2,1,0:T(8,128)(2,1)} %get-tuple-element.62.refs_0_, bf16[4,688,128]{2,1,0:T(8,128)(2,1)} %copy-done.11, bf16[4,336,128]{2,1,0:T(8,128)(2,1)} %get-tuple-element.64.refs_2_, ...), custom_call_target="tpu_custom_call" | custom-call | bytes 1024 | tf_op jit(solution)/shard_map/pallas_call | solution.py:365
  129.8 4.2 %collective-permute-start.22 = (bf16[128,1024]{1,0:T(8,128)(2,1)}, bf16[128,1024]{1,0:T(8,128)(2,1)S(1)}, u32[]{:S(2)}, u32[]{:S(2)}) collective-permute-start(bf16[128,1024]{1,0:T(8,128)(2,1)} %get-tuple-element.69), channel_id=1, source_target_pairs={{0,56},{1,88},{2,58},{3,90},{4,60},{5,92},{6,62},{7,94},{8,48},{9,... | collective-permute-start | bytes 786440 | tf_op jit(solution)/shard_map/ppermute | solution.py:103
  134.0 2.5 %collective-permute-start.20 = (bf16[128,1024]{1,0:T(8,128)(2,1)}, bf16[128,1024]{1,0:T(8,128)(2,1)S(1)}, u32[]{:S(2)}, u32[]{:S(2)}) collective-permute-start(bf16[128,1024]{1,0:T(8,128)(2,1)} %get-tuple-element.67), channel_id=1, source_target_pairs={{0,32},{1,64},{2,34},{3,66},{4,36},{5,68},{6,38},{7,70},{8,40},{9,... | collective-permute-start | bytes 786440 | tf_op jit(solution)/shard_map/ppermute | solution.py:103
  136.5 2.9 %collective-permute-start.19 = (bf16[128,1024]{1,0:T(8,128)(2,1)}, bf16[128,1024]{1,0:T(8,128)(2,1)S(1)}, u32[]{:S(2)}, u32[]{:S(2)}) collective-permute-start(bf16[128,1024]{1,0:T(8,128)(2,1)} %get-tuple-element.66), channel_id=1, source_target_pairs={{0,0},{1,96},{2,2},{3,98},{4,4},{5,100},{6,6},{7,102},{8,8},{9,104... | collective-permute-start | bytes 786440 | tf_op jit(solution)/shard_map/ppermute | solution.py:103
  139.4 3.8 %collective-permute-done.22 = bf16[128,1024]{1,0:T(8,128)(2,1)S(1)} collective-permute-done((bf16[128,1024]{1,0:T(8,128)(2,1)}, bf16[128,1024]{1,0:T(8,128)(2,1)S(1)}, u32[]{:S(2)}, u32[]{:S(2)}) %collective-permute-start.22) | collective-permute-done | bytes 262176 | tf_op jit(solution)/shard_map/ppermute | solution.py:103
  143.3 3.9 %collective-permute-done.21 = bf16[128,1024]{1,0:T(8,128)(2,1)S(1)} collective-permute-done((bf16[128,1024]{1,0:T(8,128)(2,1)}, bf16[128,1024]{1,0:T(8,128)(2,1)S(1)}, u32[]{:S(2)}, u32[]{:S(2)}) %collective-permute-start.21) | collective-permute-done | bytes 262176 | tf_op jit(solution)/shard_map/ppermute | solution.py:103
  (69 shorter events, 20.0 us)
Async XLA Ops:
  5.1 24.0 %collective-permute-start = (bf16[512,2048]{1,0:T(8,128)(2,1)}, bf16[512,2048]{1,0:T(8,128)(2,1)}, u32[]{:S(2)}, u32[]{:S(2)}) collective-permute-start(bf16[512,2048]{1,0:T(8,128)(2,1)} %get-tuple-element.36), channel_id=1, source_target_pairs={{0,1},{1,0},{2,3},{3,2},{4,5},{5,4},{6,7},{7,6},{8,9},{9,8},{10,11... | collective-permute-start | bytes 6291464 | tf_op jit(solution)/shard_map/ppermute | solution.py:92
  6.6 22.5 %collective-permute-start.1 = (bf16[512,2048]{1,0:T(8,128)(2,1)}, bf16[512,2048]{1,0:T(8,128)(2,1)}, u32[]{:S(2)}, u32[]{:S(2)}) collective-permute-start(bf16[512,2048]{1,0:T(8,128)(2,1)} %get-tuple-element.37), channel_id=1, source_target_pairs={{0,1},{1,0},{2,3},{3,2},{4,5},{5,4},{6,7},{7,6},{8,9},{9,8},{10,11... | collective-permute-start | bytes 6291464 | tf_op jit(solution)/shard_map/ppermute | solution.py:92
  6.7 15.0 %collective-permute-start.3 = (bf16[1,336,1024]{2,1,0:T(8,128)(2,1)}, bf16[1,336,1024]{2,1,0:T(8,128)(2,1)}, u32[]{:S(2)}, u32[]{:S(2)}) collective-permute-start(bf16[1,336,1024]{2,1,0:T(8,128)(2,1)} %get-tuple-element.38.refs_0_), channel_id=1, source_target_pairs={{0,32},{1,97},{2,34},{3,99},{4,36},{5,101},{6,38},{7,103},{8,40},{... | collective-permute-start | bytes 2064392 | tf_op jit(solution)/shard_map/ppermute | solution.py:92
  9.5 12.2 %collective-permute-start.4 = (bf16[1,176,1024]{2,1,0:T(8,128)(2,1)}, bf16[1,176,1024]{2,1,0:T(8,128)(2,1)}, u32[]{:S(2)}, u32[]{:S(2)}) collective-permute-start(bf16[1,176,1024]{2,1,0:T(8,128)(2,1)} %get-tuple-element.39.refs_2_), channel_id=1, source_target_pairs={{0,24},{1,25},{2,26},{3,27},{4,28},{5,29},{6,30},{7,31},{8,16},{9,... | collective-permute-start | bytes 1081352 | tf_op jit(solution)/shard_map/ppermute | solution.py:92
  13.9 15.3 %collective-permute-start.2 = (bf16[1024,512]{1,0:T(8,128)(2,1)S(1)}, bf16[1024,512]{1,0:T(8,128)(2,1)S(1)}, u32[]{:S(2)}, u32[]{:S(2)}) collective-permute-start(bf16[1024,512]{1,0:T(8,128)(2,1)S(1)} %bitcast.8), channel_id=1, source_target_pairs={{0,1},{1,0},{2,3},{3,2},{4,5},{5,4},{6,7},{7,6},{8,9},{9,8},{10,11... | collective-permute-start | bytes 3145736 | tf_op jit(solution)/shard_map/ppermute | solution.py:92
  24.4 23.1 %collective-permute-start.7 = (bf16[2,336,1024]{2,1,0:T(8,128)(2,1)}, bf16[2,336,1024]{2,1,0:T(8,128)(2,1)S(1)}, u32[]{:S(2)}, u32[]{:S(2)}) collective-permute-start(bf16[2,336,1024]{2,1,0:T(8,128)(2,1)} %get-tuple-element.40.refs_5_.refs_0_), channel_id=1, source_target_pairs={{0,96},{1,25},{2,98},{3,27},{4,100},{5,29},{6,102},{7,31},{8,104},... | collective-permute-start | bytes 4128776 | tf_op jit(solution)/shard_map/ppermute | solution.py:92
  28.1 19.4 %collective-permute-start.8 = (bf16[2,176,1024]{2,1,0:T(8,128)(2,1)}, bf16[2,176,1024]{2,1,0:T(8,128)(2,1)S(1)}, u32[]{:S(2)}, u32[]{:S(2)}) collective-permute-start(bf16[2,176,1024]{2,1,0:T(8,128)(2,1)} %get-tuple-element.41.refs_6_.refs_2_), channel_id=1, source_target_pairs={{0,32},{1,33},{2,34},{3,35},{4,36},{5,37},{6,38},{7,39},{8,40},{9,... | collective-permute-start | bytes 2162696 | tf_op jit(solution)/shard_map/ppermute | solution.py:92
  45.0 34.5 %collective-permute-start.6 = (bf16[16,688,128]{2,1,0:T(8,128)(2,1)}, bf16[16,688,128]{2,1,0:T(8,128)(2,1)S(1)}, u32[]{:S(2)}, u32[]{:S(2)}) collective-permute-start(bf16[16,688,128]{2,1,0:T(8,128)(2,1)} %get-tuple-element.44), channel_id=1, source_target_pairs={{0,2},{1,7},{2,0},{3,5},{4,6},{5,3},{6,4},{7,1},{8,10},{9,15},{10,... | collective-permute-start | bytes 8454152 | tf_op jit(solution)/shard_map/ppermute | solution.py:92
  53.0 36.0 %collective-permute-start.12 = (bf16[4,336,1024]{2,1,0:T(8,128)(2,1)}, bf16[4,336,1024]{2,1,0:T(8,128)(2,1)}, u32[]{:S(2)}, u32[]{:S(2)}) collective-permute-start(bf16[4,336,1024]{2,1,0:T(8,128)(2,1)} %get-tuple-element.48.refs_0_), channel_id=1, source_target_pairs={{0,24},{1,33},{2,26},{3,35},{4,28},{5,37},{6,30},{7,39},{8,16},{9,... | collective-permute-start | bytes 8257544 | tf_op jit(solution)/shard_map/ppermute | solution.py:92
  54.1 34.8 %collective-permute-start.13 = (bf16[4,176,1024]{2,1,0:T(8,128)(2,1)}, bf16[4,176,1024]{2,1,0:T(8,128)(2,1)}, u32[]{:S(2)}, u32[]{:S(2)}) collective-permute-start(bf16[4,176,1024]{2,1,0:T(8,128)(2,1)} %get-tuple-element.54.refs_2_), channel_id=1, source_target_pairs={{0,96},{1,97},{2,98},{3,99},{4,100},{5,101},{6,102},{7,103},{8,104... | collective-permute-start | bytes 4325384 | tf_op jit(solution)/shard_map/ppermute | solution.py:92
  54.3 36.4 %collective-permute-start.9 = (bf16[4,336,1024]{2,1,0:T(8,128)(2,1)}, bf16[4,336,1024]{2,1,0:T(8,128)(2,1)S(1)}, u32[]{:S(2)}, u32[]{:S(2)}) collective-permute-start(bf16[4,336,1024]{2,1,0:T(8,128)(2,1)} %get-tuple-element.48.refs_0_), channel_id=1, source_target_pairs={{0,1},{1,0},{2,3},{3,2},{4,5},{5,4},{6,7},{7,6},{8,9},{9,8},{10,11... | collective-permute-start | bytes 8257544 | tf_op jit(solution)/shard_map/ppermute | solution.py:92
  55.7 34.5 %collective-permute-start.5 = (bf16[16,336,128]{2,1,0:T(8,128)(2,1)}, bf16[16,336,128]{2,1,0:T(8,128)(2,1)S(1)}, u32[]{:S(2)}, u32[]{:S(2)}) collective-permute-start(bf16[16,336,128]{2,1,0:T(8,128)(2,1)} %get-tuple-element.42), channel_id=1, source_target_pairs={{0,8},{1,9},{2,10},{3,11},{4,12},{5,13},{6,14},{7,15},{8,0},{9,1},... | collective-permute-start | bytes 4128776 | tf_op jit(solution)/shard_map/ppermute | solution.py:92
  88.9 24.7 %collective-permute-start.14 = (bf16[4,336,1024]{2,1,0:T(8,128)(2,1)}, bf16[4,336,1024]{2,1,0:T(8,128)(2,1)S(1)}, u32[]{:S(2)}, u32[]{:S(2)}) collective-permute-start(bf16[4,336,1024]{2,1,0:T(8,128)(2,1)} %collective-permute-done.12.refs_1_), channel_id=1, source_target_pairs={{0,1},{1,0},{2,3},{3,2},{4,5},{5,4},{6,7},{7,6},{8,9},{9,8},{10,11... | collective-permute-start | bytes 8257544 | tf_op jit(solution)/shard_map/ppermute | solution.py:92
  89.3 18.1 %collective-permute-start.11 = (bf16[8,688,128]{2,1,0:T(8,128)(2,1)}, bf16[8,688,128]{2,1,0:T(8,128)(2,1)}, u32[]{:S(2)}, u32[]{:S(2)}) collective-permute-start(bf16[8,688,128]{2,1,0:T(8,128)(2,1)} %get-tuple-element.71), channel_id=1, source_target_pairs={{0,6},{1,9},{2,4},{3,11},{4,2},{5,13},{6,0},{7,15},{8,14},{9,1},{1... | collective-permute-start | bytes 4227080 | tf_op jit(solution)/shard_map/ppermute | solution.py:92
  89.3 24.3 %collective-permute-start.15 = (bf16[4,176,1024]{2,1,0:T(8,128)(2,1)}, bf16[4,176,1024]{2,1,0:T(8,128)(2,1)S(1)}, u32[]{:S(2)}, u32[]{:S(2)}) collective-permute-start(bf16[4,176,1024]{2,1,0:T(8,128)(2,1)} %get-tuple-element.54.refs_2_), channel_id=1, source_target_pairs={{0,1},{1,0},{2,3},{3,2},{4,5},{5,4},{6,7},{7,6},{8,9},{9,8},{10,11... | collective-permute-start | bytes 4325384 | tf_op jit(solution)/shard_map/ppermute | solution.py:92
  90.1 23.4 %collective-permute-start.16 = (bf16[4,176,1024]{2,1,0:T(8,128)(2,1)}, bf16[4,176,1024]{2,1,0:T(8,128)(2,1)S(1)}, u32[]{:S(2)}, u32[]{:S(2)}) collective-permute-start(bf16[4,176,1024]{2,1,0:T(8,128)(2,1)} %collective-permute-done.13.refs_3_), channel_id=1, source_target_pairs={{0,1},{1,0},{2,3},{3,2},{4,5},{5,4},{6,7},{7,6},{8,9},{9,8},{10,11... | collective-permute-start | bytes 4325384 | tf_op jit(solution)/shard_map/ppermute | solution.py:92
  92.5 18.0 %collective-permute-start.10 = (bf16[8,336,128]{2,1,0:T(8,128)(2,1)}, bf16[8,336,128]{2,1,0:T(8,128)(2,1)}, u32[]{:S(2)}, u32[]{:S(2)}) collective-permute-start(bf16[8,336,128]{2,1,0:T(8,128)(2,1)} %get-tuple-element.75), channel_id=1, source_target_pairs={{0,2},{1,3},{2,0},{3,1},{4,6},{5,7},{6,4},{7,5},{8,10},{9,11},{10,... | collective-permute-start | bytes 2064392 | tf_op jit(solution)/shard_map/ppermute | solution.py:92
  110.3 15.9 %collective-permute-start.17 = (bf16[4,688,128]{2,1,0:T(8,128)(2,1)}, bf16[4,688,128]{2,1,0:T(8,128)(2,1)S(1)}, u32[]{:S(2)}, u32[]{:S(2)}) collective-permute-start(bf16[4,688,128]{2,1,0:T(8,128)(2,1)} %get-tuple-element.73), channel_id=1, source_target_pairs={{0,8},{1,3},{2,10},{3,1},{4,12},{5,7},{6,14},{7,5},{8,0},{9,11},{1... | collective-permute-start | bytes 2113544 | tf_op jit(solution)/shard_map/ppermute | solution.py:92
  112.6 13.6 %collective-permute-start.18 = (bf16[4,336,128]{2,1,0:T(8,128)(2,1)S(1)}, bf16[4,336,128]{2,1,0:T(8,128)(2,1)S(1)}, u32[]{:S(2)}, u32[]{:S(2)}) collective-permute-start(bf16[4,336,128]{2,1,0:T(8,128)(2,1)S(1)} %get-tuple-element.77), channel_id=1, source_target_pairs={{0,6},{1,7},{2,4},{3,5},{4,2},{5,3},{6,0},{7,1},{8,14},{9,15},{10,... | collective-permute-start | bytes 1032200 | tf_op jit(solution)/shard_map/ppermute | solution.py:92
  129.8 13.5 %collective-permute-start.22 = (bf16[128,1024]{1,0:T(8,128)(2,1)}, bf16[128,1024]{1,0:T(8,128)(2,1)S(1)}, u32[]{:S(2)}, u32[]{:S(2)}) collective-permute-start(bf16[128,1024]{1,0:T(8,128)(2,1)} %get-tuple-element.69), channel_id=1, source_target_pairs={{0,56},{1,88},{2,58},{3,90},{4,60},{5,92},{6,62},{7,94},{8,48},{9,... | collective-permute-start | bytes 786440 | tf_op jit(solution)/shard_map/ppermute | solution.py:103
  134.0 13.1 %collective-permute-start.21 = (bf16[128,1024]{1,0:T(8,128)(2,1)}, bf16[128,1024]{1,0:T(8,128)(2,1)S(1)}, u32[]{:S(2)}, u32[]{:S(2)}) collective-permute-start(bf16[128,1024]{1,0:T(8,128)(2,1)} %get-tuple-element.68), channel_id=1, source_target_pairs={{0,24},{1,120},{2,26},{3,122},{4,28},{5,124},{6,30},{7,126},{8,16}... | collective-permute-start | bytes 786440 | tf_op jit(solution)/shard_map/ppermute | solution.py:103
  134.0 13.1 %collective-permute-start.20 = (bf16[128,1024]{1,0:T(8,128)(2,1)}, bf16[128,1024]{1,0:T(8,128)(2,1)S(1)}, u32[]{:S(2)}, u32[]{:S(2)}) collective-permute-start(bf16[128,1024]{1,0:T(8,128)(2,1)} %get-tuple-element.67), channel_id=1, source_target_pairs={{0,32},{1,64},{2,34},{3,66},{4,36},{5,68},{6,38},{7,70},{8,40},{9,... | collective-permute-start | bytes 786440 | tf_op jit(solution)/shard_map/ppermute | solution.py:103
  136.5 11.0 %collective-permute-start.19 = (bf16[128,1024]{1,0:T(8,128)(2,1)}, bf16[128,1024]{1,0:T(8,128)(2,1)S(1)}, u32[]{:S(2)}, u32[]{:S(2)}) collective-permute-start(bf16[128,1024]{1,0:T(8,128)(2,1)} %get-tuple-element.66), channel_id=1, source_target_pairs={{0,0},{1,96},{2,2},{3,98},{4,4},{5,100},{6,6},{7,102},{8,8},{9,104... | collective-permute-start | bytes 786440 | tf_op jit(solution)/shard_map/ppermute | solution.py:103
  147.7 2.3 %collective-permute-start.23 = (f32[64,1024]{1,0:T(8,128)S(1)}, f32[64,1024]{1,0:T(8,128)S(1)}, u32[]{:S(2)}, u32[]{:S(2)}) collective-permute-start(f32[64,1024]{1,0:T(8,128)S(1)} %constant_dynamic-slice_fusion), channel_id=1, source_target_pairs={{0,1},{1,0},{2,3},{3,2},{4,5},{5,4},{6,7},{7,6},{8,9},{9,8},{10,11... | collective-permute-start | bytes 786440 | tf_op jit(solution)/shard_map/ppermute | solution.py:92
  (13 other events, 105.0 us)

commit v6 on v5

--- a/solution.py
+++ b/solution.py
@@ -10,7 +10,7 @@
 
 SIZES = (4, 2, 2, 4, 2)
 AXES = ("intra", "inter")
-S1 = 688
+S1 = 720
 T1 = 336
 BLK = 128
 

time: 151 us -> 150 us (level)
    unnamed x27 -> x25, local copies, waits for them, and re-layouts: 7.19 us -> 6.77 us
  transfers between devices with their start and end apart: 24 -> 24, of which waited for: 8 -> 8; matrix products, arithmetic and copies ran while one was open for 7% -> 6% of each run, Pallas kernels for 27% -> 27%
where the time goes in v6:
time: 150 us; the launch traced here: 149 us
  waiting for transfers between devices  54.7 us (36%)
  Pallas kernels  47.5 us (32%)
  starting transfers between devices  30 us (20%)
  other arithmetic  8.27 us (6%)
  local copies, waits for them, and re-layouts  8.07 us (5%)
    ppermute x20, waiting for transfers between devices, move(): return lax.ppermute(value, AXES, pairs)  46.6 us
    ppermute x20, starting transfers between devices, move(): return lax.ppermute(value, AXES, pairs)  20.4 us
    pallas_call x2, Pallas kernels, project(): pl.pallas_call(functools.partial(project_body, half, rest, len(lasts)), i...  18.9 us
    pallas_call x1, Pallas kernels, partial_blocks(): pl.pallas_call(body, in_specs=[pl.BlockSpec(memory_space=pltpu.SMEM)] + [...  14.8 us
    ppermute x4, starting transfers between devices, deliver(): return lax.ppermute(value, AXES, pairs)  9.61 us
    ppermute x4, waiting for transfers between devices, deliver(): return lax.ppermute(value, AXES, pairs)  8.16 us
    convert_element_type x4, other arithmetic, add16(): return (a.astype(jnp.float32) + b.astype(jnp.float32)).astype(jnp.bfloat16)  6.8 us
    unnamed x25, local copies, waits for them, and re-layouts  6.77 us
  transfers between devices with their start and end apart: 24, of which 8 were waited for; matrix products, arithmetic and copies ran while one was open for 6% of the time, Pallas kernels for 27%

profile of v6, /device:TPU:1, one launch (start us, length us, event | category | flops | bytes accessed | tf_op | source)
XLA Modules:
  0.0 149.5 jit_solution(12884273083192668722)
XLA Ops:
  0.7 4.5 %shard_map.59 = (bf16[1,336,1024]{2,1,0:T(8,128)(2,1)}, bf16[1,176,1024]{2,1,0:T(8,128)(2,1)}, bf16[512,2048]{1,0:T(8,128)(2,1)}, bf16[512,2048]{1,0:T(8,128)(2,1)}) custom-call(s32[1]{0:T(128)} %bitcast.2.core_ref, bf16[512,8192]{1,0:T(8,128)(2,1)} %refs_0_.1, bf16[1024,1024]{1,0:T(8,128)(2,1)} %weight.1), custom_call_target="tpu_custom_call" | custom-call | bytes 1024 | tf_op jit(solution)/shard_map/pallas_call | solution.py:141
  6.8 2.8 %collective-permute-start.3 = (bf16[1,336,1024]{2,1,0:T(8,128)(2,1)}, bf16[1,336,1024]{2,1,0:T(8,128)(2,1)}, u32[]{:S(2)}, u32[]{:S(2)}) collective-permute-start(bf16[1,336,1024]{2,1,0:T(8,128)(2,1)} %get-tuple-element.38.refs_0_), channel_id=1, source_target_pairs={{0,32},{1,97},{2,34},{3,99},{4,36},{5,101},{6,38},{7,103},{8,40},{... | collective-permute-start | bytes 2064392 | tf_op jit(solution)/shard_map/ppermute | solution.py:92
  9.6 3.8 %collective-permute-start.4 = (bf16[1,176,1024]{2,1,0:T(8,128)(2,1)}, bf16[1,176,1024]{2,1,0:T(8,128)(2,1)}, u32[]{:S(2)}, u32[]{:S(2)}) collective-permute-start(bf16[1,176,1024]{2,1,0:T(8,128)(2,1)} %get-tuple-element.39.refs_2_), channel_id=1, source_target_pairs={{0,24},{1,25},{2,26},{3,27},{4,28},{5,29},{6,30},{7,31},{8,16},{9,... | collective-permute-start | bytes 1081352 | tf_op jit(solution)/shard_map/ppermute | solution.py:92
  14.0 7.8 %collective-permute-done.4.refs_3_ = bf16[1,176,1024]{2,1,0:T(8,128)(2,1)} collective-permute-done((bf16[1,176,1024]{2,1,0:T(8,128)(2,1)}, bf16[1,176,1024]{2,1,0:T(8,128)(2,1)}, u32[]{:S(2)}, u32[]{:S(2)}) %collective-permute-start.4) | collective-permute-done | bytes 360480 | tf_op jit(solution)/shard_map/ppermute | solution.py:92
  21.8 2.6 %shard_map.60 = (bf16[2,336,1024]{2,1,0:T(8,128)(2,1)}, bf16[2,176,1024]{2,1,0:T(8,128)(2,1)}) custom-call(bf16[1,336,1024]{2,1,0:T(8,128)(2,1)} %get-tuple-element.38.refs_0_, bf16[1,336,1024]{2,1,0:T(8,128)(2,1)} %collective-permute-done.3.refs_1_, bf16[1,176,1024]{2,1,0:T(8,128)(2,1)} %get-tuple-element.39.refs_2_, ...), custom_call_target="tpu_custom_call" | custom-call | bytes 1024 | tf_op jit(solution)/shard_map/pallas_call | solution.py:337
  24.4 3.0 %collective-permute-start.7 = (bf16[2,336,1024]{2,1,0:T(8,128)(2,1)}, bf16[2,336,1024]{2,1,0:T(8,128)(2,1)S(1)}, u32[]{:S(2)}, u32[]{:S(2)}) collective-permute-start(bf16[2,336,1024]{2,1,0:T(8,128)(2,1)} %get-tuple-element.40.refs_5_.refs_0_), channel_id=1, source_target_pairs={{0,96},{1,25},{2,98},{3,27},{4,100},{5,29},{6,102},{7,31},{8,104},... | collective-permute-start | bytes 4128776 | tf_op jit(solution)/shard_map/ppermute | solution.py:92
  30.1 14.8 %shard_map.61 = (bf16[16,720,128]{2,1,0:T(8,128)(2,1)}, bf16[16,720,128]{2,1,0:T(8,128)(2,1)}, bf16[16,304,128]{2,1,0:T(8,128)(2,1)}, bf16[16,304,128]{2,1,0:T(8,128)(2,1)}) custom-call(s32[65]{0:T(128)} %pad_add_fusion.where_ref, bf16[512,8192]{1,0:T(8,128)(2,1)} %refs_0_.1, bf16[512,2048]{1,0:T(8,128)(2,1)} %collective-permute-done.refs_1_, ...), custom_call_target="tpu_custom_call" | custom-call | bytes 1024 | tf_op jit(solution)/shard_map/pallas_call | solution.py:233
  45.0 2.6 %collective-permute-start.6 = (bf16[16,720,128]{2,1,0:T(8,128)(2,1)}, bf16[16,720,128]{2,1,0:T(8,128)(2,1)S(1)}, u32[]{:S(2)}, u32[]{:S(2)}) collective-permute-start(bf16[16,720,128]{2,1,0:T(8,128)(2,1)} %get-tuple-element.44), channel_id=1, source_target_pairs={{0,2},{1,7},{2,0},{3,5},{4,6},{5,3},{6,4},{7,1},{8,10},{9,15},{10,... | collective-permute-start | bytes 8847368 | tf_op jit(solution)/shard_map/ppermute | solution.py:92
  48.9 4.0 %shard_map.62 = (bf16[4,336,1024]{2,1,0:T(8,128)(2,1)}, bf16[4,176,1024]{2,1,0:T(8,128)(2,1)}) custom-call(bf16[2,336,1024]{2,1,0:T(8,128)(2,1)} %get-tuple-element.40.refs_5_.refs_0_, bf16[2,336,1024]{2,1,0:T(8,128)(2,1)} %copy-done.6, bf16[2,176,1024]{2,1,0:T(8,128)(2,1)} %get-tuple-element.41.refs_6_.refs_2_, bf16[2,176,1024]{2,1,0:T(8,128)(2,1)} %copy-done.10), custom_call_target="tpu_custom_call" | custom-call | bytes 1024 | tf_op jit(solution)/shard_map/pallas_call | solution.py:337
  55.6 25.2 %collective-permute-done.6 = bf16[16,720,128]{2,1,0:T(8,128)(2,1)S(1)} collective-permute-done((bf16[16,720,128]{2,1,0:T(8,128)(2,1)}, bf16[16,720,128]{2,1,0:T(8,128)(2,1)S(1)}, u32[]{:S(2)}, u32[]{:S(2)}) %collective-permute-start.6) | collective-permute-done | bytes 2949152 | tf_op jit(solution)/shard_map/ppermute | solution.py:92
  80.9 1.9 %add_convert_fusion = (bf16[8,720,128]{2,1,0:T(8,128)(2,1)S(1)}, bf16[8,720,128]{2,1,0:T(8,128)(2,1)}) fusion(bf16[16,720,128]{2,1,0:T(8,128)(2,1)S(1)} %collective-permute-done.6, bf16[16,720,128]{2,1,0:T(8,128)(2,1)S(1)} %copy-done.2), kind=kLoop, calls=%fused_computation | loop fusion | flops 5898240 | bytes 8847360 | tf_op jit(solution)/shard_map/convert_element_type | solution.py:381
  82.8 6.1 %collective-permute-done.13.refs_3_ = bf16[4,176,1024]{2,1,0:T(8,128)(2,1)} collective-permute-done((bf16[4,176,1024]{2,1,0:T(8,128)(2,1)}, bf16[4,176,1024]{2,1,0:T(8,128)(2,1)}, u32[]{:S(2)}, u32[]{:S(2)}) %collective-permute-start.13) | collective-permute-done | bytes 1441824 | tf_op jit(solution)/shard_map/ppermute | solution.py:92
  92.4 9.4 %shard_map.63.refs_4_ = bf16[512,8192]{1,0:T(8,128)(2,1)} custom-call(s32[16]{0:T(128)} %get-tuple-element.53.sched_ref, bf16[512,1024]{1,0:T(8,128)(2,1)} %kg_ref.3, bf16[4,336,1024]{2,1,0:T(8,128)(2,1)} %get-tuple-element.48.refs_0_, bf16[4,336,1024]{2,1,0:T(8,128)(2,1)} %collective-permute-done.12.refs_1_, ...), custom_call_target="tpu_custom_call" | custom-call | flops 4294967296 | bytes 31457280 | tf_op jit(solution)/shard_map/pallas_call | solution.py:294
  101.9 6.2 %collective-permute-done.11 = bf16[8,720,128]{2,1,0:T(8,128)(2,1)S(1)} collective-permute-done((bf16[8,720,128]{2,1,0:T(8,128)(2,1)}, bf16[8,720,128]{2,1,0:T(8,128)(2,1)S(1)}, u32[]{:S(2)}, u32[]{:S(2)}) %collective-permute-start.11) | collective-permute-done | bytes 1474592 | tf_op jit(solution)/shard_map/ppermute | solution.py:92
  108.1 1.6 %add_convert_fusion.2 = (bf16[4,720,128]{2,1,0:T(8,128)(2,1)}, bf16[4,720,128]{2,1,0:T(8,128)(2,1)}) fusion(bf16[8,720,128]{2,1,0:T(8,128)(2,1)S(1)} %collective-permute-done.11, bf16[8,720,128]{2,1,0:T(8,128)(2,1)S(1)} %get-tuple-element.55), kind=kLoop, calls=%fused_computation.2 | loop fusion | flops 2949120 | bytes 4423680 | tf_op jit(solution)/shard_map/convert_element_type | solution.py:381
  109.9 2.0 %add_convert_fusion.6 = (bf16[4,304,128]{2,1,0:T(8,128)(2,1)}, bf16[4,304,128]{2,1,0:T(8,128)(2,1)S(1)}) fusion(bf16[8,304,128]{2,1,0:T(8,128)(2,1)} %collective-permute-done.10, bf16[8,304,128]{2,1,0:T(8,128)(2,1)S(1)} %get-tuple-element.57), kind=kLoop, calls=%fused_computation.6 | loop fusion | flops 1245184 | bytes 1867776 | tf_op jit(solution)/shard_map/convert_element_type | solution.py:381
  113.9 1.6 %copy-done.4 = bf16[4,336,1024]{2,1,0:T(8,128)(2,1)} copy-done((bf16[4,336,1024]{2,1,0:T(8,128)(2,1)}, bf16[4,336,1024]{2,1,0:T(8,128)(2,1)S(1)}, u32[]{:S(2)}) %copy-start.4) | copy-done | bytes 2752536
  115.4 9.4 %shard_map.64 = bf16[512,8192]{1,0:T(8,128)(2,1)} custom-call(s32[16]{0:T(128)} %get-tuple-element.59.sched_ref, bf16[512,1024]{1,0:T(8,128)(2,1)} %kg_ref.3, bf16[4,336,1024]{2,1,0:T(8,128)(2,1)} %copy-done.3, bf16[4,336,1024]{2,1,0:T(8,128)(2,1)} %copy-done.4, bf16[4,176,1024]{2,1,0:T(8,128)(2,1)} %copy-done.5, ...), custom_call_target="tpu_custom_call", output_to_operand_aliasing={{}: (6, {})} | custom-call | flops 4294967296 | bytes 31457280 | tf_op jit(solution)/shard_map/pallas_call | solution.py:294
  125.9 2.6 %shard_map.65 = (bf16[128,1024]{1,0:T(8,128)(2,1)}, bf16[128,1024]{1,0:T(8,128)(2,1)}, bf16[128,1024]{1,0:T(8,128)(2,1)}, bf16[128,1024]{1,0:T(8,128)(2,1)}) custom-call(bf16[4,720,128]{2,1,0:T(8,128)(2,1)} %get-tuple-element.62.refs_0_, bf16[4,720,128]{2,1,0:T(8,128)(2,1)} %copy-done.9, bf16[4,304,128]{2,1,0:T(8,128)(2,1)} %get-tuple-element.64.refs_2_, ...), custom_call_target="tpu_custom_call" | custom-call | bytes 1024 | tf_op jit(solution)/shard_map/pallas_call | solution.py:365
  128.5 4.3 %collective-permute-start.22 = (bf16[128,1024]{1,0:T(8,128)(2,1)}, bf16[128,1024]{1,0:T(8,128)(2,1)S(1)}, u32[]{:S(2)}, u32[]{:S(2)}) collective-permute-start(bf16[128,1024]{1,0:T(8,128)(2,1)} %get-tuple-element.69), channel_id=1, source_target_pairs={{0,56},{1,88},{2,58},{3,90},{4,60},{5,92},{6,62},{7,94},{8,48},{9,... | collective-permute-start | bytes 786440 | tf_op jit(solution)/shard_map/ppermute | solution.py:103
  132.8 2.2 %collective-permute-start.20 = (bf16[128,1024]{1,0:T(8,128)(2,1)}, bf16[128,1024]{1,0:T(8,128)(2,1)S(1)}, u32[]{:S(2)}, u32[]{:S(2)}) collective-permute-start(bf16[128,1024]{1,0:T(8,128)(2,1)} %get-tuple-element.67), channel_id=1, source_target_pairs={{0,32},{1,64},{2,34},{3,66},{4,36},{5,68},{6,38},{7,70},{8,40},{9,... | collective-permute-start | bytes 786440 | tf_op jit(solution)/shard_map/ppermute | solution.py:103
  135.0 3.1 %collective-permute-start.19 = (bf16[128,1024]{1,0:T(8,128)(2,1)}, bf16[128,1024]{1,0:T(8,128)(2,1)S(1)}, u32[]{:S(2)}, u32[]{:S(2)}) collective-permute-start(bf16[128,1024]{1,0:T(8,128)(2,1)} %get-tuple-element.66), channel_id=1, source_target_pairs={{0,0},{1,96},{2,2},{3,98},{4,4},{5,100},{6,6},{7,102},{8,8},{9,104... | collective-permute-start | bytes 786440 | tf_op jit(solution)/shard_map/ppermute | solution.py:103
  138.1 3.8 %collective-permute-done.22 = bf16[128,1024]{1,0:T(8,128)(2,1)S(1)} collective-permute-done((bf16[128,1024]{1,0:T(8,128)(2,1)}, bf16[128,1024]{1,0:T(8,128)(2,1)S(1)}, u32[]{:S(2)}, u32[]{:S(2)}) %collective-permute-start.22) | collective-permute-done | bytes 262176 | tf_op jit(solution)/shard_map/ppermute | solution.py:103
  141.9 3.9 %collective-permute-done.21 = bf16[128,1024]{1,0:T(8,128)(2,1)S(1)} collective-permute-done((bf16[128,1024]{1,0:T(8,128)(2,1)}, bf16[128,1024]{1,0:T(8,128)(2,1)S(1)}, u32[]{:S(2)}, u32[]{:S(2)}) %collective-permute-start.21) | collective-permute-done | bytes 262176 | tf_op jit(solution)/shard_map/ppermute | solution.py:103
  (67 shorter events, 19.3 us)
Async XLA Ops:
  5.2 24.0 %collective-permute-start = (bf16[512,2048]{1,0:T(8,128)(2,1)}, bf16[512,2048]{1,0:T(8,128)(2,1)}, u32[]{:S(2)}, u32[]{:S(2)}) collective-permute-start(bf16[512,2048]{1,0:T(8,128)(2,1)} %get-tuple-element.36), channel_id=1, source_target_pairs={{0,1},{1,0},{2,3},{3,2},{4,5},{5,4},{6,7},{7,6},{8,9},{9,8},{10,11... | collective-permute-start | bytes 6291464 | tf_op jit(solution)/shard_map/ppermute | solution.py:92
  6.7 22.5 %collective-permute-start.1 = (bf16[512,2048]{1,0:T(8,128)(2,1)}, bf16[512,2048]{1,0:T(8,128)(2,1)}, u32[]{:S(2)}, u32[]{:S(2)}) collective-permute-start(bf16[512,2048]{1,0:T(8,128)(2,1)} %get-tuple-element.37), channel_id=1, source_target_pairs={{0,1},{1,0},{2,3},{3,2},{4,5},{5,4},{6,7},{7,6},{8,9},{9,8},{10,11... | collective-permute-start | bytes 6291464 | tf_op jit(solution)/shard_map/ppermute | solution.py:92
  6.8 15.0 %collective-permute-start.3 = (bf16[1,336,1024]{2,1,0:T(8,128)(2,1)}, bf16[1,336,1024]{2,1,0:T(8,128)(2,1)}, u32[]{:S(2)}, u32[]{:S(2)}) collective-permute-start(bf16[1,336,1024]{2,1,0:T(8,128)(2,1)} %get-tuple-element.38.refs_0_), channel_id=1, source_target_pairs={{0,32},{1,97},{2,34},{3,99},{4,36},{5,101},{6,38},{7,103},{8,40},{... | collective-permute-start | bytes 2064392 | tf_op jit(solution)/shard_map/ppermute | solution.py:92
  9.6 12.2 %collective-permute-start.4 = (bf16[1,176,1024]{2,1,0:T(8,128)(2,1)}, bf16[1,176,1024]{2,1,0:T(8,128)(2,1)}, u32[]{:S(2)}, u32[]{:S(2)}) collective-permute-start(bf16[1,176,1024]{2,1,0:T(8,128)(2,1)} %get-tuple-element.39.refs_2_), channel_id=1, source_target_pairs={{0,24},{1,25},{2,26},{3,27},{4,28},{5,29},{6,30},{7,31},{8,16},{9,... | collective-permute-start | bytes 1081352 | tf_op jit(solution)/shard_map/ppermute | solution.py:92
  13.9 15.3 %collective-permute-start.2 = (bf16[1024,512]{1,0:T(8,128)(2,1)S(1)}, bf16[1024,512]{1,0:T(8,128)(2,1)S(1)}, u32[]{:S(2)}, u32[]{:S(2)}) collective-permute-start(bf16[1024,512]{1,0:T(8,128)(2,1)S(1)} %bitcast.8), channel_id=1, source_target_pairs={{0,1},{1,0},{2,3},{3,2},{4,5},{5,4},{6,7},{7,6},{8,9},{9,8},{10,11... | collective-permute-start | bytes 3145736 | tf_op jit(solution)/shard_map/ppermute | solution.py:92
  24.4 23.1 %collective-permute-start.7 = (bf16[2,336,1024]{2,1,0:T(8,128)(2,1)}, bf16[2,336,1024]{2,1,0:T(8,128)(2,1)S(1)}, u32[]{:S(2)}, u32[]{:S(2)}) collective-permute-start(bf16[2,336,1024]{2,1,0:T(8,128)(2,1)} %get-tuple-element.40.refs_5_.refs_0_), channel_id=1, source_target_pairs={{0,96},{1,25},{2,98},{3,27},{4,100},{5,29},{6,102},{7,31},{8,104},... | collective-permute-start | bytes 4128776 | tf_op jit(solution)/shard_map/ppermute | solution.py:92
  28.2 19.4 %collective-permute-start.8 = (bf16[2,176,1024]{2,1,0:T(8,128)(2,1)}, bf16[2,176,1024]{2,1,0:T(8,128)(2,1)S(1)}, u32[]{:S(2)}, u32[]{:S(2)}) collective-permute-start(bf16[2,176,1024]{2,1,0:T(8,128)(2,1)} %get-tuple-element.41.refs_6_.refs_2_), channel_id=1, source_target_pairs={{0,32},{1,33},{2,34},{3,35},{4,36},{5,37},{6,38},{7,39},{8,40},{9,... | collective-permute-start | bytes 2162696 | tf_op jit(solution)/shard_map/ppermute | solution.py:92
  45.0 35.9 %collective-permute-start.6 = (bf16[16,720,128]{2,1,0:T(8,128)(2,1)}, bf16[16,720,128]{2,1,0:T(8,128)(2,1)S(1)}, u32[]{:S(2)}, u32[]{:S(2)}) collective-permute-start(bf16[16,720,128]{2,1,0:T(8,128)(2,1)} %get-tuple-element.44), channel_id=1, source_target_pairs={{0,2},{1,7},{2,0},{3,5},{4,6},{5,3},{6,4},{7,1},{8,10},{9,15},{10,... | collective-permute-start | bytes 8847368 | tf_op jit(solution)/shard_map/ppermute | solution.py:92
  52.9 35.9 %collective-permute-start.12 = (bf16[4,336,1024]{2,1,0:T(8,128)(2,1)}, bf16[4,336,1024]{2,1,0:T(8,128)(2,1)}, u32[]{:S(2)}, u32[]{:S(2)}) collective-permute-start(bf16[4,336,1024]{2,1,0:T(8,128)(2,1)} %get-tuple-element.48.refs_0_), channel_id=1, source_target_pairs={{0,24},{1,33},{2,26},{3,35},{4,28},{5,37},{6,30},{7,39},{8,16},{9,... | collective-permute-start | bytes 8257544 | tf_op jit(solution)/shard_map/ppermute | solution.py:92
  54.1 34.8 %collective-permute-start.13 = (bf16[4,176,1024]{2,1,0:T(8,128)(2,1)}, bf16[4,176,1024]{2,1,0:T(8,128)(2,1)}, u32[]{:S(2)}, u32[]{:S(2)}) collective-permute-start(bf16[4,176,1024]{2,1,0:T(8,128)(2,1)} %get-tuple-element.54.refs_2_), channel_id=1, source_target_pairs={{0,96},{1,97},{2,98},{3,99},{4,100},{5,101},{6,102},{7,103},{8,104... | collective-permute-start | bytes 4325384 | tf_op jit(solution)/shard_map/ppermute | solution.py:92
  54.3 36.4 %collective-permute-start.9 = (bf16[4,336,1024]{2,1,0:T(8,128)(2,1)}, bf16[4,336,1024]{2,1,0:T(8,128)(2,1)S(1)}, u32[]{:S(2)}, u32[]{:S(2)}) collective-permute-start(bf16[4,336,1024]{2,1,0:T(8,128)(2,1)} %get-tuple-element.48.refs_0_), channel_id=1, source_target_pairs={{0,1},{1,0},{2,3},{3,2},{4,5},{5,4},{6,7},{7,6},{8,9},{9,8},{10,11... | collective-permute-start | bytes 8257544 | tf_op jit(solution)/shard_map/ppermute | solution.py:92
  55.6 34.5 %collective-permute-start.5 = (bf16[16,304,128]{2,1,0:T(8,128)(2,1)}, bf16[16,304,128]{2,1,0:T(8,128)(2,1)S(1)}, u32[]{:S(2)}, u32[]{:S(2)}) collective-permute-start(bf16[16,304,128]{2,1,0:T(8,128)(2,1)} %get-tuple-element.42), channel_id=1, source_target_pairs={{0,8},{1,9},{2,10},{3,11},{4,12},{5,13},{6,14},{7,15},{8,0},{9,1},... | collective-permute-start | bytes 3735560 | tf_op jit(solution)/shard_map/ppermute | solution.py:92
  88.9 23.9 %collective-permute-start.14 = (bf16[4,336,1024]{2,1,0:T(8,128)(2,1)}, bf16[4,336,1024]{2,1,0:T(8,128)(2,1)S(1)}, u32[]{:S(2)}, u32[]{:S(2)}) collective-permute-start(bf16[4,336,1024]{2,1,0:T(8,128)(2,1)} %collective-permute-done.12.refs_1_), channel_id=1, source_target_pairs={{0,1},{1,0},{2,3},{3,2},{4,5},{5,4},{6,7},{7,6},{8,9},{9,8},{10,11... | collective-permute-start | bytes 8257544 | tf_op jit(solution)/shard_map/ppermute | solution.py:92
  89.3 18.8 %collective-permute-start.11 = (bf16[8,720,128]{2,1,0:T(8,128)(2,1)}, bf16[8,720,128]{2,1,0:T(8,128)(2,1)S(1)}, u32[]{:S(2)}, u32[]{:S(2)}) collective-permute-start(bf16[8,720,128]{2,1,0:T(8,128)(2,1)} %get-tuple-element.71), channel_id=1, source_target_pairs={{0,6},{1,9},{2,4},{3,11},{4,2},{5,13},{6,0},{7,15},{8,14},{9,1},{1... | collective-permute-start | bytes 4423688 | tf_op jit(solution)/shard_map/ppermute | solution.py:92
  89.3 23.5 %collective-permute-start.15 = (bf16[4,176,1024]{2,1,0:T(8,128)(2,1)}, bf16[4,176,1024]{2,1,0:T(8,128)(2,1)S(1)}, u32[]{:S(2)}, u32[]{:S(2)}) collective-permute-start(bf16[4,176,1024]{2,1,0:T(8,128)(2,1)} %get-tuple-element.54.refs_2_), channel_id=1, source_target_pairs={{0,1},{1,0},{2,3},{3,2},{4,5},{5,4},{6,7},{7,6},{8,9},{9,8},{10,11... | collective-permute-start | bytes 4325384 | tf_op jit(solution)/shard_map/ppermute | solution.py:92
  90.1 22.7 %collective-permute-start.16 = (bf16[4,176,1024]{2,1,0:T(8,128)(2,1)}, bf16[4,176,1024]{2,1,0:T(8,128)(2,1)}, u32[]{:S(2)}, u32[]{:S(2)}) collective-permute-start(bf16[4,176,1024]{2,1,0:T(8,128)(2,1)} %collective-permute-done.13.refs_3_), channel_id=1, source_target_pairs={{0,1},{1,0},{2,3},{3,2},{4,5},{5,4},{6,7},{7,6},{8,9},{9,8},{10,11... | collective-permute-start | bytes 4325384 | tf_op jit(solution)/shard_map/ppermute | solution.py:92
  92.4 17.5 %collective-permute-start.10 = (bf16[8,304,128]{2,1,0:T(8,128)(2,1)}, bf16[8,304,128]{2,1,0:T(8,128)(2,1)}, u32[]{:S(2)}, u32[]{:S(2)}) collective-permute-start(bf16[8,304,128]{2,1,0:T(8,128)(2,1)} %get-tuple-element.75), channel_id=1, source_target_pairs={{0,2},{1,3},{2,0},{3,1},{4,6},{5,7},{6,4},{7,5},{8,10},{9,11},{10,... | collective-permute-start | bytes 1867784 | tf_op jit(solution)/shard_map/ppermute | solution.py:92
  109.7 15.2 %collective-permute-start.17 = (bf16[4,720,128]{2,1,0:T(8,128)(2,1)}, bf16[4,720,128]{2,1,0:T(8,128)(2,1)S(1)}, u32[]{:S(2)}, u32[]{:S(2)}) collective-permute-start(bf16[4,720,128]{2,1,0:T(8,128)(2,1)} %get-tuple-element.73), channel_id=1, source_target_pairs={{0,8},{1,3},{2,10},{3,1},{4,12},{5,7},{6,14},{7,5},{8,0},{9,11},{1... | collective-permute-start | bytes 2211848 | tf_op jit(solution)/shard_map/ppermute | solution.py:92
  111.9 13.0 %collective-permute-start.18 = (bf16[4,304,128]{2,1,0:T(8,128)(2,1)S(1)}, bf16[4,304,128]{2,1,0:T(8,128)(2,1)S(1)}, u32[]{:S(2)}, u32[]{:S(2)}) collective-permute-start(bf16[4,304,128]{2,1,0:T(8,128)(2,1)S(1)} %get-tuple-element.77), channel_id=1, source_target_pairs={{0,6},{1,7},{2,4},{3,5},{4,2},{5,3},{6,0},{7,1},{8,14},{9,15},{10,... | collective-permute-start | bytes 933896 | tf_op jit(solution)/shard_map/ppermute | solution.py:92
  128.5 13.4 %collective-permute-start.22 = (bf16[128,1024]{1,0:T(8,128)(2,1)}, bf16[128,1024]{1,0:T(8,128)(2,1)S(1)}, u32[]{:S(2)}, u32[]{:S(2)}) collective-permute-start(bf16[128,1024]{1,0:T(8,128)(2,1)} %get-tuple-element.69), channel_id=1, source_target_pairs={{0,56},{1,88},{2,58},{3,90},{4,60},{5,92},{6,62},{7,94},{8,48},{9,... | collective-permute-start | bytes 786440 | tf_op jit(solution)/shard_map/ppermute | solution.py:103
  132.8 13.1 %collective-permute-start.21 = (bf16[128,1024]{1,0:T(8,128)(2,1)}, bf16[128,1024]{1,0:T(8,128)(2,1)S(1)}, u32[]{:S(2)}, u32[]{:S(2)}) collective-permute-start(bf16[128,1024]{1,0:T(8,128)(2,1)} %get-tuple-element.68), channel_id=1, source_target_pairs={{0,24},{1,120},{2,26},{3,122},{4,28},{5,124},{6,30},{7,126},{8,16}... | collective-permute-start | bytes 786440 | tf_op jit(solution)/shard_map/ppermute | solution.py:103
  132.8 13.1 %collective-permute-start.20 = (bf16[128,1024]{1,0:T(8,128)(2,1)}, bf16[128,1024]{1,0:T(8,128)(2,1)S(1)}, u32[]{:S(2)}, u32[]{:S(2)}) collective-permute-start(bf16[128,1024]{1,0:T(8,128)(2,1)} %get-tuple-element.67), channel_id=1, source_target_pairs={{0,32},{1,64},{2,34},{3,66},{4,36},{5,68},{6,38},{7,70},{8,40},{9,... | collective-permute-start | bytes 786440 | tf_op jit(solution)/shard_map/ppermute | solution.py:103
  135.0 11.3 %collective-permute-start.19 = (bf16[128,1024]{1,0:T(8,128)(2,1)}, bf16[128,1024]{1,0:T(8,128)(2,1)S(1)}, u32[]{:S(2)}, u32[]{:S(2)}) collective-permute-start(bf16[128,1024]{1,0:T(8,128)(2,1)} %get-tuple-element.66), channel_id=1, source_target_pairs={{0,0},{1,96},{2,2},{3,98},{4,4},{5,100},{6,6},{7,102},{8,8},{9,104... | collective-permute-start | bytes 786440 | tf_op jit(solution)/shard_map/ppermute | solution.py:103
  146.5 2.3 %collective-permute-start.23 = (f32[64,1024]{1,0:T(8,128)S(1)}, f32[64,1024]{1,0:T(8,128)S(1)}, u32[]{:S(2)}, u32[]{:S(2)}) collective-permute-start(f32[64,1024]{1,0:T(8,128)S(1)} %constant_dynamic-slice_fusion), channel_id=1, source_target_pairs={{0,1},{1,0},{2,3},{3,2},{4,5},{5,4},{6,7},{7,6},{8,9},{9,8},{10,11... | collective-permute-start | bytes 786440 | tf_op jit(solution)/shard_map/ppermute | solution.py:92
  (12 other events, 104.8 us)
